TPU v7x, 32 devices: a whole 2x2x4 slice. The times are simulated.
32 devices in a mesh: dp: 4 (over z), cols: 8 (over y, x, core).
Axes of the slice: x: 2, y: 2, z: 4, core: 2. Of those that a mesh axis runs over, the one named last changes fastest.
Arguments:
- inputs: bfloat16 [4096, 4096], P('dp', 'cols'), may hold values from -6 to 6
- query_grads: bfloat16 [4096, 8192], P('dp'), may hold values from -0.125 to 0.125, as said below
- momentum: float32 [8192, 4096], P('dp', 'cols'), may hold values from -14 to 14, as said below
Outputs:
- new_momentum: float32 [8192, 4096], P('dp', 'cols')
- update: float32 [8192, 4096], P('dp', 'cols')
Inputs may be any that keep to these rules, and one draw needn't show every extreme that they name: `query_grads`: entries of scale about 4096 ** -0.5. `momentum`: entries of order two.
All inputs are finite; a program needn't handle non-finite values.
Results may differ from a plain program's by a relative error of at most 0.0003.
Values may be sent and summed in bfloat16 or wider, within the bound.
No kernel may reach another device: no remote copies, remote signals or barrier semaphores. Data moves between devices by JAX's collectives and lax.ppermute only.
A program may use at most 128 MiB of HBM per device.

v0:
```python
import math

import jax
import jax.numpy as jnp
from jax import lax
from jax.sharding import PartitionSpec as P

D = 4096
HEAD_DIM = 128
NEWTON_STEPS = 5


MOMENTUM_DECAY = 0.95
NORM_EPS = 1e-07
LINEAR_COEF = 3.4445
CUBIC_COEF = -4.775
QUINTIC_COEF = 2.0315
HIGHEST = lax.Precision.HIGHEST
CONTRACT_TOKENS = (((0,), (0,)), ((), ()))


def polynomial(gram_matrix):
    matrix_order = gram_matrix.shape[-1]
    trace_sum = jnp.sum(jnp.diagonal(gram_matrix, axis1=1, axis2=2), axis=1)
    norm_scale = jnp.sqrt(trace_sum) + NORM_EPS
    current = gram_matrix / (norm_scale * norm_scale)[:, None, None]
    identity = jnp.eye(matrix_order, dtype=jnp.float32)
    factor = jnp.broadcast_to(identity, gram_matrix.shape)
    for sweep_index in range(NEWTON_STEPS):
        square = jnp.einsum("hij,hjk->hik", current, current, precision=HIGHEST)
        poly_term = LINEAR_COEF * identity + CUBIC_COEF * current + QUINTIC_COEF * square
        factor = jnp.einsum("hij,hjk->hik", poly_term, factor, precision=HIGHEST)
        if sweep_index + 1 < NEWTON_STEPS:
            inner = jnp.einsum("hij,hjk->hik", current, poly_term, precision=HIGHEST)
            current = jnp.einsum("hij,hjk->hik", poly_term, inner, precision=HIGHEST)
    return factor / norm_scale[:, None, None]


def shards(inputs, query_grads, momentum):
    row_count = momentum.shape[0]
    col_count = momentum.shape[1]
    gradient = lax.psum_scatter(
        lax.dot_general(query_grads, inputs, CONTRACT_TOKENS, preferred_element_type=jnp.float32),
        "dp",
        scatter_dimension=0,
        tiled=True,
    )
    new_momentum = MOMENTUM_DECAY * momentum + gradient
    local_heads = row_count // HEAD_DIM
    blocks = new_momentum.reshape(local_heads, HEAD_DIM, col_count)
    partial_value = jnp.einsum("hik,hjk->hij", blocks, blocks, precision=HIGHEST)
    owners = lax.axis_size("cols")
    slot_count = -(-local_heads // owners)
    padded = jnp.pad(partial_value, ((0, slot_count * owners - local_heads), (0, 0), (0, 0)))
    owned_gram = lax.psum_scatter(
        padded.reshape(slot_count, owners, HEAD_DIM, HEAD_DIM),
        "cols",
        scatter_dimension=1,
        tiled=True,
    )
    owned_factor = polynomial(owned_gram.reshape(slot_count, HEAD_DIM, HEAD_DIM))
    returned = lax.all_gather(
        owned_factor.reshape(slot_count, 1, HEAD_DIM, HEAD_DIM), "cols", axis=1, tiled=True
    )
    factor = returned.reshape(slot_count * owners, HEAD_DIM, HEAD_DIM)[:local_heads]
    update = math.sqrt(D) * jnp.einsum("hij,hjk->hik", factor, blocks, precision=HIGHEST)
    return (new_momentum, update.reshape(row_count, col_count))


def solution(mesh):
    placed = (P("dp", "cols"), P("dp", None), P("dp", "cols"))
    return jax.shard_map(
        shards,
        mesh=mesh,
        in_specs=placed,
        out_specs=(P("dp", "cols"), P("dp", "cols")),
        check_vma=False,
    )
```

profile of v0, /device:TPU:0, one launch (start us, length us, event | category | flops | bytes accessed | tf_op | source)
XLA Modules:
  0.0 405.4 jit_solution(10221366583601642505)
XLA Ops:
  7.2 0.0 copy-start
  7.2 0.0 reduce-scatter.3.cloned.1.call-start
  7.2 1.2 copy-done
  8.4 15.8 %fusion.13 = f32[8192,512]{1,0:T(8,128)} fusion(bf16[1024,8192]{1,0:T(8,128)(2,1)} %param.4, bf16[1024,512]{1,0:T(8,128)(2,1)S(1)} %copy-done), kind=kOutput, calls=%fused_computation.26 | convolution fusion | flops 8589934592 | bytes 34603008 | tf_op jit(solution)/shard_map/dot_general | solution.py:43
  24.1 0.0 reduce-scatter.3.cloned.1.call-update
  24.2 0.0 reduce-scatter.5.cloned.1.call-start
  24.2 283.1 %reduce-scatter.3.cloned.1.call-done = f32[2048,512]{1,0:T(8,128)} async-done(((f32[8192,512]{1,0:T(8,128)}), f32[2048,512]{1,0:T(8,128)}) %reduce-scatter.3.cloned.1.call-update) | async-done | bytes 4194320 | tf_op jit(solution)/shard_map/reduce_scatter | solution.py:42
  307.3 4.5 %multiply_add_fusion = f32[2048,512]{1,0:T(8,128)S(1)} fusion(f32[2048,512]{1,0:T(8,128)} %reduce-scatter.3.cloned.1.call-done, f32[2048,512]{1,0:T(8,128)} %param.5), kind=kLoop, calls=%fused_computation.1 | loop fusion | flops 2097152 | bytes 12582912 | tf_op jit(solution)/shard_map/add | solution.py:48
  311.8 0.0 copy-start.1
  311.8 4.0 fusion.14
  315.9 0.0 copy-done.1
  315.9 1.1 copy.5
  316.9 0.0 reduce-scatter.5.cloned.1.call-update
  316.9 0.2 all-gather.3.cloned.1.call-start
  317.2 36.7 %reduce-scatter.5.cloned.1.call-done = f32[2,1,128,128]{3,2,0,1:T(8,128)} async-done(((f32[2,8,128,128]{3,2,0,1:T(8,128)}), f32[2,1,128,128]{3,2,0,1:T(8,128)}) %reduce-scatter.5.cloned.1.call-update) | async-done | bytes 131088 | tf_op jit(solution)/shard_map/reduce_scatter | solution.py:55
  353.9 0.0 copy-start.2
  353.9 5.6 %copy.6 = f32[2,128,128]{0,2,1:T(8,128)} copy(f32[2,128,128]{2,1,0:T(8,128)} %bitcast.58) | data formatting | bytes 262144 | tf_op jit(solution)/shard_map/reshape | solution.py:61
  359.4 1.8 gather_fusion
  361.3 0.0 copy-done.2
  361.3 0.4 fusion.4
  361.6 0.3 fusion.9
  362.0 0.3 fusion.15
  362.2 0.3 fusion.3
  362.5 0.3 fusion.5
  362.8 0.3 fusion.16
  363.1 0.3 fusion.22
  363.3 0.3 fusion.17
  363.6 0.3 fusion.2
  363.9 0.3 fusion.18
  364.2 0.3 fusion.23
  364.4 0.3 fusion.19
  364.7 0.3 fusion.1
  365.0 0.3 fusion.20
  365.3 0.3 fusion.24
  365.5 0.3 fusion.21
  365.8 0.3 fusion
  366.1 0.9 convolution_divide_fusion
  367.0 0.0 all-gather.3.cloned.1.call-update
  367.1 23.6 %all-gather.3.cloned.1.call-done = f32[2,1024,128]{2,1,0:T(8,128)} async-done(((f32[2,128,128]{2,1,0:T(8,128)}), f32[2,1024,128]{2,1,0:T(8,128)}) %all-gather.3.cloned.1.call-update) | async-done | bytes 1048592 | tf_op jit(solution)/shard_map/all_gather | solution.py:62
  390.7 8.2 %convolution_multiply_fusion = f32[16,128,512]{2,1,0:T(8,128)} fusion(f32[16,128,128]{2,1,0:T(8,128)} %bitcast.57, f32[16,128,512]{2,1,0:T(8,128)} %bitcast.54), kind=kOutput, calls=%fused_computation.2 | convolution fusion | flops 1611661312 | bytes 9437184 | tf_op jit(solution)/shard_map/hij,hjk->hik/dot_general | solution.py:66
  (5 shorter events, 0.1 us)
Async XLA Ops:
  7.2 1.2 copy-start
  7.2 300.1 %reduce-scatter.3.cloned.1.call-start = ((), (), s32[]{:S(2)}) async-start(), calls=%async_computation.2 | async-start | bytes 20971520 | tf_op jit(solution)/shard_map/reduce_scatter | solution.py:42
  24.2 329.7 %reduce-scatter.5.cloned.1.call-start = ((), (), s32[]{:S(2)}) async-start(), calls=%async_computation.3 | async-start | bytes 1179648 | tf_op jit(solution)/shard_map/reduce_scatter | solution.py:55
  311.8 4.0 copy-start.1
  316.9 73.7 %all-gather.3.cloned.1.call-start = ((), (), s32[]{:S(2)}) async-start(), calls=%async_computation.4 | async-start | bytes 1179648 | tf_op jit(solution)/shard_map/all_gather | solution.py:62
  353.9 7.4 %copy-start.2 = (f32[2,1,128,128]{3,2,0,1:T(8,128)S(1)}, f32[2,1,128,128]{3,2,0,1:T(8,128)}, u32[]{:S(2)}) copy-start(f32[2,1,128,128]{3,2,0,1:T(8,128)} %reduce-scatter.5.cloned.1.call-done) | copy-start | bytes 393220
Sparse Core Ops, SparseCore 0:
  24.3 282.9 reduce-scatter.2
  317.1 36.7 reduce-scatter.4
  367.2 23.4 all-gather.2
where the time goes:
time: 406 us; the launch traced here: 405 us
  waiting for transfers between devices  343 us (84%)
  matrix products  33.6 us (8%)
  between operations  13.9 us (3%)
  local copies, waits for them, and re-layouts  9.58 us (2%)
  other arithmetic  4.57 us (1%)
    reduce_scatter x1, waiting for transfers between devices, shards(): lax.psum_scatter(lax.dot_general(query_grads, inputs, CONTRACT_TOKENS, pr...  283 us
    reduce_scatter x1, waiting for transfers between devices, shards(): lax.psum_scatter(padded.reshape(slot_count, owners, HEAD_DIM, HEAD_DIM),...  36.7 us
    all_gather x1, waiting for transfers between devices, shards(): lax.all_gather(owned_factor.reshape(slot_count, 1, HEAD_DIM, HEAD_DIM), '...  23.6 us
    dot_general x1, matrix products, shards(): lax.dot_general(query_grads, inputs, CONTRACT_TOKENS, preferred_element_t...  15.8 us
    dot_general x1, matrix products, shards(): jnp.einsum('hij,hjk->hik', factor, blocks, precision=HIGHEST)  8.23 us
  transfers between devices with their start and end apart: 3, of which 3 were waited for; matrix products, arithmetic and copies ran while one was open for 0% of the time, Pallas kernels for 0%

commit v1 on v0

--- a/solution.py
+++ b/solution.py
@@ -1,15 +1,15 @@
+import functools
 import math
 
 import jax
 import jax.numpy as jnp
 from jax import lax
+from jax.experimental import pallas as pl
+from jax.experimental.pallas import tpu as pltpu
 from jax.sharding import PartitionSpec as P
 
-D = 4096
 HEAD_DIM = 128
 NEWTON_STEPS = 5
-
-
 MOMENTUM_DECAY = 0.95
 NORM_EPS = 1e-07
 LINEAR_COEF = 3.4445
@@ -17,6 +17,225 @@
 QUINTIC_COEF = 2.0315
 HIGHEST = lax.Precision.HIGHEST
 CONTRACT_TOKENS = (((0,), (0,)), ((), ()))
+SMALL_BYTES = 16 * 1024 * 1024
+VMEM_BYTES = 32 * 1024 * 1024
+
+
+def split(value):
+    high = value.astype(jnp.bfloat16)
+    return high, (value - high.astype(jnp.float32)).astype(jnp.bfloat16)
+
+
+def dot3(left, right, dims):
+    lh, ll = left
+    rh, rl = right
+    dot = functools.partial(lax.dot_general, dimension_numbers=dims, preferred_element_type=jnp.float32)
+    return dot(lh, rh) + (dot(lh, rl) + dot(ll, rh))
+
+
+def accumulate_kernel(layouts, decay, final, place, total, *refs):
+    refs = list(refs)
+    taken = [([refs.pop(0) for _ in layout], layout, refs.pop(0)) for layout in layouts]
+    out = refs.pop(0)
+    out[...] = total[...] * decay if decay else total[...]
+    pair_rows = out.shape[0] // 2
+    for q_refs, layout, x_ref in taken:
+        for q_ref, piece in zip(q_refs, layout):
+            if piece is None:
+                out[...] += lax.dot_general(
+                    q_ref[...], x_ref[...], CONTRACT_TOKENS, preferred_element_type=jnp.float32
+                )
+                continue
+            core, offset, count = piece
+            start = pl.multiple_of(((place[1] + core) % 2) * pair_rows + offset, count)
+            value = jnp.dot(q_ref[0], x_ref[...], preferred_element_type=jnp.float32)
+            out[pl.ds(start, count), :] += value
+    if not final:
+        return
+    gram = refs.pop(0)
+    pair_heads = gram.shape[1]
+    for head in range(out.shape[0] // HEAD_DIM):
+        parts = split(out[head * HEAD_DIM : (head + 1) * HEAD_DIM, :])
+        pair = pl.program_id(0) * 2 + head // pair_heads
+        other = place[1] ^ pair
+        slot = other // 2 + (other % 2) * (gram.shape[0] // 2)
+        gram[slot, head % pair_heads] = dot3(parts, parts, (((1,), (1,)), ((), ())))
+
+
+def polynomial_kernel(*refs):
+    parts, factor = refs[:-1], refs[-1]
+    gram = functools.reduce(lambda total, piece: total + piece[...], parts[1:], parts[0][...])
+    order = gram.shape[-1]
+    rows = lax.broadcasted_iota(jnp.int32, (order, order), 0)
+    cols = lax.broadcasted_iota(jnp.int32, (order, order), 1)
+    identity = (rows == cols).astype(jnp.float32)
+    heads = range(gram.shape[0])
+    dot = functools.partial(jnp.dot, precision=HIGHEST, preferred_element_type=jnp.float32)
+    norms = [jnp.sqrt(jnp.sum(gram[h] * identity)) + NORM_EPS for h in heads]
+    current = [gram[h] / (norms[h] * norms[h]) for h in heads]
+    factors = [None for h in heads]
+    for sweep in range(NEWTON_STEPS):
+        square = [dot(current[h], current[h]) for h in heads]
+        poly = [LINEAR_COEF * identity + CUBIC_COEF * current[h] + QUINTIC_COEF * square[h] for h in heads]
+        factors = [poly[h] if sweep == 0 else dot(poly[h], factors[h]) for h in heads]
+        if sweep + 1 < NEWTON_STEPS:
+            inner = [dot(current[h], poly[h]) for h in heads]
+            current = [dot(poly[h], inner[h]) for h in heads]
+    for h in heads:
+        factor[h] = factors[h] / norms[h]
+
+
+def update_kernel(scale, place, factor, block, *refs):
+    update = refs[-1]
+    for head in range(factor.shape[1]):
+        rows = slice(head * HEAD_DIM, (head + 1) * HEAD_DIM)
+        product = dot3(split(factor[0, head]), split(block[rows, :]), (((1,), (0,)), ((), ())))
+        update[rows, :] = scale * product
+
+
+def shards(model_width, inputs, query_grads, momentum):
+    depth = lax.axis_size("dp")
+    owners = lax.axis_size("cols")
+    z = lax.axis_index("dp")
+    c = lax.axis_index("cols")
+    tokens, col_count = inputs.shape
+    row_count = momentum.shape[0]
+    pair_rows = row_count // owners
+    pair_heads = pair_rows // HEAD_DIM
+    def over(bits, value):
+        return lax.ppermute(value, "cols", [(i, i ^ bits) for i in range(owners)])
+
+    def onward(k, value):
+        return lax.ppermute(value, "dp", [(i, (i + k) % depth) for i in range(depth)])
+
+    def both(held, got):
+        return [jnp.concatenate(pair) for pair in zip(held, got)]
+
+    pieces = [
+        lax.dynamic_slice(query_grads, (0, lax.rem(z + k, depth) * row_count + c * pair_rows), (tokens, pair_rows)).T
+        for k in range(1, depth)
+    ]
+    turns = ((4, 2), (2, 4))
+    half = pair_rows // 2
+
+    near = [onward(k, pieces[k - 1]) for k in (1, 3)]
+    near, pieces = lax.optimization_barrier((near, pieces))
+
+    far = onward(2, pieces[1])
+    near = [piece[None] for piece in near]
+    got = [over(turn[0], piece) for turn, piece in zip(turns, near)]
+    far, near, got, moved = lax.optimization_barrier((far, near, got, inputs))
+
+    moved_1 = onward(1, moved)
+    near = both(near, got)
+    got = [over(turn[1], piece) for turn, piece in zip(turns, near)]
+    far, near, got, moved_1 = lax.optimization_barrier((far, near, got, moved_1))
+
+    moved_2 = onward(1, moved_1)
+    near = both(near, got)
+    near_got = [over(1, piece) for piece in near]
+    far = [far[None, :half], far[None, half:]]
+    far = both(far, [over(turn[0], piece) for turn, piece in zip(turns, far)])
+    got = [over(turn[1], piece) for turn, piece in zip(turns, far)]
+    far, near, near_got, got, moved_1, moved_2 = lax.optimization_barrier((far, near, near_got, got, moved_1, moved_2))
+
+    moved_3 = onward(1, moved_2)
+    far = both(far, got)
+    far_got = [over(1, piece) for piece in far]
+
+    place = jnp.stack([z, c]).astype(jnp.int32)
+
+    def pair_of(i, place):
+        return place[1] ^ ((i % 4) * 2 + i // 4)
+
+    def rows_spec(part, columns):
+        return pl.BlockSpec((pair_rows, columns), lambda i, place: (pair_of(i, place), part))
+
+    pairs = 2
+    gram_dims = (owners, pair_heads, HEAD_DIM, HEAD_DIM)
+    gram_spec = pl.BlockSpec(gram_dims, lambda i, place: (0, 0, 0, 0))
+    gram_shape = jax.ShapeDtypeStruct(gram_dims, jnp.float32)
+
+    def spots(order):
+        def index_map(i, place):
+            other = (place[1] // 2) ^ i
+            return (other if order else (other % 2) * 2 + other // 2), 0, 0
+
+        return index_map
+
+    def term_specs(layout):
+        if layout[0] is None:
+            return [pl.BlockSpec((tokens, pairs * pair_rows), lambda i, place: (0, place[0] * (owners // pairs) + i))]
+        return [pl.BlockSpec((1, count, tokens), spots(order)) for _, _, count, order in layout]
+
+    def accumulate(total, terms, decay, final):
+        block = pl.BlockSpec((pairs * pair_rows, col_count), lambda i, place: (i, 0))
+        whole = pl.BlockSpec((tokens, col_count), lambda i, place: (0, 0))
+        arrays = [array for rows, _, x in terms for array in (*rows, x)]
+        shape = jax.ShapeDtypeStruct((row_count, col_count), jnp.float32)
+        layouts = [[piece and piece[:3] for piece in layout] for _, layout, _ in terms]
+        return pl.pallas_call(
+            functools.partial(accumulate_kernel, layouts, decay, final),
+            grid_spec=pltpu.PrefetchScalarGridSpec(
+                num_scalar_prefetch=1,
+                grid=(owners // pairs,),
+                in_specs=[block] + [spec for _, layout, _ in terms for spec in (*term_specs(layout), whole)],
+                out_specs=[block, gram_spec] if final else block,
+            ),
+            out_shape=[shape, gram_shape] if final else shape,
+            compiler_params=pltpu.CompilerParams(vmem_limit_bytes=VMEM_BYTES),
+            cost_estimate=pl.CostEstimate(
+                flops=2 * len(terms) * tokens * row_count * col_count,
+                bytes_accessed=2 * row_count * (len(terms) * tokens + 4 * col_count),
+                transcendentals=0,
+            ),
+        )(place, total, *arrays)
+
+    whole_pair = [[(core, 0, pair_rows, order) for core in range(2)] for order in range(2)]
+    halves = [(core, part * half, half, part) for part in range(2) for core in range(2)]
+    own = ([query_grads], [None], inputs)
+    one = ([near[0], near_got[0]], whole_pair[0], moved_1)
+    two = ([far[0], far_got[0], far[1], far_got[1]], halves, moved_2)
+    three = ([near[1], near_got[1]], whole_pair[1], moved_3)
+    total = accumulate(momentum, [own, one], MOMENTUM_DECAY, False)
+    total = accumulate(total, [two], None, False)
+    new_momentum, gram = accumulate(total, [three], None, True)
+
+    four = gram[:4] + over(1, gram[4:])
+    pieces = [four[0]] + [over(2 * i, four[i]) for i in range(1, 4)]
+    factor = pl.pallas_call(
+        polynomial_kernel,
+        out_shape=jax.ShapeDtypeStruct(pieces[0].shape, jnp.float32),
+        compiler_params=pltpu.CompilerParams(vmem_limit_bytes=SMALL_BYTES),
+    )(*pieces)
+    factors = jnp.stack([factor] + [over(2 * i, factor) for i in range(1, 4)])
+    others = over(1, factors)
+
+    def update_half(core, values, *before):
+        def spec():
+            return pl.BlockSpec((pair_rows, col_count), lambda i, place: (pair_of(i + core * (owners // 2), place), 0))
+
+        return pl.pallas_call(
+            functools.partial(update_kernel, math.sqrt(model_width)),
+            grid_spec=pltpu.PrefetchScalarGridSpec(
+                num_scalar_prefetch=1,
+                grid=(owners // 2,),
+                in_specs=[
+                    pl.BlockSpec((1, pair_heads, HEAD_DIM, HEAD_DIM), lambda i, place: (i, 0, 0, 0)),
+                    spec(),
+                ]
+                + [pl.BlockSpec(memory_space=pl.ANY)] * len(before),
+                out_specs=spec(),
+            ),
+            out_shape=jax.ShapeDtypeStruct((row_count, col_count), jnp.float32),
+            input_output_aliases={3: 0} if before else {},
+            compiler_params=pltpu.CompilerParams(vmem_limit_bytes=SMALL_BYTES),
+            cost_estimate=pl.CostEstimate(
+                flops=3 * row_count * col_count * HEAD_DIM, bytes_accessed=4 * row_count * col_count, transcendentals=0
+            ),
+        )(place, values, new_momentum, *before)
+
+    return new_momentum, update_half(1, others, update_half(0, factors))
 
 
 def polynomial(gram_matrix):
@@ -36,9 +255,8 @@
     return factor / norm_scale[:, None, None]
 
 
-def shards(inputs, query_grads, momentum):
-    row_count = momentum.shape[0]
-    col_count = momentum.shape[1]
+def plain_shards(model_width, inputs, query_grads, momentum):
+    row_count, col_count = momentum.shape
     gradient = lax.psum_scatter(
         lax.dot_general(query_grads, inputs, CONTRACT_TOKENS, preferred_element_type=jnp.float32),
         "dp",
@@ -53,26 +271,29 @@
     slot_count = -(-local_heads // owners)
     padded = jnp.pad(partial_value, ((0, slot_count * owners - local_heads), (0, 0), (0, 0)))
     owned_gram = lax.psum_scatter(
-        padded.reshape(slot_count, owners, HEAD_DIM, HEAD_DIM),
-        "cols",
-        scatter_dimension=1,
-        tiled=True,
+        padded.reshape(slot_count, owners, HEAD_DIM, HEAD_DIM), "cols", scatter_dimension=1, tiled=True
     )
     owned_factor = polynomial(owned_gram.reshape(slot_count, HEAD_DIM, HEAD_DIM))
     returned = lax.all_gather(
         owned_factor.reshape(slot_count, 1, HEAD_DIM, HEAD_DIM), "cols", axis=1, tiled=True
     )
     factor = returned.reshape(slot_count * owners, HEAD_DIM, HEAD_DIM)[:local_heads]
-    update = math.sqrt(D) * jnp.einsum("hij,hjk->hik", factor, blocks, precision=HIGHEST)
-    return (new_momentum, update.reshape(row_count, col_count))
+    update = math.sqrt(model_width) * jnp.einsum("hij,hjk->hik", factor, blocks, precision=HIGHEST)
+    return new_momentum, update.reshape(row_count, col_count)
 
 
 def solution(mesh):
-    placed = (P("dp", "cols"), P("dp", None), P("dp", "cols"))
-    return jax.shard_map(
-        shards,
-        mesh=mesh,
-        in_specs=placed,
-        out_specs=(P("dp", "cols"), P("dp", "cols")),
-        check_vma=False,
-    )
+    depth, owners = mesh.shape["dp"], mesh.shape["cols"]
+
+    def run(inputs, query_grads, momentum):
+        local_heads = momentum.shape[0] // depth // HEAD_DIM
+        chosen = shards if (depth, owners) == (4, 8) and local_heads % owners == 0 else plain_shards
+        return jax.shard_map(
+            functools.partial(chosen, momentum.shape[1]),
+            mesh=mesh,
+            in_specs=(P("dp", "cols"), P("dp", None), P("dp", "cols")),
+            out_specs=(P("dp", "cols"), P("dp", "cols")),
+            check_vma=False,
+        )(inputs, query_grads, momentum)
+
+    return run

time: 406 us -> 178 us (0.44)
  waiting for transfers between devices: 343 us -> 124 us
  matrix products: 33.6 us -> 0 us
  Pallas kernels: 0 us -> 27.1 us
  starting transfers between devices: 0.3 us -> 23.5 us
  between operations: 13.9 us -> 0.89 us
  local copies, waits for them, and re-layouts: 9.58 us -> 2.79 us
  other arithmetic: 4.57 us -> 0.3 us
    reduce_scatter x2 -> x0, waiting for transfers between devices: 320 us -> none  [the longest x1 283 us: shards(): lax.psum_scatter(lax.dot_general(query_grads, inputs, CONTRACT_TOKENS, pr...]
    ppermute x0 -> x26, waiting for transfers between devices: none -> 124 us  [the longest x20 64 us: over(): return lax.ppermute(value, 'cols', [(i, i ^ bits) for i in range(owners)])]
    dot_general x21 -> x0, matrix products: 33.6 us -> none  [the longest x1 15.8 us: shards(): lax.dot_general(query_grads, inputs, CONTRACT_TOKENS, preferred_element_t...]
    pallas_call x0 -> x6, Pallas kernels: none -> 27.1 us  [the longest x3 16.9 us: accumulate(): pl.pallas_call(functools.partial(accumulate_kernel, layouts, decay, final...]
    all_gather x1 -> x0, waiting for transfers between devices: 23.6 us -> none  [shards(): lax.all_gather(owned_factor.reshape(slot_count, 1, HEAD_DIM, HEAD_DIM), '...]
    ppermute x0 -> x26, starting transfers between devices: none -> 23.5 us  [the longest x20 17.2 us: over(): return lax.ppermute(value, 'cols', [(i, i ^ bits) for i in range(owners)])]
    reshape x2 -> x0, local copies, waits for them, and re-layouts: 6.62 us -> none  [the longest x1 5.56 us: shards(): owned_gram.reshape(slot_count, HEAD_DIM, HEAD_DIM)]
    add x2 -> x1, other arithmetic: 4.51 us -> 0.08 us  [shards(): four = gram[:4] + over(1, gram[4:])]
  transfers between devices with their start and end apart: 3 -> 26, of which waited for: 3 -> 18; matrix products, arithmetic and copies ran while one was open for 0% -> 0% of each run, Pallas kernels for 0% -> 8%
where the time goes in v1:
time: 178 us
  waiting for transfers between devices  124 us (70%)
  Pallas kernels  27.1 us (15%)
  starting transfers between devices  23.5 us (13%)
  local copies, waits for them, and re-layouts  2.79 us (2%)
    ppermute x20, waiting for transfers between devices, over(): return lax.ppermute(value, 'cols', [(i, i ^ bits) for i in range(owners)])  64 us
    ppermute x6, waiting for transfers between devices, onward(): lax.ppermute(value, 'dp', [(i, (i + k) % depth) for i in range(depth)])  59.7 us
    ppermute x20, starting transfers between devices, over(): return lax.ppermute(value, 'cols', [(i, i ^ bits) for i in range(owners)])  17.2 us
    pallas_call x3, Pallas kernels, accumulate(): pl.pallas_call(functools.partial(accumulate_kernel, layouts, decay, final...  16.9 us
    pallas_call x2, Pallas kernels, update_half(): pl.pallas_call(functools.partial(update_kernel, math.sqrt(model_width)),...  6.58 us
    ppermute x6, starting transfers between devices, onward(): lax.ppermute(value, 'dp', [(i, (i + k) % depth) for i in range(depth)])  6.21 us
    pallas_call x1, Pallas kernels, shards(): pl.pallas_call(polynomial_kernel, out_shape=jax.ShapeDtypeStruct(pieces[0...  3.62 us
  transfers between devices with their start and end apart: 26, of which 18 were waited for; matrix products, arithmetic and copies ran while one was open for 0% of the time, Pallas kernels for 8%

profile of v1, /device:TPU:0, one launch (start us, length us, event | category | flops | bytes accessed | tf_op | source)
XLA Modules:
  0.0 178.2 jit_solution(9135880314523976241)
XLA Ops:
  0.7 1.5 constant_dynamic-slice_fusion
  2.1 0.2 copy.9
  2.4 3.1 %collective-permute-start = (bf16[256,1024]{1,0:T(8,128)(2,1)S(1)}, bf16[256,1024]{1,0:T(8,128)(2,1)S(1)}, u32[]{:S(2)}, u32[]{:S(2)}) collective-permute-start(bf16[256,1024]{1,0:T(8,128)(2,1)S(1)} %bitcast.29), channel_id=1, source_target_pairs={{0,8},{8,16},{16,24},{24,0},{1,9},{9,17},{17,25},{25,1},{2,10},{10... | collective-permute-start | bytes 1572872 | tf_op jit(solution)/shard_map/ppermute | solution.py:109
  5.4 0.2 copy.10
  5.6 2.1 %collective-permute-start.1 = (bf16[256,1024]{1,0:T(8,128)(2,1)S(1)}, bf16[256,1024]{1,0:T(8,128)(2,1)S(1)}, u32[]{:S(2)}, u32[]{:S(2)}) collective-permute-start(bf16[256,1024]{1,0:T(8,128)(2,1)S(1)} %bitcast.30), channel_id=1, source_target_pairs={{0,24},{8,0},{16,8},{24,16},{1,25},{9,1},{17,9},{25,17},{2,26},{10... | collective-permute-start | bytes 1572872 | tf_op jit(solution)/shard_map/ppermute | solution.py:109
  7.7 0.2 copy.11
  7.9 12.3 %collective-permute-done = bf16[256,1024]{1,0:T(8,128)(2,1)S(1)} collective-permute-done((bf16[256,1024]{1,0:T(8,128)(2,1)S(1)}, bf16[256,1024]{1,0:T(8,128)(2,1)S(1)}, u32[]{:S(2)}, u32[]{:S(2)}) %collective-permute-start) | collective-permute-done | bytes 524320 | tf_op jit(solution)/shard_map/ppermute | solution.py:109
  20.3 10.1 %collective-permute-done.1 = bf16[256,1024]{1,0:T(8,128)(2,1)S(1)} collective-permute-done((bf16[256,1024]{1,0:T(8,128)(2,1)S(1)}, bf16[256,1024]{1,0:T(8,128)(2,1)S(1)}, u32[]{:S(2)}, u32[]{:S(2)}) %collective-permute-start.1) | collective-permute-done | bytes 524320 | tf_op jit(solution)/shard_map/ppermute | solution.py:109
  30.3 1.5 collective-permute-start.3
  31.8 1.0 collective-permute-start.2
  32.9 1.5 collective-permute-start.4
  34.4 9.4 %collective-permute-done.3 = bf16[1,256,1024]{2,1,0:T(8,128)(2,1)S(1)} collective-permute-done((bf16[1,256,1024]{2,1,0:T(8,128)(2,1)S(1)}, bf16[1,256,1024]{2,1,0:T(8,128)(2,1)S(1)}, u32[]{:S(2)}, u32[]{:S(2)}) %collective-permute-start.3) | collective-permute-done | bytes 524320 | tf_op jit(solution)/shard_map/ppermute | solution.py:106
  43.8 13.4 %collective-permute-done.2 = bf16[256,1024]{1,0:T(8,128)(2,1)S(1)} collective-permute-done((bf16[256,1024]{1,0:T(8,128)(2,1)S(1)}, bf16[256,1024]{1,0:T(8,128)(2,1)S(1)}, u32[]{:S(2)}, u32[]{:S(2)}) %collective-permute-start.2) | collective-permute-done | bytes 524320 | tf_op jit(solution)/shard_map/ppermute | solution.py:109
  57.3 0.6 collective-permute-start.6
  57.9 1.6 collective-permute-start.5
  59.5 22.2 %collective-permute-done.6 = bf16[2,256,1024]{2,1,0:T(8,128)(2,1)S(1)} collective-permute-done((bf16[2,256,1024]{2,1,0:T(8,128)(2,1)S(1)}, bf16[2,256,1024]{2,1,0:T(8,128)(2,1)S(1)}, u32[]{:S(2)}, u32[]{:S(2)}) %collective-permute-start.6) | collective-permute-done | bytes 1048608 | tf_op jit(solution)/shard_map/ppermute | solution.py:106
  81.7 0.3 collective-permute-done.5
  82.0 3.1 %collective-permute-done.7.refs_4_ = bf16[1024,512]{1,0:T(8,128)(2,1)S(1)} collective-permute-done((bf16[1024,512]{1,0:T(8,128)(2,1)S(1)}, bf16[1024,512]{1,0:T(8,128)(2,1)S(1)}, u32[]{:S(2)}, u32[]{:S(2)}) %collective-permute-start.7) | collective-permute-done | bytes 1048608 | tf_op jit(solution)/shard_map/ppermute | solution.py:109
  85.5 0.6 collective-permute-start.10
  86.1 1.5 collective-permute-start.8
  87.6 0.5 collective-permute-start.9
  88.2 6.3 %collective-permute-done.8 = bf16[1,128,1024]{2,1,0:T(8,128)(2,1)S(1)} collective-permute-done((bf16[1,128,1024]{2,1,0:T(8,128)(2,1)S(1)}, bf16[1,128,1024]{2,1,0:T(8,128)(2,1)S(1)}, u32[]{:S(2)}, u32[]{:S(2)}) %collective-permute-start.8) | collective-permute-done | bytes 262176 | tf_op jit(solution)/shard_map/ppermute | solution.py:106
  94.5 0.5 collective-permute-start.12
  95.1 0.6 collective-permute-done.9
  95.7 1.0 collective-permute-start.13
  96.7 11.0 %collective-permute-done.12 = bf16[2,128,1024]{2,1,0:T(8,128)(2,1)S(1)} collective-permute-done((bf16[2,128,1024]{2,1,0:T(8,128)(2,1)S(1)}, bf16[2,128,1024]{2,1,0:T(8,128)(2,1)S(1)}, u32[]{:S(2)}, u32[]{:S(2)}) %collective-permute-start.12) | collective-permute-done | bytes 524320 | tf_op jit(solution)/shard_map/ppermute | solution.py:106
  107.7 0.8 collective-permute-done.13
  108.5 4.5 %collective-permute-done.14.refs_4_ = bf16[1024,512]{1,0:T(8,128)(2,1)S(1)} collective-permute-done((bf16[1024,512]{1,0:T(8,128)(2,1)S(1)}, bf16[1024,512]{1,0:T(8,128)(2,1)S(1)}, u32[]{:S(2)}, u32[]{:S(2)}) %collective-permute-start.14) | collective-permute-done | bytes 1048608 | tf_op jit(solution)/shard_map/ppermute | solution.py:109
  113.3 0.6 collective-permute-start.15
  113.9 6.9 %shard_map.50.total = f32[2048,512]{1,0:T(8,128)S(1)} custom-call(s32[2]{0:T(128)S(1)} %pad_add_fusion.place, f32[2048,512]{1,0:T(8,128)S(1)} %copy-done.1, bf16[1024,8192]{1,0:T(8,128)(2,1)} %refs_0_.1, bf16[1024,512]{1,0:T(8,128)(2,1)S(1)} %copy-done.2, bf16[4,256,1024]{2,1,0:T(8,128)(2,1)S(1)} %constant_dynamic-update-slice_fusion.4.refs_2_, ...), custom_call_target="tpu_custom_call" | custom-call | flops 4294967296 | bytes 16777216 | tf_op jit(solution)/shard_map/pallas_call | solution.py:177
  120.9 3.5 %shard_map.51.total = f32[2048,512]{1,0:T(8,128)S(1)} custom-call(s32[2]{0:T(128)S(1)} %pad_add_fusion.place, f32[2048,512]{1,0:T(8,128)S(1)} %shard_map.50.total, bf16[4,128,1024]{2,1,0:T(8,128)(2,1)S(1)} %constant_dynamic-update-slice_fusion.8.refs_0_, bf16[4,128,1024]{2,1,0:T(8,128)(2,1)S(1)} %collective-permute-done.15.refs_1_, ...), custom_call_target="tpu_custom_call" | custom-call | flops 2147483648 | bytes 12582912 | tf_op jit(solution)/shard_map/pallas_call | solution.py:177
  124.4 16.3 %collective-permute-done.17.refs_2_ = bf16[1024,512]{1,0:T(8,128)(2,1)S(1)} collective-permute-done((bf16[1024,512]{1,0:T(8,128)(2,1)S(1)}, bf16[1024,512]{1,0:T(8,128)(2,1)S(1)}, u32[]{:S(2)}, u32[]{:S(2)}) %collective-permute-start.17) | collective-permute-done | bytes 1048608 | tf_op jit(solution)/shard_map/ppermute | solution.py:109
  140.8 6.4 %shard_map.52 = (f32[2048,512]{1,0:T(8,128)}, f32[8,2,128,128]{3,2,1,0:T(8,128)S(1)}) custom-call(s32[2]{0:T(128)S(1)} %pad_add_fusion.place, f32[2048,512]{1,0:T(8,128)S(1)} %shard_map.51.total, bf16[4,256,1024]{2,1,0:T(8,128)(2,1)S(1)} %constant_dynamic-update-slice_fusion.6.refs_0_, bf16[4,256,1024]{2,1,0:T(8,128)(2,1)S(1)} %collective-permute-done.11.refs_1_, ...), custom_call_target="tpu_custom_call" | custom-call | flops 2147483648 | bytes 12582912 | tf_op jit(solution)/shard_map/pallas_call | solution.py:177
  147.3 1.9 %collective-permute-done.18 = f32[4,2,128,128]{3,2,1,0:T(8,128)S(1)} collective-permute-done((f32[4,2,128,128]{3,2,1,0:T(8,128)S(1)}, f32[4,2,128,128]{3,2,1,0:T(8,128)S(1)}, u32[]{:S(2)}, u32[]{:S(2)}) %collective-permute-start.18) | collective-permute-done | bytes 524320 | tf_op jit(solution)/shard_map/ppermute | solution.py:106
  149.2 0.1 slice_add_fusion
  149.3 1.5 collective-permute-start.21
  150.8 0.5 collective-permute-start.20
  151.3 1.6 collective-permute-start.19
  152.9 3.8 %collective-permute-done.21.refs_3_ = f32[2,128,128]{2,1,0:T(8,128)S(1)} collective-permute-done((f32[2,128,128]{2,1,0:T(8,128)S(1)}, f32[2,128,128]{2,1,0:T(8,128)S(1)}, u32[]{:S(2)}, u32[]{:S(2)}) %collective-permute-start.21) | collective-permute-done | bytes 131104 | tf_op jit(solution)/shard_map/ppermute | solution.py:106
  156.7 2.0 %collective-permute-done.20.refs_2_ = f32[2,128,128]{2,1,0:T(8,128)S(1)} collective-permute-done((f32[2,128,128]{2,1,0:T(8,128)S(1)}, f32[2,128,128]{2,1,0:T(8,128)S(1)}, u32[]{:S(2)}, u32[]{:S(2)}) %collective-permute-start.20) | collective-permute-done | bytes 131104 | tf_op jit(solution)/shard_map/ppermute | solution.py:106
  158.7 3.6 %shard_map.53 = f32[2,128,128]{2,1,0:T(8,128)S(1)} custom-call(f32[2,128,128]{2,1,0:T(8,128)S(1)} %get-tuple-element.62.refs_0_, f32[2,128,128]{2,1,0:T(8,128)S(1)} %collective-permute-done.19.refs_1_, f32[2,128,128]{2,1,0:T(8,128)S(1)} %collective-permute-done.20.refs_2_, f32[2,128,128]{2,1,0:T(8,128)S(1)} %collective-permute-done.21.refs_3_), custom_call_target="tpu_custom_call" | custom-call | tf_op jit(solution)/shard_map/pallas_call | solution.py:206
  162.3 1.5 collective-permute-start.24
  163.8 0.6 collective-permute-start.23
  164.3 1.5 collective-permute-start.22
  165.9 3.8 %collective-permute-done.24 = f32[2,128,128]{2,1,0:T(8,128)S(1)} collective-permute-done((f32[2,128,128]{2,1,0:T(8,128)S(1)}, f32[2,128,128]{2,1,0:T(8,128)S(1)}, u32[]{:S(2)}, u32[]{:S(2)}) %collective-permute-start.24) | collective-permute-done | bytes 131104 | tf_op jit(solution)/shard_map/ppermute | solution.py:106
  169.6 1.8 %collective-permute-done.23 = f32[2,128,128]{2,1,0:T(8,128)S(1)} collective-permute-done((f32[2,128,128]{2,1,0:T(8,128)S(1)}, f32[2,128,128]{2,1,0:T(8,128)S(1)}, u32[]{:S(2)}, u32[]{:S(2)}) %collective-permute-start.23) | collective-permute-done | bytes 131104 | tf_op jit(solution)/shard_map/ppermute | solution.py:106
  171.6 3.3 %shard_map.54.refs_0_ = f32[2048,512]{1,0:T(8,128)} custom-call(s32[2]{0:T(128)S(1)} %pad_add_fusion.place, f32[4,2,128,128]{3,2,1,0:T(8,128)S(1)} %pad_maximum_fusion.2.factor, f32[2048,512]{1,0:T(8,128)S(1)} %copy-done), custom_call_target="tpu_custom_call" | custom-call | flops 402653184 | bytes 4194304 | tf_op jit(solution)/shard_map/pallas_call | solution.py:218
  174.9 3.3 %shard_map.55 = f32[2048,512]{1,0:T(8,128)} custom-call(s32[2]{0:T(128)S(1)} %pad_add_fusion.place, f32[4,2,128,128]{3,2,1,0:T(8,128)S(1)} %collective-permute-done.25.factor, f32[2048,512]{1,0:T(8,128)S(1)} %copy-done, f32[2048,512]{1,0:T(8,128)} %shard_map.54.refs_0_), custom_call_target="tpu_custom_call", output_to_operand_aliasing={{}: (3, {})} | custom-call | flops 402653184 | bytes 4194304 | tf_op jit(solution)/shard_map/pallas_call | solution.py:218
  (40 shorter events, 1.2 us)
Async XLA Ops:
  2.4 17.9 %collective-permute-start = (bf16[256,1024]{1,0:T(8,128)(2,1)S(1)}, bf16[256,1024]{1,0:T(8,128)(2,1)S(1)}, u32[]{:S(2)}, u32[]{:S(2)}) collective-permute-start(bf16[256,1024]{1,0:T(8,128)(2,1)S(1)} %bitcast.29), channel_id=1, source_target_pairs={{0,8},{8,16},{16,24},{24,0},{1,9},{9,17},{17,25},{25,1},{2,10},{10... | collective-permute-start | bytes 1572872 | tf_op jit(solution)/shard_map/ppermute | solution.py:109
  5.6 24.7 %collective-permute-start.1 = (bf16[256,1024]{1,0:T(8,128)(2,1)S(1)}, bf16[256,1024]{1,0:T(8,128)(2,1)S(1)}, u32[]{:S(2)}, u32[]{:S(2)}) collective-permute-start(bf16[256,1024]{1,0:T(8,128)(2,1)S(1)} %bitcast.30), channel_id=1, source_target_pairs={{0,24},{8,0},{16,8},{24,16},{1,25},{9,1},{17,9},{25,17},{2,26},{10... | collective-permute-start | bytes 1572872 | tf_op jit(solution)/shard_map/ppermute | solution.py:109
  30.3 13.5 %collective-permute-start.3 = (bf16[1,256,1024]{2,1,0:T(8,128)(2,1)S(1)}, bf16[1,256,1024]{2,1,0:T(8,128)(2,1)S(1)}, u32[]{:S(2)}, u32[]{:S(2)}) collective-permute-start(bf16[1,256,1024]{2,1,0:T(8,128)(2,1)S(1)} %bitcast.24), channel_id=1, source_target_pairs={{0,4},{1,5},{2,6},{3,7},{4,0},{5,1},{6,2},{7,3},{8,12},{9,13},{10,... | collective-permute-start | bytes 1572872 | tf_op jit(solution)/shard_map/ppermute | solution.py:106
  31.8 25.3 %collective-permute-start.2 = (bf16[256,1024]{1,0:T(8,128)(2,1)S(1)}, bf16[256,1024]{1,0:T(8,128)(2,1)S(1)}, u32[]{:S(2)}, u32[]{:S(2)}) collective-permute-start(bf16[256,1024]{1,0:T(8,128)(2,1)S(1)} %bitcast.28), channel_id=1, source_target_pairs={{0,16},{8,24},{16,0},{24,8},{1,17},{9,25},{17,1},{25,9},{2,18},{10... | collective-permute-start | bytes 1572872 | tf_op jit(solution)/shard_map/ppermute | solution.py:109
  32.9 26.6 %copy-start.2 = (bf16[1024,512]{1,0:T(8,128)(2,1)S(1)}, bf16[1024,512]{1,0:T(8,128)(2,1)}, u32[]{:S(2)}) copy-start(bf16[1024,512]{1,0:T(8,128)(2,1)} %refs_1_.1) | copy-start | bytes 3145732
  32.9 24.3 %collective-permute-start.4 = (bf16[1,256,1024]{2,1,0:T(8,128)(2,1)S(1)}, bf16[1,256,1024]{2,1,0:T(8,128)(2,1)S(1)}, u32[]{:S(2)}, u32[]{:S(2)}) collective-permute-start(bf16[1,256,1024]{2,1,0:T(8,128)(2,1)S(1)} %bitcast.26), channel_id=1, source_target_pairs={{0,2},{1,3},{2,0},{3,1},{4,6},{5,7},{6,4},{7,5},{8,10},{9,11},{10,... | collective-permute-start | bytes 1572872 | tf_op jit(solution)/shard_map/ppermute | solution.py:106
  57.3 24.4 %collective-permute-start.6 = (bf16[2,256,1024]{2,1,0:T(8,128)(2,1)S(1)}, bf16[2,256,1024]{2,1,0:T(8,128)(2,1)S(1)}, u32[]{:S(2)}, u32[]{:S(2)}) collective-permute-start(bf16[2,256,1024]{2,1,0:T(8,128)(2,1)S(1)} %constant_dynamic-update-slice_fusion.2), channel_id=1, source_target_pairs={{0,4},{1,5},{2,6},{3,7},{4,0},{5,1},{6,2},{7,3},{8,12},{9,13},{10,... | collective-permute-start | bytes 3145736 | tf_op jit(solution)/shard_map/ppermute | solution.py:106
  57.9 24.1 %collective-permute-start.5 = (bf16[2,256,1024]{2,1,0:T(8,128)(2,1)S(1)}, bf16[2,256,1024]{2,1,0:T(8,128)(2,1)S(1)}, u32[]{:S(2)}, u32[]{:S(2)}) collective-permute-start(bf16[2,256,1024]{2,1,0:T(8,128)(2,1)S(1)} %constant_dynamic-update-slice_fusion), channel_id=1, source_target_pairs={{0,2},{1,3},{2,0},{3,1},{4,6},{5,7},{6,4},{7,5},{8,10},{9,11},{10,... | collective-permute-start | bytes 3145736 | tf_op jit(solution)/shard_map/ppermute | solution.py:106
  59.5 25.6 %collective-permute-start.7 = (bf16[1024,512]{1,0:T(8,128)(2,1)S(1)}, bf16[1024,512]{1,0:T(8,128)(2,1)S(1)}, u32[]{:S(2)}, u32[]{:S(2)}) collective-permute-start(bf16[1024,512]{1,0:T(8,128)(2,1)S(1)} %copy-done.2), channel_id=1, source_target_pairs={{0,8},{8,16},{16,24},{24,0},{1,9},{9,17},{17,25},{25,1},{2,10},{10... | collective-permute-start | bytes 3145736 | tf_op jit(solution)/shard_map/ppermute | solution.py:109
  85.4 27.6 %collective-permute-start.11 = (bf16[4,256,1024]{2,1,0:T(8,128)(2,1)S(1)}, bf16[4,256,1024]{2,1,0:T(8,128)(2,1)S(1)}, u32[]{:S(2)}, u32[]{:S(2)}) collective-permute-start(bf16[4,256,1024]{2,1,0:T(8,128)(2,1)S(1)} %constant_dynamic-update-slice_fusion.6.refs_0_), channel_id=1, source_target_pairs={{0,1},{1,0},{2,3},{3,2},{4,5},{5,4},{6,7},{7,6},{8,9},{9,8},{10,11... | collective-permute-start | bytes 6291464 | tf_op jit(solution)/shard_map/ppermute | solution.py:106
  85.5 27.5 %collective-permute-start.10 = (bf16[4,256,1024]{2,1,0:T(8,128)(2,1)S(1)}, bf16[4,256,1024]{2,1,0:T(8,128)(2,1)S(1)}, u32[]{:S(2)}, u32[]{:S(2)}) collective-permute-start(bf16[4,256,1024]{2,1,0:T(8,128)(2,1)S(1)} %constant_dynamic-update-slice_fusion.4.refs_2_), channel_id=1, source_target_pairs={{0,1},{1,0},{2,3},{3,2},{4,5},{5,4},{6,7},{7,6},{8,9},{9,8},{10,11... | collective-permute-start | bytes 6291464 | tf_op jit(solution)/shard_map/ppermute | solution.py:106
  86.1 26.9 %collective-permute-start.14 = (bf16[1024,512]{1,0:T(8,128)(2,1)S(1)}, bf16[1024,512]{1,0:T(8,128)(2,1)S(1)}, u32[]{:S(2)}, u32[]{:S(2)}) collective-permute-start(bf16[1024,512]{1,0:T(8,128)(2,1)S(1)} %collective-permute-done.7.refs_4_), channel_id=1, source_target_pairs={{0,8},{8,16},{16,24},{24,0},{1,9},{9,17},{17,25},{25,1},{2,10},{10... | collective-permute-start | bytes 3145736 | tf_op jit(solution)/shard_map/ppermute | solution.py:109
  86.1 8.4 %collective-permute-start.8 = (bf16[1,128,1024]{2,1,0:T(8,128)(2,1)S(1)}, bf16[1,128,1024]{2,1,0:T(8,128)(2,1)S(1)}, u32[]{:S(2)}, u32[]{:S(2)}) collective-permute-start(bf16[1,128,1024]{2,1,0:T(8,128)(2,1)S(1)} %get-tuple-element.64), channel_id=1, source_target_pairs={{0,4},{1,5},{2,6},{3,7},{4,0},{5,1},{6,2},{7,3},{8,12},{9,13},{10,... | collective-permute-start | bytes 786440 | tf_op jit(solution)/shard_map/ppermute | solution.py:106
  87.6 8.0 %collective-permute-start.9 = (bf16[1,128,1024]{2,1,0:T(8,128)(2,1)S(1)}, bf16[1,128,1024]{2,1,0:T(8,128)(2,1)S(1)}, u32[]{:S(2)}, u32[]{:S(2)}) collective-permute-start(bf16[1,128,1024]{2,1,0:T(8,128)(2,1)S(1)} %get-tuple-element.63), channel_id=1, source_target_pairs={{0,2},{1,3},{2,0},{3,1},{4,6},{5,7},{6,4},{7,5},{8,10},{9,11},{10,... | collective-permute-start | bytes 786440 | tf_op jit(solution)/shard_map/ppermute | solution.py:106
  94.5 13.1 %collective-permute-start.12 = (bf16[2,128,1024]{2,1,0:T(8,128)(2,1)S(1)}, bf16[2,128,1024]{2,1,0:T(8,128)(2,1)S(1)}, u32[]{:S(2)}, u32[]{:S(2)}) collective-permute-start(bf16[2,128,1024]{2,1,0:T(8,128)(2,1)S(1)} %pad_maximum_fusion), channel_id=1, source_target_pairs={{0,2},{1,3},{2,0},{3,1},{4,6},{5,7},{6,4},{7,5},{8,10},{9,11},{10,... | collective-permute-start | bytes 1572872 | tf_op jit(solution)/shard_map/ppermute | solution.py:106
  95.7 18.2 %copy-start.1 = (f32[2048,512]{1,0:T(8,128)S(1)}, f32[2048,512]{1,0:T(8,128)}, u32[]{:S(2)}) copy-start(f32[2048,512]{1,0:T(8,128)} %total.1) | copy-start | bytes 12582916
  95.7 12.8 %collective-permute-start.13 = (bf16[2,128,1024]{2,1,0:T(8,128)(2,1)S(1)}, bf16[2,128,1024]{2,1,0:T(8,128)(2,1)S(1)}, u32[]{:S(2)}, u32[]{:S(2)}) collective-permute-start(bf16[2,128,1024]{2,1,0:T(8,128)(2,1)S(1)} %pad_maximum_fusion.1), channel_id=1, source_target_pairs={{0,4},{1,5},{2,6},{3,7},{4,0},{5,1},{6,2},{7,3},{8,12},{9,13},{10,... | collective-permute-start | bytes 1572872 | tf_op jit(solution)/shard_map/ppermute | solution.py:106
  113.2 7.7 %collective-permute-start.16 = (bf16[4,128,1024]{2,1,0:T(8,128)(2,1)S(1)}, bf16[4,128,1024]{2,1,0:T(8,128)(2,1)S(1)}, u32[]{:S(2)}, u32[]{:S(2)}) collective-permute-start(bf16[4,128,1024]{2,1,0:T(8,128)(2,1)S(1)} %constant_dynamic-update-slice_fusion.10.refs_2_), channel_id=1, source_target_pairs={{0,1},{1,0},{2,3},{3,2},{4,5},{5,4},{6,7},{7,6},{8,9},{9,8},{10,11... | collective-permute-start | bytes 3145736 | tf_op jit(solution)/shard_map/ppermute | solution.py:106
  113.3 7.6 %collective-permute-start.15 = (bf16[4,128,1024]{2,1,0:T(8,128)(2,1)S(1)}, bf16[4,128,1024]{2,1,0:T(8,128)(2,1)S(1)}, u32[]{:S(2)}, u32[]{:S(2)}) collective-permute-start(bf16[4,128,1024]{2,1,0:T(8,128)(2,1)S(1)} %constant_dynamic-update-slice_fusion.8.refs_0_), channel_id=1, source_target_pairs={{0,1},{1,0},{2,3},{3,2},{4,5},{5,4},{6,7},{7,6},{8,9},{9,8},{10,11... | collective-permute-start | bytes 3145736 | tf_op jit(solution)/shard_map/ppermute | solution.py:106
  113.8 26.9 %collective-permute-start.17 = (bf16[1024,512]{1,0:T(8,128)(2,1)S(1)}, bf16[1024,512]{1,0:T(8,128)(2,1)S(1)}, u32[]{:S(2)}, u32[]{:S(2)}) collective-permute-start(bf16[1024,512]{1,0:T(8,128)(2,1)S(1)} %collective-permute-done.14.refs_4_), channel_id=1, source_target_pairs={{0,8},{8,16},{16,24},{24,0},{1,9},{9,17},{17,25},{25,1},{2,10},{10... | collective-permute-start | bytes 3145736 | tf_op jit(solution)/shard_map/ppermute | solution.py:109
  147.2 24.4 %copy-start = (f32[2048,512]{1,0:T(8,128)S(1)}, f32[2048,512]{1,0:T(8,128)}, u32[]{:S(2)}) copy-start(f32[2048,512]{1,0:T(8,128)} %get-tuple-element.27.block) | copy-start | bytes 12582916
  147.2 2.0 %collective-permute-start.18 = (f32[4,2,128,128]{3,2,1,0:T(8,128)S(1)}, f32[4,2,128,128]{3,2,1,0:T(8,128)S(1)}, u32[]{:S(2)}, u32[]{:S(2)}) collective-permute-start(f32[4,2,128,128]{3,2,1,0:T(8,128)S(1)} %slice.27), channel_id=1, source_target_pairs={{0,1},{1,0},{2,3},{3,2},{4,5},{5,4},{6,7},{7,6},{8,9},{9,8},{10,11... | collective-permute-start | bytes 1572872 | tf_op jit(solution)/shard_map/ppermute | solution.py:106
  149.3 7.3 %collective-permute-start.21 = (f32[2,128,128]{2,1,0:T(8,128)S(1)}, f32[2,128,128]{2,1,0:T(8,128)S(1)}, u32[]{:S(2)}, u32[]{:S(2)}) collective-permute-start(f32[2,128,128]{2,1,0:T(8,128)S(1)} %get-tuple-element.59), channel_id=1, source_target_pairs={{0,6},{1,7},{2,4},{3,5},{4,2},{5,3},{6,0},{7,1},{8,14},{9,15},{10,... | collective-permute-start | bytes 393224 | tf_op jit(solution)/shard_map/ppermute | solution.py:106
  150.8 7.8 %collective-permute-start.20 = (f32[2,128,128]{2,1,0:T(8,128)S(1)}, f32[2,128,128]{2,1,0:T(8,128)S(1)}, u32[]{:S(2)}, u32[]{:S(2)}) collective-permute-start(f32[2,128,128]{2,1,0:T(8,128)S(1)} %get-tuple-element.60), channel_id=1, source_target_pairs={{0,4},{1,5},{2,6},{3,7},{4,0},{5,1},{6,2},{7,3},{8,12},{9,13},{10,... | collective-permute-start | bytes 393224 | tf_op jit(solution)/shard_map/ppermute | solution.py:106
  151.3 7.3 %collective-permute-start.19 = (f32[2,128,128]{2,1,0:T(8,128)S(1)}, f32[2,128,128]{2,1,0:T(8,128)S(1)}, u32[]{:S(2)}, u32[]{:S(2)}) collective-permute-start(f32[2,128,128]{2,1,0:T(8,128)S(1)} %get-tuple-element.61), channel_id=1, source_target_pairs={{0,2},{1,3},{2,0},{3,1},{4,6},{5,7},{6,4},{7,5},{8,10},{9,11},{10,... | collective-permute-start | bytes 393224 | tf_op jit(solution)/shard_map/ppermute | solution.py:106
  162.3 7.3 %collective-permute-start.24 = (f32[2,128,128]{2,1,0:T(8,128)S(1)}, f32[2,128,128]{2,1,0:T(8,128)S(1)}, u32[]{:S(2)}, u32[]{:S(2)}) collective-permute-start(f32[2,128,128]{2,1,0:T(8,128)S(1)} %shard_map.53), channel_id=1, source_target_pairs={{0,6},{1,7},{2,4},{3,5},{4,2},{5,3},{6,0},{7,1},{8,14},{9,15},{10,... | collective-permute-start | bytes 393224 | tf_op jit(solution)/shard_map/ppermute | solution.py:106
  163.8 7.7 %collective-permute-start.23 = (f32[2,128,128]{2,1,0:T(8,128)S(1)}, f32[2,128,128]{2,1,0:T(8,128)S(1)}, u32[]{:S(2)}, u32[]{:S(2)}) collective-permute-start(f32[2,128,128]{2,1,0:T(8,128)S(1)} %shard_map.53), channel_id=1, source_target_pairs={{0,4},{1,5},{2,6},{3,7},{4,0},{5,1},{6,2},{7,3},{8,12},{9,13},{10,... | collective-permute-start | bytes 393224 | tf_op jit(solution)/shard_map/ppermute | solution.py:106
  164.3 7.1 %collective-permute-start.22 = (f32[2,128,128]{2,1,0:T(8,128)S(1)}, f32[2,128,128]{2,1,0:T(8,128)S(1)}, u32[]{:S(2)}, u32[]{:S(2)}) collective-permute-start(f32[2,128,128]{2,1,0:T(8,128)S(1)} %shard_map.53), channel_id=1, source_target_pairs={{0,2},{1,3},{2,0},{3,1},{4,6},{5,7},{6,4},{7,5},{8,10},{9,11},{10,... | collective-permute-start | bytes 393224 | tf_op jit(solution)/shard_map/ppermute | solution.py:106
  171.5 3.4 %collective-permute-start.25 = (f32[4,2,128,128]{3,2,1,0:T(8,128)S(1)}, f32[4,2,128,128]{3,2,1,0:T(8,128)S(1)}, u32[]{:S(2)}, u32[]{:S(2)}) collective-permute-start(f32[4,2,128,128]{3,2,1,0:T(8,128)S(1)} %pad_maximum_fusion.2.factor), channel_id=1, source_target_pairs={{0,1},{1,0},{2,3},{3,2},{4,5},{5,4},{6,7},{7,6},{8,9},{9,8},{10,11... | collective-permute-start | bytes 1572872 | tf_op jit(solution)/shard_map/ppermute | solution.py:106

commit v2 on v1

--- a/solution.py
+++ b/solution.py
@@ -33,13 +33,12 @@
     return dot(lh, rh) + (dot(lh, rl) + dot(ll, rh))
 
 
-def accumulate_kernel(layouts, decay, final, place, total, *refs):
-    refs = list(refs)
-    taken = [([refs.pop(0) for _ in layout], layout, refs.pop(0)) for layout in layouts]
-    out = refs.pop(0)
+def accumulate_kernel(layouts, decay, place, total, *refs):
+    refs, out = list(refs[:-1]), refs[-1]
     out[...] = total[...] * decay if decay else total[...]
     pair_rows = out.shape[0] // 2
-    for q_refs, layout, x_ref in taken:
+    for layout in layouts:
+        q_refs, x_ref = [refs.pop(0) for _ in layout], refs.pop(0)
         for q_ref, piece in zip(q_refs, layout):
             if piece is None:
                 out[...] += lax.dot_general(
@@ -50,16 +49,29 @@
             start = pl.multiple_of(((place[1] + core) % 2) * pair_rows + offset, count)
             value = jnp.dot(q_ref[0], x_ref[...], preferred_element_type=jnp.float32)
             out[pl.ds(start, count), :] += value
-    if not final:
-        return
-    gram = refs.pop(0)
-    pair_heads = gram.shape[1]
-    for head in range(out.shape[0] // HEAD_DIM):
-        parts = split(out[head * HEAD_DIM : (head + 1) * HEAD_DIM, :])
-        pair = pl.program_id(0) * 2 + head // pair_heads
-        other = place[1] ^ pair
-        slot = other // 2 + (other % 2) * (gram.shape[0] // 2)
-        gram[slot, head % pair_heads] = dot3(parts, parts, (((1,), (1,)), ((), ())))
+
+
+def rows_at(place, core, index, count):
+    return pl.ds(pl.multiple_of((place[1] ^ (2 * index + core)) * count, count), count)
+
+
+def last_kernel(core, place, total, queries, x_ref, *refs):
+    new_momentum, blocks, gram, sems = refs[-4:]
+    copies = []
+    count = queries.shape[1]
+    depth = queries.shape[2]
+    product = jnp.dot(queries[...].reshape(-1, depth), x_ref[...], preferred_element_type=jnp.float32)
+    for index in range(queries.shape[0]):
+        rows = rows_at(place, core, index, count)
+        value = total[rows, :] + product[index * count : (index + 1) * count, :]
+        blocks[index] = value
+        copies.append(pltpu.make_async_copy(blocks.at[index], new_momentum.at[rows, :], sems.at[index]))
+        copies[-1].start()
+        for head in range(gram.shape[1]):
+            parts = split(value[head * HEAD_DIM : (head + 1) * HEAD_DIM, :])
+            gram[index, head] = dot3(parts, parts, (((1,), (1,)), ((), ())))
+    for copy in copies:
+        copy.wait()
 
 
 def polynomial_kernel(*refs):
@@ -70,7 +82,10 @@
     cols = lax.broadcasted_iota(jnp.int32, (order, order), 1)
     identity = (rows == cols).astype(jnp.float32)
     heads = range(gram.shape[0])
-    dot = functools.partial(jnp.dot, precision=HIGHEST, preferred_element_type=jnp.float32)
+
+    def dot(left, right):
+        return dot3(split(left), split(right), (((1,), (0,)), ((), ())))
+
     norms = [jnp.sqrt(jnp.sum(gram[h] * identity)) + NORM_EPS for h in heads]
     current = [gram[h] / (norms[h] * norms[h]) for h in heads]
     factors = [None for h in heads]
@@ -85,12 +100,19 @@
         factor[h] = factors[h] / norms[h]
 
 
-def update_kernel(scale, place, factor, block, *refs):
-    update = refs[-1]
-    for head in range(factor.shape[1]):
-        rows = slice(head * HEAD_DIM, (head + 1) * HEAD_DIM)
-        product = dot3(split(factor[0, head]), split(block[rows, :]), (((1,), (0,)), ((), ())))
-        update[rows, :] = scale * product
+def update_kernel(scale, core, place, factor, blocks, *refs):
+    update, held, sems = refs[-3:]
+    copies = []
+    for index in range(blocks.shape[0]):
+        for head in range(factor.shape[1]):
+            rows = slice(head * HEAD_DIM, (head + 1) * HEAD_DIM)
+            product = dot3(split(factor[index, head]), split(blocks[index, rows, :]), (((1,), (0,)), ((), ())))
+            held[index, rows, :] = scale * product
+        rows = rows_at(place, core, index, blocks.shape[1])
+        copies.append(pltpu.make_async_copy(held.at[index], update.at[rows, :], sems.at[index]))
+        copies[-1].start()
+    for copy in copies:
+        copy.wait()
 
 
 def shards(model_width, inputs, query_grads, momentum):
@@ -152,10 +174,6 @@
         return pl.BlockSpec((pair_rows, columns), lambda i, place: (pair_of(i, place), part))
 
     pairs = 2
-    gram_dims = (owners, pair_heads, HEAD_DIM, HEAD_DIM)
-    gram_spec = pl.BlockSpec(gram_dims, lambda i, place: (0, 0, 0, 0))
-    gram_shape = jax.ShapeDtypeStruct(gram_dims, jnp.float32)
-
     def spots(order):
         def index_map(i, place):
             other = (place[1] // 2) ^ i
@@ -168,21 +186,21 @@
             return [pl.BlockSpec((tokens, pairs * pair_rows), lambda i, place: (0, place[0] * (owners // pairs) + i))]
         return [pl.BlockSpec((1, count, tokens), spots(order)) for _, _, count, order in layout]
 
-    def accumulate(total, terms, decay, final):
+    def accumulate(total, terms, decay):
         block = pl.BlockSpec((pairs * pair_rows, col_count), lambda i, place: (i, 0))
         whole = pl.BlockSpec((tokens, col_count), lambda i, place: (0, 0))
         arrays = [array for rows, _, x in terms for array in (*rows, x)]
         shape = jax.ShapeDtypeStruct((row_count, col_count), jnp.float32)
         layouts = [[piece and piece[:3] for piece in layout] for _, layout, _ in terms]
         return pl.pallas_call(
-            functools.partial(accumulate_kernel, layouts, decay, final),
+            functools.partial(accumulate_kernel, layouts, decay),
             grid_spec=pltpu.PrefetchScalarGridSpec(
                 num_scalar_prefetch=1,
                 grid=(owners // pairs,),
                 in_specs=[block] + [spec for _, layout, _ in terms for spec in (*term_specs(layout), whole)],
-                out_specs=[block, gram_spec] if final else block,
+                out_specs=block,
             ),
-            out_shape=[shape, gram_shape] if final else shape,
+            out_shape=shape,
             compiler_params=pltpu.CompilerParams(vmem_limit_bytes=VMEM_BYTES),
             cost_estimate=pl.CostEstimate(
                 flops=2 * len(terms) * tokens * row_count * col_count,
@@ -196,12 +214,38 @@
     own = ([query_grads], [None], inputs)
     one = ([near[0], near_got[0]], whole_pair[0], moved_1)
     two = ([far[0], far_got[0], far[1], far_got[1]], halves, moved_2)
-    three = ([near[1], near_got[1]], whole_pair[1], moved_3)
-    total = accumulate(momentum, [own, one], MOMENTUM_DECAY, False)
-    total = accumulate(total, [two], None, False)
-    new_momentum, gram = accumulate(total, [three], None, True)
-
-    four = gram[:4] + over(1, gram[4:])
+    total = accumulate(momentum, [own, one], MOMENTUM_DECAY)
+    total = accumulate(total, [two], None)
+
+    whole_vmem = pl.BlockSpec(memory_space=pltpu.VMEM)
+    anywhere = pl.BlockSpec(memory_space=pl.ANY)
+    in_smem = pl.BlockSpec(memory_space=pltpu.SMEM)
+    count = owners // 2
+    whole_shape = jax.ShapeDtypeStruct((row_count, col_count), jnp.float32)
+    block_shape = jax.ShapeDtypeStruct((count, pair_rows, col_count), jnp.float32)
+
+    def last(core, rows, *before):
+        return pl.pallas_call(
+            functools.partial(last_kernel, core),
+            in_specs=[in_smem] + [whole_vmem] * 3 + [anywhere] * len(before),
+            out_specs=[anywhere, whole_vmem, whole_vmem],
+            out_shape=[
+                whole_shape,
+                block_shape,
+                jax.ShapeDtypeStruct((count, pair_heads, HEAD_DIM, HEAD_DIM), jnp.float32),
+            ],
+            scratch_shapes=[pltpu.SemaphoreType.DMA((count,))],
+            input_output_aliases={4: 0} if before else {},
+            compiler_params=pltpu.CompilerParams(vmem_limit_bytes=VMEM_BYTES),
+            cost_estimate=pl.CostEstimate(
+                flops=tokens * row_count * col_count, bytes_accessed=2 * row_count * col_count, transcendentals=0
+            ),
+        )(place, total, rows, moved_3, *before)
+
+    new_momentum, other_blocks, gram = last(1, near_got[1])
+    arrived = over(1, gram)
+    new_momentum, own_blocks, gram = last(0, near[1], new_momentum)
+    four = gram + arrived
     pieces = [four[0]] + [over(2 * i, four[i]) for i in range(1, 4)]
     factor = pl.pallas_call(
         polynomial_kernel,
@@ -211,31 +255,21 @@
     factors = jnp.stack([factor] + [over(2 * i, factor) for i in range(1, 4)])
     others = over(1, factors)
 
-    def update_half(core, values, *before):
-        def spec():
-            return pl.BlockSpec((pair_rows, col_count), lambda i, place: (pair_of(i + core * (owners // 2), place), 0))
-
+    def update_half(core, values, blocks, *before):
         return pl.pallas_call(
-            functools.partial(update_kernel, math.sqrt(model_width)),
-            grid_spec=pltpu.PrefetchScalarGridSpec(
-                num_scalar_prefetch=1,
-                grid=(owners // 2,),
-                in_specs=[
-                    pl.BlockSpec((1, pair_heads, HEAD_DIM, HEAD_DIM), lambda i, place: (i, 0, 0, 0)),
-                    spec(),
-                ]
-                + [pl.BlockSpec(memory_space=pl.ANY)] * len(before),
-                out_specs=spec(),
-            ),
-            out_shape=jax.ShapeDtypeStruct((row_count, col_count), jnp.float32),
+            functools.partial(update_kernel, math.sqrt(model_width), core),
+            in_specs=[in_smem] + [whole_vmem] * 2 + [anywhere] * len(before),
+            out_specs=anywhere,
+            out_shape=whole_shape,
+            scratch_shapes=[pltpu.VMEM(blocks.shape, jnp.float32), pltpu.SemaphoreType.DMA((count,))],
             input_output_aliases={3: 0} if before else {},
             compiler_params=pltpu.CompilerParams(vmem_limit_bytes=SMALL_BYTES),
             cost_estimate=pl.CostEstimate(
                 flops=3 * row_count * col_count * HEAD_DIM, bytes_accessed=4 * row_count * col_count, transcendentals=0
             ),
-        )(place, values, new_momentum, *before)
-
-    return new_momentum, update_half(1, others, update_half(0, factors))
+        )(place, values, blocks, *before)
+
+    return new_momentum, update_half(1, others, other_blocks, update_half(0, factors, own_blocks))
 
 
 def polynomial(gram_matrix):

time: 178 us -> 174 us (0.978)
  Pallas kernels: 27.1 us -> 23.8 us
  waiting for transfers between devices: 124 us -> 122 us
    pallas_call x5 -> x6, Pallas kernels: 23.5 us -> 21.1 us  [the longest x2 10.5 us: accumulate(): pl.pallas_call(functools.partial(accumulate_kernel, layouts, decay), grid...]
  transfers between devices with their start and end apart: 26 -> 26, of which waited for: 18 -> 17; matrix products, arithmetic and copies ran while one was open for 0% -> 0% of each run, Pallas kernels for 8% -> 9%
where the time goes in v2:
time: 174 us; the launch traced here: 173 us
  waiting for transfers between devices  122 us (70%)
  Pallas kernels  23.8 us (14%)
  starting transfers between devices  23.5 us (14%)
  local copies, waits for them, and re-layouts  2.75 us (2%)
    ppermute x20, waiting for transfers between devices, over(): return lax.ppermute(value, 'cols', [(i, i ^ bits) for i in range(owners)])  62.5 us
    ppermute x6, waiting for transfers between devices, onward(): lax.ppermute(value, 'dp', [(i, (i + k) % depth) for i in range(depth)])  59.7 us
    ppermute x20, starting transfers between devices, over(): return lax.ppermute(value, 'cols', [(i, i ^ bits) for i in range(owners)])  17.2 us
    pallas_call x2, Pallas kernels, accumulate(): pl.pallas_call(functools.partial(accumulate_kernel, layouts, decay), grid...  10.5 us
    ppermute x6, starting transfers between devices, onward(): lax.ppermute(value, 'dp', [(i, (i + k) % depth) for i in range(depth)])  6.21 us
    pallas_call x2, Pallas kernels, last(): pl.pallas_call(functools.partial(last_kernel, core), in_specs=[in_smem] +...  5.87 us
    pallas_call x2, Pallas kernels, update_half(): pl.pallas_call(functools.partial(update_kernel, math.sqrt(model_width), c...  4.7 us
  transfers between devices with their start and end apart: 26, of which 17 were waited for; matrix products, arithmetic and copies ran while one was open for 0% of the time, Pallas kernels for 9%

profile of v2, /device:TPU:0, one launch (start us, length us, event | category | flops | bytes accessed | tf_op | source)
XLA Modules:
  0.0 173.4 jit_solution(16465892659834788925)
XLA Ops:
  0.7 1.5 constant_dynamic-slice_fusion
  2.1 0.2 copy.10
  2.4 3.1 %collective-permute-start = (bf16[256,1024]{1,0:T(8,128)(2,1)S(1)}, bf16[256,1024]{1,0:T(8,128)(2,1)S(1)}, u32[]{:S(2)}, u32[]{:S(2)}) collective-permute-start(bf16[256,1024]{1,0:T(8,128)(2,1)S(1)} %bitcast.29), channel_id=1, source_target_pairs={{0,8},{8,16},{16,24},{24,0},{1,9},{9,17},{17,25},{25,1},{2,10},{10... | collective-permute-start | bytes 1572872 | tf_op jit(solution)/shard_map/ppermute | solution.py:131
  5.4 0.2 copy.11
  5.6 2.1 %collective-permute-start.1 = (bf16[256,1024]{1,0:T(8,128)(2,1)S(1)}, bf16[256,1024]{1,0:T(8,128)(2,1)S(1)}, u32[]{:S(2)}, u32[]{:S(2)}) collective-permute-start(bf16[256,1024]{1,0:T(8,128)(2,1)S(1)} %bitcast.30), channel_id=1, source_target_pairs={{0,24},{8,0},{16,8},{24,16},{1,25},{9,1},{17,9},{25,17},{2,26},{10... | collective-permute-start | bytes 1572872 | tf_op jit(solution)/shard_map/ppermute | solution.py:131
  7.7 0.2 copy.12
  7.9 12.3 %collective-permute-done = bf16[256,1024]{1,0:T(8,128)(2,1)S(1)} collective-permute-done((bf16[256,1024]{1,0:T(8,128)(2,1)S(1)}, bf16[256,1024]{1,0:T(8,128)(2,1)S(1)}, u32[]{:S(2)}, u32[]{:S(2)}) %collective-permute-start) | collective-permute-done | bytes 524320 | tf_op jit(solution)/shard_map/ppermute | solution.py:131
  20.3 10.1 %collective-permute-done.1 = bf16[256,1024]{1,0:T(8,128)(2,1)S(1)} collective-permute-done((bf16[256,1024]{1,0:T(8,128)(2,1)S(1)}, bf16[256,1024]{1,0:T(8,128)(2,1)S(1)}, u32[]{:S(2)}, u32[]{:S(2)}) %collective-permute-start.1) | collective-permute-done | bytes 524320 | tf_op jit(solution)/shard_map/ppermute | solution.py:131
  30.3 1.5 collective-permute-start.3
  31.8 1.0 collective-permute-start.2
  32.9 1.5 collective-permute-start.4
  34.4 9.4 %collective-permute-done.3 = bf16[1,256,1024]{2,1,0:T(8,128)(2,1)S(1)} collective-permute-done((bf16[1,256,1024]{2,1,0:T(8,128)(2,1)S(1)}, bf16[1,256,1024]{2,1,0:T(8,128)(2,1)S(1)}, u32[]{:S(2)}, u32[]{:S(2)}) %collective-permute-start.3) | collective-permute-done | bytes 524320 | tf_op jit(solution)/shard_map/ppermute | solution.py:128
  43.8 13.4 %collective-permute-done.2 = bf16[256,1024]{1,0:T(8,128)(2,1)S(1)} collective-permute-done((bf16[256,1024]{1,0:T(8,128)(2,1)S(1)}, bf16[256,1024]{1,0:T(8,128)(2,1)S(1)}, u32[]{:S(2)}, u32[]{:S(2)}) %collective-permute-start.2) | collective-permute-done | bytes 524320 | tf_op jit(solution)/shard_map/ppermute | solution.py:131
  57.3 0.6 collective-permute-start.6
  57.9 1.6 collective-permute-start.5
  59.5 22.2 %collective-permute-done.6 = bf16[2,256,1024]{2,1,0:T(8,128)(2,1)S(1)} collective-permute-done((bf16[2,256,1024]{2,1,0:T(8,128)(2,1)S(1)}, bf16[2,256,1024]{2,1,0:T(8,128)(2,1)S(1)}, u32[]{:S(2)}, u32[]{:S(2)}) %collective-permute-start.6) | collective-permute-done | bytes 1048608 | tf_op jit(solution)/shard_map/ppermute | solution.py:128
  81.7 0.3 collective-permute-done.5
  82.0 3.1 %collective-permute-done.7.refs_4_ = bf16[1024,512]{1,0:T(8,128)(2,1)S(1)} collective-permute-done((bf16[1024,512]{1,0:T(8,128)(2,1)S(1)}, bf16[1024,512]{1,0:T(8,128)(2,1)S(1)}, u32[]{:S(2)}, u32[]{:S(2)}) %collective-permute-start.7) | collective-permute-done | bytes 1048608 | tf_op jit(solution)/shard_map/ppermute | solution.py:131
  85.5 0.6 collective-permute-start.10
  86.1 1.5 collective-permute-start.8
  87.6 0.5 collective-permute-start.9
  88.2 6.3 %collective-permute-done.8 = bf16[1,128,1024]{2,1,0:T(8,128)(2,1)S(1)} collective-permute-done((bf16[1,128,1024]{2,1,0:T(8,128)(2,1)S(1)}, bf16[1,128,1024]{2,1,0:T(8,128)(2,1)S(1)}, u32[]{:S(2)}, u32[]{:S(2)}) %collective-permute-start.8) | collective-permute-done | bytes 262176 | tf_op jit(solution)/shard_map/ppermute | solution.py:128
  94.5 0.5 collective-permute-start.12
  95.1 0.6 collective-permute-done.9
  95.7 1.0 collective-permute-start.13
  96.7 11.0 %collective-permute-done.12 = bf16[2,128,1024]{2,1,0:T(8,128)(2,1)S(1)} collective-permute-done((bf16[2,128,1024]{2,1,0:T(8,128)(2,1)S(1)}, bf16[2,128,1024]{2,1,0:T(8,128)(2,1)S(1)}, u32[]{:S(2)}, u32[]{:S(2)}) %collective-permute-start.12) | collective-permute-done | bytes 524320 | tf_op jit(solution)/shard_map/ppermute | solution.py:128
  107.7 0.8 collective-permute-done.13
  108.5 4.5 %collective-permute-done.14.refs_4_ = bf16[1024,512]{1,0:T(8,128)(2,1)S(1)} collective-permute-done((bf16[1024,512]{1,0:T(8,128)(2,1)S(1)}, bf16[1024,512]{1,0:T(8,128)(2,1)S(1)}, u32[]{:S(2)}, u32[]{:S(2)}) %collective-permute-start.14) | collective-permute-done | bytes 1048608 | tf_op jit(solution)/shard_map/ppermute | solution.py:131
  113.3 0.6 collective-permute-start.15
  113.9 6.9 %shard_map.50.total = f32[2048,512]{1,0:T(8,128)S(1)} custom-call(s32[2]{0:T(128)S(1)} %pad_add_fusion.place, f32[2048,512]{1,0:T(8,128)S(1)} %copy-done, bf16[1024,8192]{1,0:T(8,128)(2,1)} %refs_0_.1, bf16[1024,512]{1,0:T(8,128)(2,1)S(1)} %copy-done.1, bf16[4,256,1024]{2,1,0:T(8,128)(2,1)S(1)} %constant_dynamic-update-slice_fusion.4.refs_2_, ...), custom_call_target="tpu_custom_call" | custom-call | flops 4294967296 | bytes 16777216 | tf_op jit(solution)/shard_map/pallas_call | solution.py:195
  120.9 3.5 %shard_map.51.total = f32[2048,512]{1,0:T(8,128)S(1)} custom-call(s32[2]{0:T(128)S(1)} %pad_add_fusion.place, f32[2048,512]{1,0:T(8,128)S(1)} %shard_map.50.total, bf16[4,128,1024]{2,1,0:T(8,128)(2,1)S(1)} %constant_dynamic-update-slice_fusion.8.refs_0_, bf16[4,128,1024]{2,1,0:T(8,128)(2,1)S(1)} %collective-permute-done.15.refs_1_, ...), custom_call_target="tpu_custom_call" | custom-call | flops 2147483648 | bytes 12582912 | tf_op jit(solution)/shard_map/pallas_call | solution.py:195
  124.4 16.3 %collective-permute-done.17.x_ref = bf16[1024,512]{1,0:T(8,128)(2,1)S(1)} collective-permute-done((bf16[1024,512]{1,0:T(8,128)(2,1)S(1)}, bf16[1024,512]{1,0:T(8,128)(2,1)S(1)}, u32[]{:S(2)}, u32[]{:S(2)}) %collective-permute-start.17) | collective-permute-done | bytes 1048608 | tf_op jit(solution)/shard_map/ppermute | solution.py:131
  140.8 2.9 %shard_map.52 = (f32[2048,512]{1,0:T(8,128)}, f32[4,256,512]{2,1,0:T(8,128)S(1)}, f32[4,2,128,128]{3,2,1,0:T(8,128)S(1)}) custom-call(s32[2]{0:T(128)S(1)} %pad_add_fusion.place, f32[2048,512]{1,0:T(8,128)S(1)} %shard_map.51.total, bf16[4,256,1024]{2,1,0:T(8,128)(2,1)S(1)} %collective-permute-done.11.queries, bf16[1024,512]{1,0:T(8,128)(2,1)S(1)} %collective-permute-done.17.x_ref), custom_call_target="tpu_custom_call" | custom-call | flops 1073741824 | bytes 2097152 | tf_op jit(solution)/shard_map/pallas_call | solution.py:228
  143.8 2.9 %shard_map.53 = (f32[2048,512]{1,0:T(8,128)}, f32[4,256,512]{2,1,0:T(8,128)S(1)}, f32[4,2,128,128]{3,2,1,0:T(8,128)S(1)}) custom-call(s32[2]{0:T(128)S(1)} %pad_add_fusion.place, f32[2048,512]{1,0:T(8,128)S(1)} %shard_map.51.total, bf16[4,256,1024]{2,1,0:T(8,128)(2,1)S(1)} %constant_dynamic-update-slice_fusion.6.queries, ...), custom_call_target="tpu_custom_call", output_to_operand_aliasing={{0}: (4, {})} | custom-call | flops 1073741824 | bytes 2097152 | tf_op jit(solution)/shard_map/pallas_call | solution.py:228
  146.7 0.1 add.39
  146.9 1.5 collective-permute-start.21
  148.3 0.5 collective-permute-start.20
  148.8 1.6 collective-permute-start.19
  150.4 3.7 %collective-permute-done.21.refs_3_ = f32[2,128,128]{2,1,0:T(8,128)S(1)} collective-permute-done((f32[2,128,128]{2,1,0:T(8,128)S(1)}, f32[2,128,128]{2,1,0:T(8,128)S(1)}, u32[]{:S(2)}, u32[]{:S(2)}) %collective-permute-start.21) | collective-permute-done | bytes 131104 | tf_op jit(solution)/shard_map/ppermute | solution.py:128
  154.2 2.4 %collective-permute-done.20.refs_2_ = f32[2,128,128]{2,1,0:T(8,128)S(1)} collective-permute-done((f32[2,128,128]{2,1,0:T(8,128)S(1)}, f32[2,128,128]{2,1,0:T(8,128)S(1)}, u32[]{:S(2)}, u32[]{:S(2)}) %collective-permute-start.20) | collective-permute-done | bytes 131104 | tf_op jit(solution)/shard_map/ppermute | solution.py:128
  156.5 2.8 %shard_map.54 = f32[2,128,128]{2,1,0:T(8,128)S(1)} custom-call(f32[2,128,128]{2,1,0:T(8,128)S(1)} %get-tuple-element.70.refs_0_, f32[2,128,128]{2,1,0:T(8,128)S(1)} %collective-permute-done.19.refs_1_, f32[2,128,128]{2,1,0:T(8,128)S(1)} %collective-permute-done.20.refs_2_, f32[2,128,128]{2,1,0:T(8,128)S(1)} %collective-permute-done.21.refs_3_), custom_call_target="tpu_custom_call" | custom-call | tf_op jit(solution)/shard_map/pallas_call | solution.py:250
  159.3 1.4 collective-permute-start.24
  160.8 0.6 collective-permute-start.23
  161.4 1.5 collective-permute-start.22
  162.9 3.8 %collective-permute-done.24 = f32[2,128,128]{2,1,0:T(8,128)S(1)} collective-permute-done((f32[2,128,128]{2,1,0:T(8,128)S(1)}, f32[2,128,128]{2,1,0:T(8,128)S(1)}, u32[]{:S(2)}, u32[]{:S(2)}) %collective-permute-start.24) | collective-permute-done | bytes 131104 | tf_op jit(solution)/shard_map/ppermute | solution.py:128
  166.7 1.9 %collective-permute-done.23 = f32[2,128,128]{2,1,0:T(8,128)S(1)} collective-permute-done((f32[2,128,128]{2,1,0:T(8,128)S(1)}, f32[2,128,128]{2,1,0:T(8,128)S(1)}, u32[]{:S(2)}, u32[]{:S(2)}) %collective-permute-start.23) | collective-permute-done | bytes 131104 | tf_op jit(solution)/shard_map/ppermute | solution.py:128
  168.7 2.3 %shard_map.55.refs_0_ = f32[2048,512]{1,0:T(8,128)} custom-call(s32[2]{0:T(128)S(1)} %pad_add_fusion.place, f32[4,2,128,128]{3,2,1,0:T(8,128)S(1)} %pad_maximum_fusion.2.factor, f32[4,256,512]{2,1,0:T(8,128)S(1)} %get-tuple-element.63.blocks), custom_call_target="tpu_custom_call" | custom-call | flops 402653184 | bytes 4194304 | tf_op jit(solution)/shard_map/pallas_call | solution.py:259
  171.0 2.4 %shard_map.56 = f32[2048,512]{1,0:T(8,128)} custom-call(s32[2]{0:T(128)S(1)} %pad_add_fusion.place, f32[4,2,128,128]{3,2,1,0:T(8,128)S(1)} %collective-permute-done.25.factor, f32[4,256,512]{2,1,0:T(8,128)S(1)} %get-tuple-element.62.blocks, f32[2048,512]{1,0:T(8,128)} %shard_map.55.refs_0_), custom_call_target="tpu_custom_call", output_to_operand_aliasing={{}: (3, {})} | custom-call | flops 402653184 | bytes 4194304 | tf_op jit(solution)/shard_map/pallas_call | solution.py:259
  (38 shorter events, 1.2 us)
Async XLA Ops:
  2.4 17.9 %collective-permute-start = (bf16[256,1024]{1,0:T(8,128)(2,1)S(1)}, bf16[256,1024]{1,0:T(8,128)(2,1)S(1)}, u32[]{:S(2)}, u32[]{:S(2)}) collective-permute-start(bf16[256,1024]{1,0:T(8,128)(2,1)S(1)} %bitcast.29), channel_id=1, source_target_pairs={{0,8},{8,16},{16,24},{24,0},{1,9},{9,17},{17,25},{25,1},{2,10},{10... | collective-permute-start | bytes 1572872 | tf_op jit(solution)/shard_map/ppermute | solution.py:131
  5.6 24.7 %collective-permute-start.1 = (bf16[256,1024]{1,0:T(8,128)(2,1)S(1)}, bf16[256,1024]{1,0:T(8,128)(2,1)S(1)}, u32[]{:S(2)}, u32[]{:S(2)}) collective-permute-start(bf16[256,1024]{1,0:T(8,128)(2,1)S(1)} %bitcast.30), channel_id=1, source_target_pairs={{0,24},{8,0},{16,8},{24,16},{1,25},{9,1},{17,9},{25,17},{2,26},{10... | collective-permute-start | bytes 1572872 | tf_op jit(solution)/shard_map/ppermute | solution.py:131
  30.3 13.5 %collective-permute-start.3 = (bf16[1,256,1024]{2,1,0:T(8,128)(2,1)S(1)}, bf16[1,256,1024]{2,1,0:T(8,128)(2,1)S(1)}, u32[]{:S(2)}, u32[]{:S(2)}) collective-permute-start(bf16[1,256,1024]{2,1,0:T(8,128)(2,1)S(1)} %bitcast.24), channel_id=1, source_target_pairs={{0,4},{1,5},{2,6},{3,7},{4,0},{5,1},{6,2},{7,3},{8,12},{9,13},{10,... | collective-permute-start | bytes 1572872 | tf_op jit(solution)/shard_map/ppermute | solution.py:128
  31.8 25.3 %collective-permute-start.2 = (bf16[256,1024]{1,0:T(8,128)(2,1)S(1)}, bf16[256,1024]{1,0:T(8,128)(2,1)S(1)}, u32[]{:S(2)}, u32[]{:S(2)}) collective-permute-start(bf16[256,1024]{1,0:T(8,128)(2,1)S(1)} %bitcast.28), channel_id=1, source_target_pairs={{0,16},{8,24},{16,0},{24,8},{1,17},{9,25},{17,1},{25,9},{2,18},{10... | collective-permute-start | bytes 1572872 | tf_op jit(solution)/shard_map/ppermute | solution.py:131
  32.9 26.6 %copy-start.1 = (bf16[1024,512]{1,0:T(8,128)(2,1)S(1)}, bf16[1024,512]{1,0:T(8,128)(2,1)}, u32[]{:S(2)}) copy-start(bf16[1024,512]{1,0:T(8,128)(2,1)} %refs_1_.1) | copy-start | bytes 3145732
  32.9 24.3 %collective-permute-start.4 = (bf16[1,256,1024]{2,1,0:T(8,128)(2,1)S(1)}, bf16[1,256,1024]{2,1,0:T(8,128)(2,1)S(1)}, u32[]{:S(2)}, u32[]{:S(2)}) collective-permute-start(bf16[1,256,1024]{2,1,0:T(8,128)(2,1)S(1)} %bitcast.26), channel_id=1, source_target_pairs={{0,2},{1,3},{2,0},{3,1},{4,6},{5,7},{6,4},{7,5},{8,10},{9,11},{10,... | collective-permute-start | bytes 1572872 | tf_op jit(solution)/shard_map/ppermute | solution.py:128
  57.3 24.4 %collective-permute-start.6 = (bf16[2,256,1024]{2,1,0:T(8,128)(2,1)S(1)}, bf16[2,256,1024]{2,1,0:T(8,128)(2,1)S(1)}, u32[]{:S(2)}, u32[]{:S(2)}) collective-permute-start(bf16[2,256,1024]{2,1,0:T(8,128)(2,1)S(1)} %constant_dynamic-update-slice_fusion.2), channel_id=1, source_target_pairs={{0,4},{1,5},{2,6},{3,7},{4,0},{5,1},{6,2},{7,3},{8,12},{9,13},{10,... | collective-permute-start | bytes 3145736 | tf_op jit(solution)/shard_map/ppermute | solution.py:128
  57.9 24.1 %collective-permute-start.5 = (bf16[2,256,1024]{2,1,0:T(8,128)(2,1)S(1)}, bf16[2,256,1024]{2,1,0:T(8,128)(2,1)S(1)}, u32[]{:S(2)}, u32[]{:S(2)}) collective-permute-start(bf16[2,256,1024]{2,1,0:T(8,128)(2,1)S(1)} %constant_dynamic-update-slice_fusion), channel_id=1, source_target_pairs={{0,2},{1,3},{2,0},{3,1},{4,6},{5,7},{6,4},{7,5},{8,10},{9,11},{10,... | collective-permute-start | bytes 3145736 | tf_op jit(solution)/shard_map/ppermute | solution.py:128
  59.5 25.6 %collective-permute-start.7 = (bf16[1024,512]{1,0:T(8,128)(2,1)S(1)}, bf16[1024,512]{1,0:T(8,128)(2,1)S(1)}, u32[]{:S(2)}, u32[]{:S(2)}) collective-permute-start(bf16[1024,512]{1,0:T(8,128)(2,1)S(1)} %copy-done.1), channel_id=1, source_target_pairs={{0,8},{8,16},{16,24},{24,0},{1,9},{9,17},{17,25},{25,1},{2,10},{10... | collective-permute-start | bytes 3145736 | tf_op jit(solution)/shard_map/ppermute | solution.py:131
  85.4 27.6 %collective-permute-start.11 = (bf16[4,256,1024]{2,1,0:T(8,128)(2,1)S(1)}, bf16[4,256,1024]{2,1,0:T(8,128)(2,1)S(1)}, u32[]{:S(2)}, u32[]{:S(2)}) collective-permute-start(bf16[4,256,1024]{2,1,0:T(8,128)(2,1)S(1)} %constant_dynamic-update-slice_fusion.6.queries), channel_id=1, source_target_pairs={{0,1},{1,0},{2,3},{3,2},{4,5},{5,4},{6,7},{7,6},{8,9},{9,8},{10,11... | collective-permute-start | bytes 6291464 | tf_op jit(solution)/shard_map/ppermute | solution.py:128
  85.5 27.5 %collective-permute-start.10 = (bf16[4,256,1024]{2,1,0:T(8,128)(2,1)S(1)}, bf16[4,256,1024]{2,1,0:T(8,128)(2,1)S(1)}, u32[]{:S(2)}, u32[]{:S(2)}) collective-permute-start(bf16[4,256,1024]{2,1,0:T(8,128)(2,1)S(1)} %constant_dynamic-update-slice_fusion.4.refs_2_), channel_id=1, source_target_pairs={{0,1},{1,0},{2,3},{3,2},{4,5},{5,4},{6,7},{7,6},{8,9},{9,8},{10,11... | collective-permute-start | bytes 6291464 | tf_op jit(solution)/shard_map/ppermute | solution.py:128
  86.1 26.9 %collective-permute-start.14 = (bf16[1024,512]{1,0:T(8,128)(2,1)S(1)}, bf16[1024,512]{1,0:T(8,128)(2,1)S(1)}, u32[]{:S(2)}, u32[]{:S(2)}) collective-permute-start(bf16[1024,512]{1,0:T(8,128)(2,1)S(1)} %collective-permute-done.7.refs_4_), channel_id=1, source_target_pairs={{0,8},{8,16},{16,24},{24,0},{1,9},{9,17},{17,25},{25,1},{2,10},{10... | collective-permute-start | bytes 3145736 | tf_op jit(solution)/shard_map/ppermute | solution.py:131
  86.1 8.4 %collective-permute-start.8 = (bf16[1,128,1024]{2,1,0:T(8,128)(2,1)S(1)}, bf16[1,128,1024]{2,1,0:T(8,128)(2,1)S(1)}, u32[]{:S(2)}, u32[]{:S(2)}) collective-permute-start(bf16[1,128,1024]{2,1,0:T(8,128)(2,1)S(1)} %get-tuple-element.72), channel_id=1, source_target_pairs={{0,4},{1,5},{2,6},{3,7},{4,0},{5,1},{6,2},{7,3},{8,12},{9,13},{10,... | collective-permute-start | bytes 786440 | tf_op jit(solution)/shard_map/ppermute | solution.py:128
  87.6 8.0 %collective-permute-start.9 = (bf16[1,128,1024]{2,1,0:T(8,128)(2,1)S(1)}, bf16[1,128,1024]{2,1,0:T(8,128)(2,1)S(1)}, u32[]{:S(2)}, u32[]{:S(2)}) collective-permute-start(bf16[1,128,1024]{2,1,0:T(8,128)(2,1)S(1)} %get-tuple-element.71), channel_id=1, source_target_pairs={{0,2},{1,3},{2,0},{3,1},{4,6},{5,7},{6,4},{7,5},{8,10},{9,11},{10,... | collective-permute-start | bytes 786440 | tf_op jit(solution)/shard_map/ppermute | solution.py:128
  94.5 13.1 %collective-permute-start.12 = (bf16[2,128,1024]{2,1,0:T(8,128)(2,1)S(1)}, bf16[2,128,1024]{2,1,0:T(8,128)(2,1)S(1)}, u32[]{:S(2)}, u32[]{:S(2)}) collective-permute-start(bf16[2,128,1024]{2,1,0:T(8,128)(2,1)S(1)} %pad_maximum_fusion), channel_id=1, source_target_pairs={{0,2},{1,3},{2,0},{3,1},{4,6},{5,7},{6,4},{7,5},{8,10},{9,11},{10,... | collective-permute-start | bytes 1572872 | tf_op jit(solution)/shard_map/ppermute | solution.py:128
  95.7 18.2 %copy-start = (f32[2048,512]{1,0:T(8,128)S(1)}, f32[2048,512]{1,0:T(8,128)}, u32[]{:S(2)}) copy-start(f32[2048,512]{1,0:T(8,128)} %total.1) | copy-start | bytes 12582916
  95.7 12.8 %collective-permute-start.13 = (bf16[2,128,1024]{2,1,0:T(8,128)(2,1)S(1)}, bf16[2,128,1024]{2,1,0:T(8,128)(2,1)S(1)}, u32[]{:S(2)}, u32[]{:S(2)}) collective-permute-start(bf16[2,128,1024]{2,1,0:T(8,128)(2,1)S(1)} %pad_maximum_fusion.1), channel_id=1, source_target_pairs={{0,4},{1,5},{2,6},{3,7},{4,0},{5,1},{6,2},{7,3},{8,12},{9,13},{10,... | collective-permute-start | bytes 1572872 | tf_op jit(solution)/shard_map/ppermute | solution.py:128
  113.2 7.7 %collective-permute-start.16 = (bf16[4,128,1024]{2,1,0:T(8,128)(2,1)S(1)}, bf16[4,128,1024]{2,1,0:T(8,128)(2,1)S(1)}, u32[]{:S(2)}, u32[]{:S(2)}) collective-permute-start(bf16[4,128,1024]{2,1,0:T(8,128)(2,1)S(1)} %constant_dynamic-update-slice_fusion.10.refs_2_), channel_id=1, source_target_pairs={{0,1},{1,0},{2,3},{3,2},{4,5},{5,4},{6,7},{7,6},{8,9},{9,8},{10,11... | collective-permute-start | bytes 3145736 | tf_op jit(solution)/shard_map/ppermute | solution.py:128
  113.3 7.6 %collective-permute-start.15 = (bf16[4,128,1024]{2,1,0:T(8,128)(2,1)S(1)}, bf16[4,128,1024]{2,1,0:T(8,128)(2,1)S(1)}, u32[]{:S(2)}, u32[]{:S(2)}) collective-permute-start(bf16[4,128,1024]{2,1,0:T(8,128)(2,1)S(1)} %constant_dynamic-update-slice_fusion.8.refs_0_), channel_id=1, source_target_pairs={{0,1},{1,0},{2,3},{3,2},{4,5},{5,4},{6,7},{7,6},{8,9},{9,8},{10,11... | collective-permute-start | bytes 3145736 | tf_op jit(solution)/shard_map/ppermute | solution.py:128
  113.8 26.9 %collective-permute-start.17 = (bf16[1024,512]{1,0:T(8,128)(2,1)S(1)}, bf16[1024,512]{1,0:T(8,128)(2,1)S(1)}, u32[]{:S(2)}, u32[]{:S(2)}) collective-permute-start(bf16[1024,512]{1,0:T(8,128)(2,1)S(1)} %collective-permute-done.14.refs_4_), channel_id=1, source_target_pairs={{0,8},{8,16},{16,24},{24,0},{1,9},{9,17},{17,25},{25,1},{2,10},{10... | collective-permute-start | bytes 3145736 | tf_op jit(solution)/shard_map/ppermute | solution.py:131
  143.7 3.0 %collective-permute-start.18 = (f32[4,2,128,128]{3,2,1,0:T(8,128)S(1)}, f32[4,2,128,128]{3,2,1,0:T(8,128)S(1)}, u32[]{:S(2)}, u32[]{:S(2)}) collective-permute-start(f32[4,2,128,128]{3,2,1,0:T(8,128)S(1)} %get-tuple-element.61), channel_id=1, source_target_pairs={{0,1},{1,0},{2,3},{3,2},{4,5},{5,4},{6,7},{7,6},{8,9},{9,8},{10,11... | collective-permute-start | bytes 1572872 | tf_op jit(solution)/shard_map/ppermute | solution.py:128
  146.9 7.3 %collective-permute-start.21 = (f32[2,128,128]{2,1,0:T(8,128)S(1)}, f32[2,128,128]{2,1,0:T(8,128)S(1)}, u32[]{:S(2)}, u32[]{:S(2)}) collective-permute-start(f32[2,128,128]{2,1,0:T(8,128)S(1)} %get-tuple-element.67), channel_id=1, source_target_pairs={{0,6},{1,7},{2,4},{3,5},{4,2},{5,3},{6,0},{7,1},{8,14},{9,15},{10,... | collective-permute-start | bytes 393224 | tf_op jit(solution)/shard_map/ppermute | solution.py:128
  148.3 8.2 %collective-permute-start.20 = (f32[2,128,128]{2,1,0:T(8,128)S(1)}, f32[2,128,128]{2,1,0:T(8,128)S(1)}, u32[]{:S(2)}, u32[]{:S(2)}) collective-permute-start(f32[2,128,128]{2,1,0:T(8,128)S(1)} %get-tuple-element.68), channel_id=1, source_target_pairs={{0,4},{1,5},{2,6},{3,7},{4,0},{5,1},{6,2},{7,3},{8,12},{9,13},{10,... | collective-permute-start | bytes 393224 | tf_op jit(solution)/shard_map/ppermute | solution.py:128
  148.8 7.7 %collective-permute-start.19 = (f32[2,128,128]{2,1,0:T(8,128)S(1)}, f32[2,128,128]{2,1,0:T(8,128)S(1)}, u32[]{:S(2)}, u32[]{:S(2)}) collective-permute-start(f32[2,128,128]{2,1,0:T(8,128)S(1)} %get-tuple-element.69), channel_id=1, source_target_pairs={{0,2},{1,3},{2,0},{3,1},{4,6},{5,7},{6,4},{7,5},{8,10},{9,11},{10,... | collective-permute-start | bytes 393224 | tf_op jit(solution)/shard_map/ppermute | solution.py:128
  159.3 7.3 %collective-permute-start.24 = (f32[2,128,128]{2,1,0:T(8,128)S(1)}, f32[2,128,128]{2,1,0:T(8,128)S(1)}, u32[]{:S(2)}, u32[]{:S(2)}) collective-permute-start(f32[2,128,128]{2,1,0:T(8,128)S(1)} %shard_map.54), channel_id=1, source_target_pairs={{0,6},{1,7},{2,4},{3,5},{4,2},{5,3},{6,0},{7,1},{8,14},{9,15},{10,... | collective-permute-start | bytes 393224 | tf_op jit(solution)/shard_map/ppermute | solution.py:128
  160.8 7.7 %collective-permute-start.23 = (f32[2,128,128]{2,1,0:T(8,128)S(1)}, f32[2,128,128]{2,1,0:T(8,128)S(1)}, u32[]{:S(2)}, u32[]{:S(2)}) collective-permute-start(f32[2,128,128]{2,1,0:T(8,128)S(1)} %shard_map.54), channel_id=1, source_target_pairs={{0,4},{1,5},{2,6},{3,7},{4,0},{5,1},{6,2},{7,3},{8,12},{9,13},{10,... | collective-permute-start | bytes 393224 | tf_op jit(solution)/shard_map/ppermute | solution.py:128
  161.4 7.2 %collective-permute-start.22 = (f32[2,128,128]{2,1,0:T(8,128)S(1)}, f32[2,128,128]{2,1,0:T(8,128)S(1)}, u32[]{:S(2)}, u32[]{:S(2)}) collective-permute-start(f32[2,128,128]{2,1,0:T(8,128)S(1)} %shard_map.54), channel_id=1, source_target_pairs={{0,2},{1,3},{2,0},{3,1},{4,6},{5,7},{6,4},{7,5},{8,10},{9,11},{10,... | collective-permute-start | bytes 393224 | tf_op jit(solution)/shard_map/ppermute | solution.py:128
  168.6 2.4 %collective-permute-start.25 = (f32[4,2,128,128]{3,2,1,0:T(8,128)S(1)}, f32[4,2,128,128]{3,2,1,0:T(8,128)S(1)}, u32[]{:S(2)}, u32[]{:S(2)}) collective-permute-start(f32[4,2,128,128]{3,2,1,0:T(8,128)S(1)} %pad_maximum_fusion.2.factor), channel_id=1, source_target_pairs={{0,1},{1,0},{2,3},{3,2},{4,5},{5,4},{6,7},{7,6},{8,9},{9,8},{10,11... | collective-permute-start | bytes 1572872 | tf_op jit(solution)/shard_map/ppermute | solution.py:128

commit v3 on v2

--- a/solution.py
+++ b/solution.py
@@ -26,11 +26,21 @@
     return high, (value - high.astype(jnp.float32)).astype(jnp.bfloat16)
 
 
-def dot3(left, right, dims):
-    lh, ll = left
-    rh, rl = right
-    dot = functools.partial(lax.dot_general, dimension_numbers=dims, preferred_element_type=jnp.float32)
-    return dot(lh, rh) + (dot(lh, rl) + dot(ll, rh))
+def dot3(left, right):
+    dot = functools.partial(jnp.dot, preferred_element_type=jnp.float32)
+    both = dot(jnp.concatenate(left), right[0])
+    rows = left[0].shape[0]
+    return both[:rows] + (both[rows:] + dot(left[0], right[1]))
+
+
+def gram_of(block):
+    high, low = split(block)
+    both = lax.dot_general(
+        jnp.concatenate([high, low]), high, (((1,), (1,)), ((), ())), preferred_element_type=jnp.float32
+    )
+    rows = high.shape[0]
+    cross = both[rows:]
+    return both[:rows] + (cross + cross.T)
 
 
 def accumulate_kernel(layouts, decay, place, total, *refs):
@@ -55,21 +65,24 @@
     return pl.ds(pl.multiple_of((place[1] ^ (2 * index + core)) * count, count), count)
 
 
-def last_kernel(core, place, total, queries, x_ref, *refs):
-    new_momentum, blocks, gram, sems = refs[-4:]
-    copies = []
+def last_kernel(core, place, total, queries, x_ref, blocks, gram):
     count = queries.shape[1]
     depth = queries.shape[2]
     product = jnp.dot(queries[...].reshape(-1, depth), x_ref[...], preferred_element_type=jnp.float32)
     for index in range(queries.shape[0]):
-        rows = rows_at(place, core, index, count)
-        value = total[rows, :] + product[index * count : (index + 1) * count, :]
+        value = total[rows_at(place, core, index, count), :] + product[index * count : (index + 1) * count, :]
         blocks[index] = value
-        copies.append(pltpu.make_async_copy(blocks.at[index], new_momentum.at[rows, :], sems.at[index]))
-        copies[-1].start()
         for head in range(gram.shape[1]):
-            parts = split(value[head * HEAD_DIM : (head + 1) * HEAD_DIM, :])
-            gram[index, head] = dot3(parts, parts, (((1,), (1,)), ((), ())))
+            gram[index, head] = gram_of(value[head * HEAD_DIM : (head + 1) * HEAD_DIM, :])
+
+
+def store_kernel(place, own, other, out, sems):
+    copies = []
+    for core, blocks in enumerate((own, other)):
+        for index in range(blocks.shape[0]):
+            rows = rows_at(place, core, index, blocks.shape[1])
+            copies.append(pltpu.make_async_copy(blocks.at[index], out.at[rows, :], sems.at[core, index]))
+            copies[-1].start()
     for copy in copies:
         copy.wait()
 
@@ -83,9 +96,7 @@
     identity = (rows == cols).astype(jnp.float32)
     heads = range(gram.shape[0])
 
-    def dot(left, right):
-        return dot3(split(left), split(right), (((1,), (0,)), ((), ())))
-
+    dot = functools.partial(jnp.dot, precision=HIGHEST, preferred_element_type=jnp.float32)
     norms = [jnp.sqrt(jnp.sum(gram[h] * identity)) + NORM_EPS for h in heads]
     current = [gram[h] / (norms[h] * norms[h]) for h in heads]
     factors = [None for h in heads]
@@ -100,17 +111,30 @@
         factor[h] = factors[h] / norms[h]
 
 
-def update_kernel(scale, core, place, factor, blocks, *refs):
-    update, held, sems = refs[-3:]
-    copies = []
+def updated(scale, factor, block):
+    heads = []
+    for head in range(factor.shape[0]):
+        rows = slice(head * HEAD_DIM, (head + 1) * HEAD_DIM)
+        heads.append(scale * dot3(split(factor[head]), split(block[rows, :])))
+    return jnp.concatenate(heads)
+
+
+def own_update_kernel(scale, factor, blocks, held):
     for index in range(blocks.shape[0]):
-        for head in range(factor.shape[1]):
-            rows = slice(head * HEAD_DIM, (head + 1) * HEAD_DIM)
-            product = dot3(split(factor[index, head]), split(blocks[index, rows, :]), (((1,), (0,)), ((), ())))
-            held[index, rows, :] = scale * product
+        held[index] = updated(scale, factor[index], blocks[index])
+
+
+def other_update_kernel(scale, place, factor, blocks, own, update, held, sems):
+    def send(core, source, index):
         rows = rows_at(place, core, index, blocks.shape[1])
-        copies.append(pltpu.make_async_copy(held.at[index], update.at[rows, :], sems.at[index]))
-        copies[-1].start()
+        copy = pltpu.make_async_copy(source.at[index], update.at[rows, :], sems.at[core, index])
+        copy.start()
+        return copy
+
+    copies = [send(0, own, index) for index in range(own.shape[0])]
+    for index in range(blocks.shape[0]):
+        held[index] = updated(scale, factor[index], blocks[index])
+        copies.append(send(1, held, index))
     for copy in copies:
         copy.wait()
 
@@ -130,6 +154,10 @@
     def onward(k, value):
         return lax.ppermute(value, "dp", [(i, (i + k) % depth) for i in range(depth)])
 
+    def over_halves(bits, value):
+        axis = 0 if value.shape[0] > 1 else 1
+        return jnp.concatenate([over(bits, piece) for piece in jnp.split(value, 2, axis)], axis)
+
     def both(held, got):
         return [jnp.concatenate(pair) for pair in zip(held, got)]
 
@@ -145,12 +173,12 @@
 
     far = onward(2, pieces[1])
     near = [piece[None] for piece in near]
-    got = [over(turn[0], piece) for turn, piece in zip(turns, near)]
+    got = [over_halves(turn[0], piece) for turn, piece in zip(turns, near)]
     far, near, got, moved = lax.optimization_barrier((far, near, got, inputs))
 
     moved_1 = onward(1, moved)
     near = both(near, got)
-    got = [over(turn[1], piece) for turn, piece in zip(turns, near)]
+    got = [over_halves(turn[1], piece) for turn, piece in zip(turns, near)]
     far, near, got, moved_1 = lax.optimization_barrier((far, near, got, moved_1))
 
     moved_2 = onward(1, moved_1)
@@ -224,29 +252,39 @@
     whole_shape = jax.ShapeDtypeStruct((row_count, col_count), jnp.float32)
     block_shape = jax.ShapeDtypeStruct((count, pair_rows, col_count), jnp.float32)
 
-    def last(core, rows, *before):
+    sems = pltpu.SemaphoreType.DMA((2, count))
+    params = pltpu.CompilerParams(vmem_limit_bytes=VMEM_BYTES)
+
+    def last(core, rows):
         return pl.pallas_call(
             functools.partial(last_kernel, core),
-            in_specs=[in_smem] + [whole_vmem] * 3 + [anywhere] * len(before),
-            out_specs=[anywhere, whole_vmem, whole_vmem],
+            in_specs=[in_smem] + [whole_vmem] * 3,
+            out_specs=[whole_vmem, whole_vmem],
             out_shape=[
-                whole_shape,
                 block_shape,
                 jax.ShapeDtypeStruct((count, pair_heads, HEAD_DIM, HEAD_DIM), jnp.float32),
             ],
-            scratch_shapes=[pltpu.SemaphoreType.DMA((count,))],
-            input_output_aliases={4: 0} if before else {},
-            compiler_params=pltpu.CompilerParams(vmem_limit_bytes=VMEM_BYTES),
+            compiler_params=params,
             cost_estimate=pl.CostEstimate(
                 flops=tokens * row_count * col_count, bytes_accessed=2 * row_count * col_count, transcendentals=0
             ),
-        )(place, total, rows, moved_3, *before)
-
-    new_momentum, other_blocks, gram = last(1, near_got[1])
+        )(place, total, rows, moved_3)
+
+    other_blocks, gram = last(1, near_got[1])
     arrived = over(1, gram)
-    new_momentum, own_blocks, gram = last(0, near[1], new_momentum)
+    own_blocks, gram = last(0, near[1])
+    new_momentum = pl.pallas_call(
+        store_kernel,
+        in_specs=[in_smem] + [whole_vmem] * 2,
+        out_specs=anywhere,
+        out_shape=whole_shape,
+        scratch_shapes=[sems],
+        compiler_params=params,
+        cost_estimate=pl.CostEstimate(flops=0, bytes_accessed=8 * row_count * col_count, transcendentals=0),
+    )(place, own_blocks, other_blocks)
     four = gram + arrived
     pieces = [four[0]] + [over(2 * i, four[i]) for i in range(1, 4)]
+    pieces, new_momentum = lax.optimization_barrier((pieces, new_momentum))
     factor = pl.pallas_call(
         polynomial_kernel,
         out_shape=jax.ShapeDtypeStruct(pieces[0].shape, jnp.float32),
@@ -255,21 +293,28 @@
     factors = jnp.stack([factor] + [over(2 * i, factor) for i in range(1, 4)])
     others = over(1, factors)
 
-    def update_half(core, values, blocks, *before):
-        return pl.pallas_call(
-            functools.partial(update_kernel, math.sqrt(model_width), core),
-            in_specs=[in_smem] + [whole_vmem] * 2 + [anywhere] * len(before),
-            out_specs=anywhere,
-            out_shape=whole_shape,
-            scratch_shapes=[pltpu.VMEM(blocks.shape, jnp.float32), pltpu.SemaphoreType.DMA((count,))],
-            input_output_aliases={3: 0} if before else {},
-            compiler_params=pltpu.CompilerParams(vmem_limit_bytes=SMALL_BYTES),
-            cost_estimate=pl.CostEstimate(
-                flops=3 * row_count * col_count * HEAD_DIM, bytes_accessed=4 * row_count * col_count, transcendentals=0
-            ),
-        )(place, values, blocks, *before)
-
-    return new_momentum, update_half(1, others, other_blocks, update_half(0, factors, own_blocks))
+    scale = math.sqrt(model_width)
+    cost = pl.CostEstimate(
+        flops=3 * row_count * col_count * HEAD_DIM, bytes_accessed=2 * row_count * col_count, transcendentals=0
+    )
+    held = pl.pallas_call(
+        functools.partial(own_update_kernel, scale),
+        in_specs=[whole_vmem] * 2,
+        out_specs=whole_vmem,
+        out_shape=block_shape,
+        compiler_params=params,
+        cost_estimate=cost,
+    )(factors, own_blocks)
+    update = pl.pallas_call(
+        functools.partial(other_update_kernel, scale),
+        in_specs=[in_smem] + [whole_vmem] * 3,
+        out_specs=anywhere,
+        out_shape=whole_shape,
+        scratch_shapes=[pltpu.VMEM(block_shape.shape, jnp.float32), sems],
+        compiler_params=params,
+        cost_estimate=cost,
+    )(place, others, other_blocks, held)
+    return new_momentum, update
 
 
 def polynomial(gram_matrix):

time: 174 us -> 172 us (0.989)
  waiting for transfers between devices: 122 us -> 113 us
  starting transfers between devices: 23.5 us -> 29.2 us
    ppermute x20 -> x24, starting transfers between devices: 17.2 us -> 23 us  [over(): return lax.ppermute(value, 'cols', [(i, i ^ bits) for i in range(owners)])]
    ppermute x6, waiting for transfers between devices: 59.7 us -> 54.5 us  [onward(): lax.ppermute(value, 'dp', [(i, (i + k) % depth) for i in range(depth)])]
    ppermute x20 -> x24, waiting for transfers between devices: 62.5 us -> 58.3 us  [over(): return lax.ppermute(value, 'cols', [(i, i ^ bits) for i in range(owners)])]
    pallas_call x2 -> x3, Pallas kernels: 4.7 us -> 6.2 us  [the longest x1 2.61 us: shards(): pl.pallas_call(functools.partial(other_update_kernel, scale), in_specs=[i...]
  transfers between devices with their start and end apart: 26 -> 30, of which waited for: 17 -> 22; matrix products, arithmetic and copies ran while one was open for 0% -> 1% of each run, Pallas kernels for 9% -> 10%
where the time goes in v3:
time: 172 us
  waiting for transfers between devices  113 us (66%)
  starting transfers between devices  29.2 us (17%)
  Pallas kernels  25.5 us (15%)
  local copies, waits for them, and re-layouts  2.67 us (2%)
    ppermute x24, waiting for transfers between devices, over(): return lax.ppermute(value, 'cols', [(i, i ^ bits) for i in range(owners)])  58.3 us
    ppermute x6, waiting for transfers between devices, onward(): lax.ppermute(value, 'dp', [(i, (i + k) % depth) for i in range(depth)])  54.5 us
    ppermute x24, starting transfers between devices, over(): return lax.ppermute(value, 'cols', [(i, i ^ bits) for i in range(owners)])  23 us
    pallas_call x2, Pallas kernels, accumulate(): pl.pallas_call(functools.partial(accumulate_kernel, layouts, decay), grid...  10.7 us
    ppermute x6, starting transfers between devices, onward(): lax.ppermute(value, 'dp', [(i, (i + k) % depth) for i in range(depth)])  6.21 us
    pallas_call x2, Pallas kernels, last(): pl.pallas_call(functools.partial(last_kernel, core), in_specs=[in_smem] +...  4.93 us
    pallas_call x1, Pallas kernels, shards(): pl.pallas_call(polynomial_kernel, out_shape=jax.ShapeDtypeStruct(pieces[0...  3.62 us
  transfers between devices with their start and end apart: 30, of which 22 were waited for; matrix products, arithmetic and copies ran while one was open for 1% of the time, Pallas kernels for 10%

profile of v3, /device:TPU:0, one launch (start us, length us, event | category | flops | bytes accessed | tf_op | source)
XLA Modules:
  0.0 172.0 jit_solution(4207932974958503440)
XLA Ops:
  0.7 1.5 constant_dynamic-slice_fusion
  2.4 3.1 %collective-permute-start = (bf16[256,1024]{1,0:T(8,128)(2,1)S(1)}, bf16[256,1024]{1,0:T(8,128)(2,1)S(1)}, u32[]{:S(2)}, u32[]{:S(2)}) collective-permute-start(bf16[256,1024]{1,0:T(8,128)(2,1)S(1)} %bitcast.31), channel_id=1, source_target_pairs={{0,8},{8,16},{16,24},{24,0},{1,9},{9,17},{17,25},{25,1},{2,10},{10... | collective-permute-start | bytes 1572872 | tf_op jit(solution)/shard_map/ppermute | solution.py:155
  5.6 2.1 %collective-permute-start.1 = (bf16[256,1024]{1,0:T(8,128)(2,1)S(1)}, bf16[256,1024]{1,0:T(8,128)(2,1)S(1)}, u32[]{:S(2)}, u32[]{:S(2)}) collective-permute-start(bf16[256,1024]{1,0:T(8,128)(2,1)S(1)} %bitcast.32), channel_id=1, source_target_pairs={{0,24},{8,0},{16,8},{24,16},{1,25},{9,1},{17,9},{25,17},{2,26},{10... | collective-permute-start | bytes 1572872 | tf_op jit(solution)/shard_map/ppermute | solution.py:155
  7.9 12.3 %collective-permute-done = bf16[256,1024]{1,0:T(8,128)(2,1)S(1)} collective-permute-done((bf16[256,1024]{1,0:T(8,128)(2,1)S(1)}, bf16[256,1024]{1,0:T(8,128)(2,1)S(1)}, u32[]{:S(2)}, u32[]{:S(2)}) %collective-permute-start) | collective-permute-done | bytes 524320 | tf_op jit(solution)/shard_map/ppermute | solution.py:155
  20.3 10.1 %collective-permute-done.1 = bf16[256,1024]{1,0:T(8,128)(2,1)S(1)} collective-permute-done((bf16[256,1024]{1,0:T(8,128)(2,1)S(1)}, bf16[256,1024]{1,0:T(8,128)(2,1)S(1)}, u32[]{:S(2)}, u32[]{:S(2)}) %collective-permute-start.1) | collective-permute-done | bytes 524320 | tf_op jit(solution)/shard_map/ppermute | solution.py:155
  30.4 1.6 collective-permute-start.3
  31.9 0.5 collective-permute-start.4
  32.4 1.0 collective-permute-start.2
  33.5 1.4 collective-permute-start.5
  35.0 0.7 collective-permute-start.6
  35.6 4.0 %collective-permute-done.3 = bf16[1,128,1024]{2,1,0:T(8,128)(2,1)S(1)} collective-permute-done((bf16[1,128,1024]{2,1,0:T(8,128)(2,1)S(1)}, bf16[1,128,1024]{2,1,0:T(8,128)(2,1)S(1)}, u32[]{:S(2)}, u32[]{:S(2)}) %collective-permute-start.3) | collective-permute-done | bytes 262176 | tf_op jit(solution)/shard_map/ppermute | solution.py:152
  39.6 4.3 %collective-permute-done.4 = bf16[1,128,1024]{2,1,0:T(8,128)(2,1)S(1)} collective-permute-done((bf16[1,128,1024]{2,1,0:T(8,128)(2,1)S(1)}, bf16[1,128,1024]{2,1,0:T(8,128)(2,1)S(1)}, u32[]{:S(2)}, u32[]{:S(2)}) %collective-permute-start.4) | collective-permute-done | bytes 262176 | tf_op jit(solution)/shard_map/ppermute | solution.py:152
  44.0 1.8 %collective-permute-done.6 = bf16[1,128,1024]{2,1,0:T(8,128)(2,1)S(1)} collective-permute-done((bf16[1,128,1024]{2,1,0:T(8,128)(2,1)S(1)}, bf16[1,128,1024]{2,1,0:T(8,128)(2,1)S(1)}, u32[]{:S(2)}, u32[]{:S(2)}) %collective-permute-start.6) | collective-permute-done | bytes 262176 | tf_op jit(solution)/shard_map/ppermute | solution.py:152
  45.8 11.7 %collective-permute-done.2 = bf16[256,1024]{1,0:T(8,128)(2,1)S(1)} collective-permute-done((bf16[256,1024]{1,0:T(8,128)(2,1)S(1)}, bf16[256,1024]{1,0:T(8,128)(2,1)S(1)}, u32[]{:S(2)}, u32[]{:S(2)}) %collective-permute-start.2) | collective-permute-done | bytes 524320 | tf_op jit(solution)/shard_map/ppermute | solution.py:155
  57.5 1.5 collective-permute-start.7
  59.5 1.5 collective-permute-start.9
  61.8 10.6 %collective-permute-done.7 = bf16[1,256,1024]{2,1,0:T(8,128)(2,1)S(1)} collective-permute-done((bf16[1,256,1024]{2,1,0:T(8,128)(2,1)S(1)}, bf16[1,256,1024]{2,1,0:T(8,128)(2,1)S(1)}, u32[]{:S(2)}, u32[]{:S(2)}) %collective-permute-start.7) | collective-permute-done | bytes 524320 | tf_op jit(solution)/shard_map/ppermute | solution.py:152
  72.4 9.5 %collective-permute-done.8 = bf16[1,256,1024]{2,1,0:T(8,128)(2,1)S(1)} collective-permute-done((bf16[1,256,1024]{2,1,0:T(8,128)(2,1)S(1)}, bf16[1,256,1024]{2,1,0:T(8,128)(2,1)S(1)}, u32[]{:S(2)}, u32[]{:S(2)}) %collective-permute-start.8) | collective-permute-done | bytes 524320 | tf_op jit(solution)/shard_map/ppermute | solution.py:152
  82.0 1.4 collective-permute-done.10
  84.0 0.6 collective-permute-start.14
  84.6 1.6 collective-permute-start.12
  86.2 1.5 collective-permute-start.13
  87.7 5.3 %collective-permute-done.12 = bf16[1,128,1024]{2,1,0:T(8,128)(2,1)S(1)} collective-permute-done((bf16[1,128,1024]{2,1,0:T(8,128)(2,1)S(1)}, bf16[1,128,1024]{2,1,0:T(8,128)(2,1)S(1)}, u32[]{:S(2)}, u32[]{:S(2)}) %collective-permute-start.12) | collective-permute-done | bytes 262176 | tf_op jit(solution)/shard_map/ppermute | solution.py:152
  93.0 1.6 collective-permute-start.16
  94.8 1.5 collective-permute-start.17
  96.3 9.9 %collective-permute-done.16 = bf16[2,128,1024]{2,1,0:T(8,128)(2,1)S(1)} collective-permute-done((bf16[2,128,1024]{2,1,0:T(8,128)(2,1)S(1)}, bf16[2,128,1024]{2,1,0:T(8,128)(2,1)S(1)}, u32[]{:S(2)}, u32[]{:S(2)}) %collective-permute-start.16) | collective-permute-done | bytes 524320 | tf_op jit(solution)/shard_map/ppermute | solution.py:152
  106.2 1.4 collective-permute-done.17
  107.6 3.9 %collective-permute-done.18.refs_4_ = bf16[1024,512]{1,0:T(8,128)(2,1)S(1)} collective-permute-done((bf16[1024,512]{1,0:T(8,128)(2,1)S(1)}, bf16[1024,512]{1,0:T(8,128)(2,1)S(1)}, u32[]{:S(2)}, u32[]{:S(2)}) %collective-permute-start.18) | collective-permute-done | bytes 1048608 | tf_op jit(solution)/shard_map/ppermute | solution.py:155
  111.8 0.6 collective-permute-start.19
  112.4 7.2 %shard_map.50.total = f32[2048,512]{1,0:T(8,128)S(1)} custom-call(s32[2]{0:T(128)S(1)} %pad_add_fusion.place, f32[2048,512]{1,0:T(8,128)S(1)} %copy-done, bf16[1024,8192]{1,0:T(8,128)(2,1)} %refs_0_.1, bf16[1024,512]{1,0:T(8,128)(2,1)S(1)} %copy-done.1, bf16[4,256,1024]{2,1,0:T(8,128)(2,1)S(1)} %constant_dynamic-update-slice_fusion.refs_2_, ...), custom_call_target="tpu_custom_call" | custom-call | flops 4294967296 | bytes 16777216 | tf_op jit(solution)/shard_map/pallas_call | solution.py:223
  119.6 3.5 %shard_map.51.total = f32[2048,512]{1,0:T(8,128)S(1)} custom-call(s32[2]{0:T(128)S(1)} %pad_add_fusion.place, f32[2048,512]{1,0:T(8,128)S(1)} %shard_map.50.total, bf16[4,128,1024]{2,1,0:T(8,128)(2,1)S(1)} %constant_dynamic-update-slice_fusion.4.refs_0_, bf16[4,128,1024]{2,1,0:T(8,128)(2,1)S(1)} %collective-permute-done.19.refs_1_, ...), custom_call_target="tpu_custom_call" | custom-call | flops 2147483648 | bytes 12582912 | tf_op jit(solution)/shard_map/pallas_call | solution.py:223
  123.2 16.3 %collective-permute-done.21.x_ref = bf16[1024,512]{1,0:T(8,128)(2,1)S(1)} collective-permute-done((bf16[1024,512]{1,0:T(8,128)(2,1)S(1)}, bf16[1024,512]{1,0:T(8,128)(2,1)S(1)}, u32[]{:S(2)}, u32[]{:S(2)}) %collective-permute-start.21) | collective-permute-done | bytes 1048608 | tf_op jit(solution)/shard_map/ppermute | solution.py:155
  139.4 2.5 %shard_map.53 = (f32[4,256,512]{2,1,0:T(8,128)S(1)}, f32[4,2,128,128]{3,2,1,0:T(8,128)S(1)}) custom-call(s32[2]{0:T(128)S(1)} %pad_add_fusion.place, f32[2048,512]{1,0:T(8,128)S(1)} %shard_map.51.total, bf16[4,256,1024]{2,1,0:T(8,128)(2,1)S(1)} %collective-permute-done.15.queries, bf16[1024,512]{1,0:T(8,128)(2,1)S(1)} %collective-permute-done.21.x_ref), custom_call_target="tpu_custom_call" | custom-call | flops 1073741824 | bytes 2097152 | tf_op jit(solution)/shard_map/pallas_call | solution.py:259
  142.0 2.5 %shard_map.52 = (f32[4,256,512]{2,1,0:T(8,128)S(1)}, f32[4,2,128,128]{3,2,1,0:T(8,128)S(1)}) custom-call(s32[2]{0:T(128)S(1)} %pad_add_fusion.place, f32[2048,512]{1,0:T(8,128)S(1)} %shard_map.51.total, bf16[4,256,1024]{2,1,0:T(8,128)(2,1)S(1)} %constant_dynamic-update-slice_fusion.2.queries, bf16[1024,512]{1,0:T(8,128)(2,1)S(1)} %collective-permute-done.21.x_ref), custom_call_target="tpu_custom_call" | custom-call | flops 1073741824 | bytes 2097152 | tf_op jit(solution)/shard_map/pallas_call | solution.py:259
  144.6 2.5 %collective-permute-start.25 = (f32[2,128,128]{2,1,0:T(8,128)S(1)}, f32[2,128,128]{2,1,0:T(8,128)S(1)}, u32[]{:S(2)}, u32[]{:S(2)}) collective-permute-start(f32[2,128,128]{2,1,0:T(8,128)S(1)} %get-tuple-element.73), channel_id=1, source_target_pairs={{0,6},{1,7},{2,4},{3,5},{4,2},{5,3},{6,0},{7,1},{8,14},{9,15},{10,... | collective-permute-start | bytes 393224 | tf_op jit(solution)/shard_map/ppermute | solution.py:152
  147.1 0.6 collective-permute-start.24
  148.2 2.6 %shard_map.54 = f32[2048,512]{1,0:T(8,128)} custom-call(s32[2]{0:T(128)S(1)} %pad_add_fusion.place, f32[4,256,512]{2,1,0:T(8,128)S(1)} %get-tuple-element.63.own.blocks, f32[4,256,512]{2,1,0:T(8,128)S(1)} %get-tuple-element.64.other.blocks), custom_call_target="tpu_custom_call" | custom-call | bytes 8388608 | tf_op jit(solution)/shard_map/pallas_call | solution.py:276
  150.8 1.0 collective-permute-done.25.refs_3_
  151.7 2.5 %collective-permute-done.24.refs_2_ = f32[2,128,128]{2,1,0:T(8,128)S(1)} collective-permute-done((f32[2,128,128]{2,1,0:T(8,128)S(1)}, f32[2,128,128]{2,1,0:T(8,128)S(1)}, u32[]{:S(2)}, u32[]{:S(2)}) %collective-permute-start.24) | collective-permute-done | bytes 131104 | tf_op jit(solution)/shard_map/ppermute | solution.py:152
  154.4 3.6 %shard_map.55 = f32[2,128,128]{2,1,0:T(8,128)S(1)} custom-call(f32[2,128,128]{2,1,0:T(8,128)S(1)} %get-tuple-element.66.refs_0_, f32[2,128,128]{2,1,0:T(8,128)S(1)} %collective-permute-done.23.refs_1_, f32[2,128,128]{2,1,0:T(8,128)S(1)} %collective-permute-done.24.refs_2_, f32[2,128,128]{2,1,0:T(8,128)S(1)} %collective-permute-done.25.refs_3_), custom_call_target="tpu_custom_call" | custom-call | tf_op jit(solution)/shard_map/pallas_call | solution.py:288
  158.0 1.7 collective-permute-start.28
  159.7 1.3 collective-permute-start.27
  161.0 0.5 collective-permute-start.26
  161.6 3.8 %collective-permute-done.28 = f32[2,128,128]{2,1,0:T(8,128)S(1)} collective-permute-done((f32[2,128,128]{2,1,0:T(8,128)S(1)}, f32[2,128,128]{2,1,0:T(8,128)S(1)}, u32[]{:S(2)}, u32[]{:S(2)}) %collective-permute-start.28) | collective-permute-done | bytes 131104 | tf_op jit(solution)/shard_map/ppermute | solution.py:152
  165.4 1.8 %collective-permute-done.27 = f32[2,128,128]{2,1,0:T(8,128)S(1)} collective-permute-done((f32[2,128,128]{2,1,0:T(8,128)S(1)}, f32[2,128,128]{2,1,0:T(8,128)S(1)}, u32[]{:S(2)}, u32[]{:S(2)}) %collective-permute-start.27) | collective-permute-done | bytes 131104 | tf_op jit(solution)/shard_map/ppermute | solution.py:152
  167.3 1.0 shard_map.56.own
  168.3 0.9 collective-permute-done.29.factor
  169.2 2.6 %shard_map.57 = f32[2048,512]{1,0:T(8,128)} custom-call(s32[2]{0:T(128)S(1)} %pad_add_fusion.place, f32[4,2,128,128]{3,2,1,0:T(8,128)S(1)} %collective-permute-done.29.factor, f32[4,256,512]{2,1,0:T(8,128)S(1)} %get-tuple-element.64.other.blocks, f32[4,256,512]{2,1,0:T(8,128)S(1)} %shard_map.56.own), custom_call_target="tpu_custom_call" | custom-call | flops 402653184 | bytes 2097152 | tf_op jit(solution)/shard_map/pallas_call | solution.py:308
  (50 shorter events, 4.1 us)
Async XLA Ops:
  2.4 17.9 %collective-permute-start = (bf16[256,1024]{1,0:T(8,128)(2,1)S(1)}, bf16[256,1024]{1,0:T(8,128)(2,1)S(1)}, u32[]{:S(2)}, u32[]{:S(2)}) collective-permute-start(bf16[256,1024]{1,0:T(8,128)(2,1)S(1)} %bitcast.31), channel_id=1, source_target_pairs={{0,8},{8,16},{16,24},{24,0},{1,9},{9,17},{17,25},{25,1},{2,10},{10... | collective-permute-start | bytes 1572872 | tf_op jit(solution)/shard_map/ppermute | solution.py:155
  5.6 24.7 %collective-permute-start.1 = (bf16[256,1024]{1,0:T(8,128)(2,1)S(1)}, bf16[256,1024]{1,0:T(8,128)(2,1)S(1)}, u32[]{:S(2)}, u32[]{:S(2)}) collective-permute-start(bf16[256,1024]{1,0:T(8,128)(2,1)S(1)} %bitcast.32), channel_id=1, source_target_pairs={{0,24},{8,0},{16,8},{24,16},{1,25},{9,1},{17,9},{25,17},{2,26},{10... | collective-permute-start | bytes 1572872 | tf_op jit(solution)/shard_map/ppermute | solution.py:155
  30.3 27.2 %copy-start.1 = (bf16[1024,512]{1,0:T(8,128)(2,1)S(1)}, bf16[1024,512]{1,0:T(8,128)(2,1)}, u32[]{:S(2)}) copy-start(bf16[1024,512]{1,0:T(8,128)(2,1)} %refs_1_.1) | copy-start | bytes 3145732
  30.4 9.3 %collective-permute-start.3 = (bf16[1,128,1024]{2,1,0:T(8,128)(2,1)S(1)}, bf16[1,128,1024]{2,1,0:T(8,128)(2,1)S(1)}, u32[]{:S(2)}, u32[]{:S(2)}) collective-permute-start(bf16[1,128,1024]{2,1,0:T(8,128)(2,1)S(1)} %get-tuple-element.81), channel_id=1, source_target_pairs={{0,4},{1,5},{2,6},{3,7},{4,0},{5,1},{6,2},{7,3},{8,12},{9,13},{10,... | collective-permute-start | bytes 786440 | tf_op jit(solution)/shard_map/ppermute | solution.py:152
  31.9 12.0 %collective-permute-start.4 = (bf16[1,128,1024]{2,1,0:T(8,128)(2,1)S(1)}, bf16[1,128,1024]{2,1,0:T(8,128)(2,1)S(1)}, u32[]{:S(2)}, u32[]{:S(2)}) collective-permute-start(bf16[1,128,1024]{2,1,0:T(8,128)(2,1)S(1)} %get-tuple-element.82), channel_id=1, source_target_pairs={{0,4},{1,5},{2,6},{3,7},{4,0},{5,1},{6,2},{7,3},{8,12},{9,13},{10,... | collective-permute-start | bytes 786440 | tf_op jit(solution)/shard_map/ppermute | solution.py:152
  32.4 25.1 %collective-permute-start.2 = (bf16[256,1024]{1,0:T(8,128)(2,1)S(1)}, bf16[256,1024]{1,0:T(8,128)(2,1)S(1)}, u32[]{:S(2)}, u32[]{:S(2)}) collective-permute-start(bf16[256,1024]{1,0:T(8,128)(2,1)S(1)} %bitcast.30), channel_id=1, source_target_pairs={{0,16},{8,24},{16,0},{24,8},{1,17},{9,25},{17,1},{25,9},{2,18},{10... | collective-permute-start | bytes 1572872 | tf_op jit(solution)/shard_map/ppermute | solution.py:155
  33.5 10.4 %collective-permute-start.5 = (bf16[1,128,1024]{2,1,0:T(8,128)(2,1)S(1)}, bf16[1,128,1024]{2,1,0:T(8,128)(2,1)S(1)}, u32[]{:S(2)}, u32[]{:S(2)}) collective-permute-start(bf16[1,128,1024]{2,1,0:T(8,128)(2,1)S(1)} %get-tuple-element.79), channel_id=1, source_target_pairs={{0,2},{1,3},{2,0},{3,1},{4,6},{5,7},{6,4},{7,5},{8,10},{9,11},{10,... | collective-permute-start | bytes 786440 | tf_op jit(solution)/shard_map/ppermute | solution.py:152
  35.0 10.8 %collective-permute-start.6 = (bf16[1,128,1024]{2,1,0:T(8,128)(2,1)S(1)}, bf16[1,128,1024]{2,1,0:T(8,128)(2,1)S(1)}, u32[]{:S(2)}, u32[]{:S(2)}) collective-permute-start(bf16[1,128,1024]{2,1,0:T(8,128)(2,1)S(1)} %get-tuple-element.80), channel_id=1, source_target_pairs={{0,2},{1,3},{2,0},{3,1},{4,6},{5,7},{6,4},{7,5},{8,10},{9,11},{10,... | collective-permute-start | bytes 786440 | tf_op jit(solution)/shard_map/ppermute | solution.py:152
  57.5 26.1 %collective-permute-start.11 = (bf16[1024,512]{1,0:T(8,128)(2,1)S(1)}, bf16[1024,512]{1,0:T(8,128)(2,1)S(1)}, u32[]{:S(2)}, u32[]{:S(2)}) collective-permute-start(bf16[1024,512]{1,0:T(8,128)(2,1)S(1)} %copy-done.1), channel_id=1, source_target_pairs={{0,8},{8,16},{16,24},{24,0},{1,9},{9,17},{17,25},{25,1},{2,10},{10... | collective-permute-start | bytes 3145736 | tf_op jit(solution)/shard_map/ppermute | solution.py:155
  57.5 14.9 %collective-permute-start.7 = (bf16[1,256,1024]{2,1,0:T(8,128)(2,1)S(1)}, bf16[1,256,1024]{2,1,0:T(8,128)(2,1)S(1)}, u32[]{:S(2)}, u32[]{:S(2)}) collective-permute-start(bf16[1,256,1024]{2,1,0:T(8,128)(2,1)S(1)} %bitcast.28), channel_id=1, source_target_pairs={{0,2},{1,3},{2,0},{3,1},{4,6},{5,7},{6,4},{7,5},{8,10},{9,11},{10,... | collective-permute-start | bytes 1572872 | tf_op jit(solution)/shard_map/ppermute | solution.py:152
  59.0 22.8 %collective-permute-start.8 = (bf16[1,256,1024]{2,1,0:T(8,128)(2,1)S(1)}, bf16[1,256,1024]{2,1,0:T(8,128)(2,1)S(1)}, u32[]{:S(2)}, u32[]{:S(2)}) collective-permute-start(bf16[1,256,1024]{2,1,0:T(8,128)(2,1)S(1)} %pad_maximum_fusion.4), channel_id=1, source_target_pairs={{0,2},{1,3},{2,0},{3,1},{4,6},{5,7},{6,4},{7,5},{8,10},{9,11},{10,... | collective-permute-start | bytes 1572872 | tf_op jit(solution)/shard_map/ppermute | solution.py:152
  59.5 22.4 %collective-permute-start.9 = (bf16[1,256,1024]{2,1,0:T(8,128)(2,1)S(1)}, bf16[1,256,1024]{2,1,0:T(8,128)(2,1)S(1)}, u32[]{:S(2)}, u32[]{:S(2)}) collective-permute-start(bf16[1,256,1024]{2,1,0:T(8,128)(2,1)S(1)} %bitcast.25), channel_id=1, source_target_pairs={{0,4},{1,5},{2,6},{3,7},{4,0},{5,1},{6,2},{7,3},{8,12},{9,13},{10,... | collective-permute-start | bytes 1572872 | tf_op jit(solution)/shard_map/ppermute | solution.py:152
  61.1 22.3 %collective-permute-start.10 = (bf16[1,256,1024]{2,1,0:T(8,128)(2,1)S(1)}, bf16[1,256,1024]{2,1,0:T(8,128)(2,1)S(1)}, u32[]{:S(2)}, u32[]{:S(2)}) collective-permute-start(bf16[1,256,1024]{2,1,0:T(8,128)(2,1)S(1)} %pad_maximum_fusion.5), channel_id=1, source_target_pairs={{0,4},{1,5},{2,6},{3,7},{4,0},{5,1},{6,2},{7,3},{8,12},{9,13},{10,... | collective-permute-start | bytes 1572872 | tf_op jit(solution)/shard_map/ppermute | solution.py:152
  83.9 27.6 %collective-permute-start.15 = (bf16[4,256,1024]{2,1,0:T(8,128)(2,1)S(1)}, bf16[4,256,1024]{2,1,0:T(8,128)(2,1)S(1)}, u32[]{:S(2)}, u32[]{:S(2)}) collective-permute-start(bf16[4,256,1024]{2,1,0:T(8,128)(2,1)S(1)} %constant_dynamic-update-slice_fusion.2.queries), channel_id=1, source_target_pairs={{0,1},{1,0},{2,3},{3,2},{4,5},{5,4},{6,7},{7,6},{8,9},{9,8},{10,11... | collective-permute-start | bytes 6291464 | tf_op jit(solution)/shard_map/ppermute | solution.py:152
  84.0 27.5 %collective-permute-start.14 = (bf16[4,256,1024]{2,1,0:T(8,128)(2,1)S(1)}, bf16[4,256,1024]{2,1,0:T(8,128)(2,1)S(1)}, u32[]{:S(2)}, u32[]{:S(2)}) collective-permute-start(bf16[4,256,1024]{2,1,0:T(8,128)(2,1)S(1)} %constant_dynamic-update-slice_fusion.refs_2_), channel_id=1, source_target_pairs={{0,1},{1,0},{2,3},{3,2},{4,5},{5,4},{6,7},{7,6},{8,9},{9,8},{10,11... | collective-permute-start | bytes 6291464 | tf_op jit(solution)/shard_map/ppermute | solution.py:152
  84.6 26.9 %collective-permute-start.18 = (bf16[1024,512]{1,0:T(8,128)(2,1)S(1)}, bf16[1024,512]{1,0:T(8,128)(2,1)S(1)}, u32[]{:S(2)}, u32[]{:S(2)}) collective-permute-start(bf16[1024,512]{1,0:T(8,128)(2,1)S(1)} %collective-permute-done.11.refs_4_), channel_id=1, source_target_pairs={{0,8},{8,16},{16,24},{24,0},{1,9},{9,17},{17,25},{25,1},{2,10},{10... | collective-permute-start | bytes 3145736 | tf_op jit(solution)/shard_map/ppermute | solution.py:155
  84.6 8.4 %collective-permute-start.12 = (bf16[1,128,1024]{2,1,0:T(8,128)(2,1)S(1)}, bf16[1,128,1024]{2,1,0:T(8,128)(2,1)S(1)}, u32[]{:S(2)}, u32[]{:S(2)}) collective-permute-start(bf16[1,128,1024]{2,1,0:T(8,128)(2,1)S(1)} %get-tuple-element.78), channel_id=1, source_target_pairs={{0,4},{1,5},{2,6},{3,7},{4,0},{5,1},{6,2},{7,3},{8,12},{9,13},{10,... | collective-permute-start | bytes 786440 | tf_op jit(solution)/shard_map/ppermute | solution.py:152
  86.2 8.5 %collective-permute-start.13 = (bf16[1,128,1024]{2,1,0:T(8,128)(2,1)S(1)}, bf16[1,128,1024]{2,1,0:T(8,128)(2,1)S(1)}, u32[]{:S(2)}, u32[]{:S(2)}) collective-permute-start(bf16[1,128,1024]{2,1,0:T(8,128)(2,1)S(1)} %get-tuple-element.77), channel_id=1, source_target_pairs={{0,2},{1,3},{2,0},{3,1},{4,6},{5,7},{6,4},{7,5},{8,10},{9,11},{10,... | collective-permute-start | bytes 786440 | tf_op jit(solution)/shard_map/ppermute | solution.py:152
  93.0 13.1 %collective-permute-start.16 = (bf16[2,128,1024]{2,1,0:T(8,128)(2,1)S(1)}, bf16[2,128,1024]{2,1,0:T(8,128)(2,1)S(1)}, u32[]{:S(2)}, u32[]{:S(2)}) collective-permute-start(bf16[2,128,1024]{2,1,0:T(8,128)(2,1)S(1)} %pad_maximum_fusion.6), channel_id=1, source_target_pairs={{0,2},{1,3},{2,0},{3,1},{4,6},{5,7},{6,4},{7,5},{8,10},{9,11},{10,... | collective-permute-start | bytes 1572872 | tf_op jit(solution)/shard_map/ppermute | solution.py:152
  94.8 17.7 %copy-start = (f32[2048,512]{1,0:T(8,128)S(1)}, f32[2048,512]{1,0:T(8,128)}, u32[]{:S(2)}) copy-start(f32[2048,512]{1,0:T(8,128)} %total.1) | copy-start | bytes 12582916
  94.8 12.9 %collective-permute-start.17 = (bf16[2,128,1024]{2,1,0:T(8,128)(2,1)S(1)}, bf16[2,128,1024]{2,1,0:T(8,128)(2,1)S(1)}, u32[]{:S(2)}, u32[]{:S(2)}) collective-permute-start(bf16[2,128,1024]{2,1,0:T(8,128)(2,1)S(1)} %pad_maximum_fusion.7), channel_id=1, source_target_pairs={{0,4},{1,5},{2,6},{3,7},{4,0},{5,1},{6,2},{7,3},{8,12},{9,13},{10,... | collective-permute-start | bytes 1572872 | tf_op jit(solution)/shard_map/ppermute | solution.py:152
  111.7 7.9 %collective-permute-start.20 = (bf16[4,128,1024]{2,1,0:T(8,128)(2,1)S(1)}, bf16[4,128,1024]{2,1,0:T(8,128)(2,1)S(1)}, u32[]{:S(2)}, u32[]{:S(2)}) collective-permute-start(bf16[4,128,1024]{2,1,0:T(8,128)(2,1)S(1)} %constant_dynamic-update-slice_fusion.6.refs_2_), channel_id=1, source_target_pairs={{0,1},{1,0},{2,3},{3,2},{4,5},{5,4},{6,7},{7,6},{8,9},{9,8},{10,11... | collective-permute-start | bytes 3145736 | tf_op jit(solution)/shard_map/ppermute | solution.py:152
  111.8 7.8 %collective-permute-start.19 = (bf16[4,128,1024]{2,1,0:T(8,128)(2,1)S(1)}, bf16[4,128,1024]{2,1,0:T(8,128)(2,1)S(1)}, u32[]{:S(2)}, u32[]{:S(2)}) collective-permute-start(bf16[4,128,1024]{2,1,0:T(8,128)(2,1)S(1)} %constant_dynamic-update-slice_fusion.4.refs_0_), channel_id=1, source_target_pairs={{0,1},{1,0},{2,3},{3,2},{4,5},{5,4},{6,7},{7,6},{8,9},{9,8},{10,11... | collective-permute-start | bytes 3145736 | tf_op jit(solution)/shard_map/ppermute | solution.py:152
  112.3 27.1 %collective-permute-start.21 = (bf16[1024,512]{1,0:T(8,128)(2,1)S(1)}, bf16[1024,512]{1,0:T(8,128)(2,1)S(1)}, u32[]{:S(2)}, u32[]{:S(2)}) collective-permute-start(bf16[1024,512]{1,0:T(8,128)(2,1)S(1)} %collective-permute-done.18.refs_4_), channel_id=1, source_target_pairs={{0,8},{8,16},{16,24},{24,0},{1,9},{9,17},{17,25},{25,1},{2,10},{10... | collective-permute-start | bytes 3145736 | tf_op jit(solution)/shard_map/ppermute | solution.py:155
  141.9 2.6 %collective-permute-start.22 = (f32[4,2,128,128]{3,2,1,0:T(8,128)S(1)}, f32[4,2,128,128]{3,2,1,0:T(8,128)S(1)}, u32[]{:S(2)}, u32[]{:S(2)}) collective-permute-start(f32[4,2,128,128]{3,2,1,0:T(8,128)S(1)} %get-tuple-element.62), channel_id=1, source_target_pairs={{0,1},{1,0},{2,3},{3,2},{4,5},{5,4},{6,7},{7,6},{8,9},{9,8},{10,11... | collective-permute-start | bytes 1572872 | tf_op jit(solution)/shard_map/ppermute | solution.py:152
  144.6 7.2 %collective-permute-start.25 = (f32[2,128,128]{2,1,0:T(8,128)S(1)}, f32[2,128,128]{2,1,0:T(8,128)S(1)}, u32[]{:S(2)}, u32[]{:S(2)}) collective-permute-start(f32[2,128,128]{2,1,0:T(8,128)S(1)} %get-tuple-element.73), channel_id=1, source_target_pairs={{0,6},{1,7},{2,4},{3,5},{4,2},{5,3},{6,0},{7,1},{8,14},{9,15},{10,... | collective-permute-start | bytes 393224 | tf_op jit(solution)/shard_map/ppermute | solution.py:152
  147.1 7.2 %collective-permute-start.24 = (f32[2,128,128]{2,1,0:T(8,128)S(1)}, f32[2,128,128]{2,1,0:T(8,128)S(1)}, u32[]{:S(2)}, u32[]{:S(2)}) collective-permute-start(f32[2,128,128]{2,1,0:T(8,128)S(1)} %get-tuple-element.74), channel_id=1, source_target_pairs={{0,4},{1,5},{2,6},{3,7},{4,0},{5,1},{6,2},{7,3},{8,12},{9,13},{10,... | collective-permute-start | bytes 393224 | tf_op jit(solution)/shard_map/ppermute | solution.py:152
  147.7 6.7 %collective-permute-start.23 = (f32[2,128,128]{2,1,0:T(8,128)S(1)}, f32[2,128,128]{2,1,0:T(8,128)S(1)}, u32[]{:S(2)}, u32[]{:S(2)}) collective-permute-start(f32[2,128,128]{2,1,0:T(8,128)S(1)} %get-tuple-element.75), channel_id=1, source_target_pairs={{0,2},{1,3},{2,0},{3,1},{4,6},{5,7},{6,4},{7,5},{8,10},{9,11},{10,... | collective-permute-start | bytes 393224 | tf_op jit(solution)/shard_map/ppermute | solution.py:152
  158.0 7.4 %collective-permute-start.28 = (f32[2,128,128]{2,1,0:T(8,128)S(1)}, f32[2,128,128]{2,1,0:T(8,128)S(1)}, u32[]{:S(2)}, u32[]{:S(2)}) collective-permute-start(f32[2,128,128]{2,1,0:T(8,128)S(1)} %shard_map.55), channel_id=1, source_target_pairs={{0,6},{1,7},{2,4},{3,5},{4,2},{5,3},{6,0},{7,1},{8,14},{9,15},{10,... | collective-permute-start | bytes 393224 | tf_op jit(solution)/shard_map/ppermute | solution.py:152
  159.7 7.4 %collective-permute-start.27 = (f32[2,128,128]{2,1,0:T(8,128)S(1)}, f32[2,128,128]{2,1,0:T(8,128)S(1)}, u32[]{:S(2)}, u32[]{:S(2)}) collective-permute-start(f32[2,128,128]{2,1,0:T(8,128)S(1)} %shard_map.55), channel_id=1, source_target_pairs={{0,4},{1,5},{2,6},{3,7},{4,0},{5,1},{6,2},{7,3},{8,12},{9,13},{10,... | collective-permute-start | bytes 393224 | tf_op jit(solution)/shard_map/ppermute | solution.py:152
  161.0 6.2 %collective-permute-start.26 = (f32[2,128,128]{2,1,0:T(8,128)S(1)}, f32[2,128,128]{2,1,0:T(8,128)S(1)}, u32[]{:S(2)}, u32[]{:S(2)}) collective-permute-start(f32[2,128,128]{2,1,0:T(8,128)S(1)} %shard_map.55), channel_id=1, source_target_pairs={{0,2},{1,3},{2,0},{3,1},{4,6},{5,7},{6,4},{7,5},{8,10},{9,11},{10,... | collective-permute-start | bytes 393224 | tf_op jit(solution)/shard_map/ppermute | solution.py:152
  167.2 2.0 %collective-permute-start.29 = (f32[4,2,128,128]{3,2,1,0:T(8,128)S(1)}, f32[4,2,128,128]{3,2,1,0:T(8,128)S(1)}, u32[]{:S(2)}, u32[]{:S(2)}) collective-permute-start(f32[4,2,128,128]{3,2,1,0:T(8,128)S(1)} %pad_maximum_fusion.8.factor), channel_id=1, source_target_pairs={{0,1},{1,0},{2,3},{3,2},{4,5},{5,4},{6,7},{7,6},{8,9},{9,8},{10,11... | collective-permute-start | bytes 1572872 | tf_op jit(solution)/shard_map/ppermute | solution.py:152

commit v4 on v3

--- a/solution.py
+++ b/solution.py
@@ -169,7 +169,7 @@
     half = pair_rows // 2
 
     near = [onward(k, pieces[k - 1]) for k in (1, 3)]
-    near, pieces = lax.optimization_barrier((near, pieces))
+    near = lax.optimization_barrier(near)
 
     far = onward(2, pieces[1])
     near = [piece[None] for piece in near]

time: 172 us -> 168 us (0.977)
  waiting for transfers between devices: 113 us -> 109 us
    ppermute x6, waiting for transfers between devices: 54.5 us -> 49.4 us  [onward(): lax.ppermute(value, 'dp', [(i, (i + k) % depth) for i in range(depth)])]
where the time goes in v4:
time: 168 us
  waiting for transfers between devices  109 us (65%)
  starting transfers between devices  29.4 us (18%)
  Pallas kernels  25.5 us (15%)
  local copies, waits for them, and re-layouts  2.67 us (2%)
    ppermute x24, waiting for transfers between devices, over(): return lax.ppermute(value, 'cols', [(i, i ^ bits) for i in range(owners)])  59.5 us
    ppermute x6, waiting for transfers between devices, onward(): lax.ppermute(value, 'dp', [(i, (i + k) % depth) for i in range(depth)])  49.4 us
    ppermute x24, starting transfers between devices, over(): return lax.ppermute(value, 'cols', [(i, i ^ bits) for i in range(owners)])  23 us
    pallas_call x2, Pallas kernels, accumulate(): pl.pallas_call(functools.partial(accumulate_kernel, layouts, decay), grid...  10.7 us
    ppermute x6, starting transfers between devices, onward(): lax.ppermute(value, 'dp', [(i, (i + k) % depth) for i in range(depth)])  6.49 us
    pallas_call x2, Pallas kernels, last(): pl.pallas_call(functools.partial(last_kernel, core), in_specs=[in_smem] +...  4.93 us
    pallas_call x1, Pallas kernels, shards(): pl.pallas_call(polynomial_kernel, out_shape=jax.ShapeDtypeStruct(pieces[0...  3.62 us
  transfers between devices with their start and end apart: 30, of which 22 were waited for; matrix products, arithmetic and copies ran while one was open for 1% of the time, Pallas kernels for 10%

profile of v4, /device:TPU:0, one launch (start us, length us, event | category | flops | bytes accessed | tf_op | source)
XLA Modules:
  0.0 168.3 jit_solution(18397111306660360482)
XLA Ops:
  0.7 1.5 constant_dynamic-slice_fusion
  2.4 3.1 %collective-permute-start.1 = (bf16[256,1024]{1,0:T(8,128)(2,1)S(1)}, bf16[256,1024]{1,0:T(8,128)(2,1)S(1)}, u32[]{:S(2)}, u32[]{:S(2)}) collective-permute-start(bf16[256,1024]{1,0:T(8,128)(2,1)S(1)} %bitcast.31), channel_id=1, source_target_pairs={{0,8},{8,16},{16,24},{24,0},{1,9},{9,17},{17,25},{25,1},{2,10},{10... | collective-permute-start | bytes 1572872 | tf_op jit(solution)/shard_map/ppermute | solution.py:155
  5.6 2.1 %collective-permute-start.2 = (bf16[256,1024]{1,0:T(8,128)(2,1)S(1)}, bf16[256,1024]{1,0:T(8,128)(2,1)S(1)}, u32[]{:S(2)}, u32[]{:S(2)}) collective-permute-start(bf16[256,1024]{1,0:T(8,128)(2,1)S(1)} %bitcast.32), channel_id=1, source_target_pairs={{0,24},{8,0},{16,8},{24,16},{1,25},{9,1},{17,9},{25,17},{2,26},{10... | collective-permute-start | bytes 1572872 | tf_op jit(solution)/shard_map/ppermute | solution.py:155
  7.9 1.1 collective-permute-start
  9.0 11.2 %collective-permute-done.1 = bf16[256,1024]{1,0:T(8,128)(2,1)S(1)} collective-permute-done((bf16[256,1024]{1,0:T(8,128)(2,1)S(1)}, bf16[256,1024]{1,0:T(8,128)(2,1)S(1)}, u32[]{:S(2)}, u32[]{:S(2)}) %collective-permute-start.1) | collective-permute-done | bytes 524320 | tf_op jit(solution)/shard_map/ppermute | solution.py:155
  20.3 10.1 %collective-permute-done.2 = bf16[256,1024]{1,0:T(8,128)(2,1)S(1)} collective-permute-done((bf16[256,1024]{1,0:T(8,128)(2,1)S(1)}, bf16[256,1024]{1,0:T(8,128)(2,1)S(1)}, u32[]{:S(2)}, u32[]{:S(2)}) %collective-permute-start.2) | collective-permute-done | bytes 524320 | tf_op jit(solution)/shard_map/ppermute | solution.py:155
  30.4 1.6 collective-permute-start.5
  31.9 0.5 collective-permute-start.6
  32.5 1.6 collective-permute-start.3
  34.6 5.1 %collective-permute-done.5 = bf16[1,128,1024]{2,1,0:T(8,128)(2,1)S(1)} collective-permute-done((bf16[1,128,1024]{2,1,0:T(8,128)(2,1)S(1)}, bf16[1,128,1024]{2,1,0:T(8,128)(2,1)S(1)}, u32[]{:S(2)}, u32[]{:S(2)}) %collective-permute-start.5) | collective-permute-done | bytes 262176 | tf_op jit(solution)/shard_map/ppermute | solution.py:152
  39.6 4.3 %collective-permute-done.6 = bf16[1,128,1024]{2,1,0:T(8,128)(2,1)S(1)} collective-permute-done((bf16[1,128,1024]{2,1,0:T(8,128)(2,1)S(1)}, bf16[1,128,1024]{2,1,0:T(8,128)(2,1)S(1)}, u32[]{:S(2)}, u32[]{:S(2)}) %collective-permute-start.6) | collective-permute-done | bytes 262176 | tf_op jit(solution)/shard_map/ppermute | solution.py:152
  44.0 1.5 collective-permute-done.4
  45.5 7.6 %collective-permute-done = bf16[256,1024]{1,0:T(8,128)(2,1)S(1)} collective-permute-done((bf16[256,1024]{1,0:T(8,128)(2,1)S(1)}, bf16[256,1024]{1,0:T(8,128)(2,1)S(1)}, u32[]{:S(2)}, u32[]{:S(2)}) %collective-permute-start) | collective-permute-done | bytes 524320 | tf_op jit(solution)/shard_map/ppermute | solution.py:155
  53.3 1.5 collective-permute-start.7
  54.8 0.5 collective-permute-start.8
  55.4 1.5 collective-permute-start.9
  57.6 10.6 %collective-permute-done.7 = bf16[1,256,1024]{2,1,0:T(8,128)(2,1)S(1)} collective-permute-done((bf16[1,256,1024]{2,1,0:T(8,128)(2,1)S(1)}, bf16[1,256,1024]{2,1,0:T(8,128)(2,1)S(1)}, u32[]{:S(2)}, u32[]{:S(2)}) %collective-permute-start.7) | collective-permute-done | bytes 524320 | tf_op jit(solution)/shard_map/ppermute | solution.py:152
  68.2 10.0 %collective-permute-done.8 = bf16[1,256,1024]{2,1,0:T(8,128)(2,1)S(1)} collective-permute-done((bf16[1,256,1024]{2,1,0:T(8,128)(2,1)S(1)}, bf16[1,256,1024]{2,1,0:T(8,128)(2,1)S(1)}, u32[]{:S(2)}, u32[]{:S(2)}) %collective-permute-start.8) | collective-permute-done | bytes 524320 | tf_op jit(solution)/shard_map/ppermute | solution.py:152
  78.3 1.4 collective-permute-done.10
  80.4 0.6 collective-permute-start.14
  81.0 1.6 collective-permute-start.12
  82.5 1.5 collective-permute-start.13
  84.0 5.3 %collective-permute-done.12 = bf16[1,128,1024]{2,1,0:T(8,128)(2,1)S(1)} collective-permute-done((bf16[1,128,1024]{2,1,0:T(8,128)(2,1)S(1)}, bf16[1,128,1024]{2,1,0:T(8,128)(2,1)S(1)}, u32[]{:S(2)}, u32[]{:S(2)}) %collective-permute-start.12) | collective-permute-done | bytes 262176 | tf_op jit(solution)/shard_map/ppermute | solution.py:152
  89.4 1.6 collective-permute-start.16
  91.0 1.6 collective-permute-start.17
  92.6 9.9 %collective-permute-done.16 = bf16[2,128,1024]{2,1,0:T(8,128)(2,1)S(1)} collective-permute-done((bf16[2,128,1024]{2,1,0:T(8,128)(2,1)S(1)}, bf16[2,128,1024]{2,1,0:T(8,128)(2,1)S(1)}, u32[]{:S(2)}, u32[]{:S(2)}) %collective-permute-start.16) | collective-permute-done | bytes 524320 | tf_op jit(solution)/shard_map/ppermute | solution.py:152
  102.5 1.3 collective-permute-done.17
  103.9 4.0 %collective-permute-done.18.refs_4_ = bf16[1024,512]{1,0:T(8,128)(2,1)S(1)} collective-permute-done((bf16[1024,512]{1,0:T(8,128)(2,1)S(1)}, bf16[1024,512]{1,0:T(8,128)(2,1)S(1)}, u32[]{:S(2)}, u32[]{:S(2)}) %collective-permute-start.18) | collective-permute-done | bytes 1048608 | tf_op jit(solution)/shard_map/ppermute | solution.py:155
  108.1 0.6 collective-permute-start.19
  108.7 7.2 %shard_map.50.total = f32[2048,512]{1,0:T(8,128)S(1)} custom-call(s32[2]{0:T(128)S(1)} %pad_add_fusion.place, f32[2048,512]{1,0:T(8,128)S(1)} %copy-done, bf16[1024,8192]{1,0:T(8,128)(2,1)} %refs_0_.1, bf16[1024,512]{1,0:T(8,128)(2,1)S(1)} %copy-done.1, bf16[4,256,1024]{2,1,0:T(8,128)(2,1)S(1)} %constant_dynamic-update-slice_fusion.refs_2_, ...), custom_call_target="tpu_custom_call" | custom-call | flops 4294967296 | bytes 16777216 | tf_op jit(solution)/shard_map/pallas_call | solution.py:223
  115.9 3.5 %shard_map.51.total = f32[2048,512]{1,0:T(8,128)S(1)} custom-call(s32[2]{0:T(128)S(1)} %pad_add_fusion.place, f32[2048,512]{1,0:T(8,128)S(1)} %shard_map.50.total, bf16[4,128,1024]{2,1,0:T(8,128)(2,1)S(1)} %constant_dynamic-update-slice_fusion.4.refs_0_, bf16[4,128,1024]{2,1,0:T(8,128)(2,1)S(1)} %collective-permute-done.19.refs_1_, ...), custom_call_target="tpu_custom_call" | custom-call | flops 2147483648 | bytes 12582912 | tf_op jit(solution)/shard_map/pallas_call | solution.py:223
  119.5 16.3 %collective-permute-done.21.x_ref = bf16[1024,512]{1,0:T(8,128)(2,1)S(1)} collective-permute-done((bf16[1024,512]{1,0:T(8,128)(2,1)S(1)}, bf16[1024,512]{1,0:T(8,128)(2,1)S(1)}, u32[]{:S(2)}, u32[]{:S(2)}) %collective-permute-start.21) | collective-permute-done | bytes 1048608 | tf_op jit(solution)/shard_map/ppermute | solution.py:155
  135.8 2.5 %shard_map.53 = (f32[4,256,512]{2,1,0:T(8,128)S(1)}, f32[4,2,128,128]{3,2,1,0:T(8,128)S(1)}) custom-call(s32[2]{0:T(128)S(1)} %pad_add_fusion.place, f32[2048,512]{1,0:T(8,128)S(1)} %shard_map.51.total, bf16[4,256,1024]{2,1,0:T(8,128)(2,1)S(1)} %collective-permute-done.15.queries, bf16[1024,512]{1,0:T(8,128)(2,1)S(1)} %collective-permute-done.21.x_ref), custom_call_target="tpu_custom_call" | custom-call | flops 1073741824 | bytes 2097152 | tf_op jit(solution)/shard_map/pallas_call | solution.py:259
  138.3 2.5 %shard_map.52 = (f32[4,256,512]{2,1,0:T(8,128)S(1)}, f32[4,2,128,128]{3,2,1,0:T(8,128)S(1)}) custom-call(s32[2]{0:T(128)S(1)} %pad_add_fusion.place, f32[2048,512]{1,0:T(8,128)S(1)} %shard_map.51.total, bf16[4,256,1024]{2,1,0:T(8,128)(2,1)S(1)} %constant_dynamic-update-slice_fusion.2.queries, bf16[1024,512]{1,0:T(8,128)(2,1)S(1)} %collective-permute-done.21.x_ref), custom_call_target="tpu_custom_call" | custom-call | flops 1073741824 | bytes 2097152 | tf_op jit(solution)/shard_map/pallas_call | solution.py:259
  140.9 2.5 %collective-permute-start.25 = (f32[2,128,128]{2,1,0:T(8,128)S(1)}, f32[2,128,128]{2,1,0:T(8,128)S(1)}, u32[]{:S(2)}, u32[]{:S(2)}) collective-permute-start(f32[2,128,128]{2,1,0:T(8,128)S(1)} %get-tuple-element.71), channel_id=1, source_target_pairs={{0,6},{1,7},{2,4},{3,5},{4,2},{5,3},{6,0},{7,1},{8,14},{9,15},{10,... | collective-permute-start | bytes 393224 | tf_op jit(solution)/shard_map/ppermute | solution.py:152
  143.9 0.5 collective-permute-start.23
  144.5 2.6 %shard_map.54 = f32[2048,512]{1,0:T(8,128)} custom-call(s32[2]{0:T(128)S(1)} %pad_add_fusion.place, f32[4,256,512]{2,1,0:T(8,128)S(1)} %get-tuple-element.61.own.blocks, f32[4,256,512]{2,1,0:T(8,128)S(1)} %get-tuple-element.62.other.blocks), custom_call_target="tpu_custom_call" | custom-call | bytes 8388608 | tf_op jit(solution)/shard_map/pallas_call | solution.py:276
  147.1 1.0 collective-permute-done.25.refs_3_
  148.0 2.5 %collective-permute-done.24.refs_2_ = f32[2,128,128]{2,1,0:T(8,128)S(1)} collective-permute-done((f32[2,128,128]{2,1,0:T(8,128)S(1)}, f32[2,128,128]{2,1,0:T(8,128)S(1)}, u32[]{:S(2)}, u32[]{:S(2)}) %collective-permute-start.24) | collective-permute-done | bytes 131104 | tf_op jit(solution)/shard_map/ppermute | solution.py:152
  150.7 3.6 %shard_map.55 = f32[2,128,128]{2,1,0:T(8,128)S(1)} custom-call(f32[2,128,128]{2,1,0:T(8,128)S(1)} %get-tuple-element.64.refs_0_, f32[2,128,128]{2,1,0:T(8,128)S(1)} %collective-permute-done.23.refs_1_, f32[2,128,128]{2,1,0:T(8,128)S(1)} %collective-permute-done.24.refs_2_, f32[2,128,128]{2,1,0:T(8,128)S(1)} %collective-permute-done.25.refs_3_), custom_call_target="tpu_custom_call" | custom-call | tf_op jit(solution)/shard_map/pallas_call | solution.py:288
  154.3 1.7 %collective-permute-start.28 = (f32[2,128,128]{2,1,0:T(8,128)S(1)}, f32[2,128,128]{2,1,0:T(8,128)S(1)}, u32[]{:S(2)}, u32[]{:S(2)}) collective-permute-start(f32[2,128,128]{2,1,0:T(8,128)S(1)} %shard_map.55), channel_id=1, source_target_pairs={{0,6},{1,7},{2,4},{3,5},{4,2},{5,3},{6,0},{7,1},{8,14},{9,15},{10,... | collective-permute-start | bytes 393224 | tf_op jit(solution)/shard_map/ppermute | solution.py:152
  156.0 1.3 collective-permute-start.27
  157.3 0.5 collective-permute-start.26
  157.9 3.8 %collective-permute-done.28 = f32[2,128,128]{2,1,0:T(8,128)S(1)} collective-permute-done((f32[2,128,128]{2,1,0:T(8,128)S(1)}, f32[2,128,128]{2,1,0:T(8,128)S(1)}, u32[]{:S(2)}, u32[]{:S(2)}) %collective-permute-start.28) | collective-permute-done | bytes 131104 | tf_op jit(solution)/shard_map/ppermute | solution.py:152
  161.7 1.8 %collective-permute-done.27 = f32[2,128,128]{2,1,0:T(8,128)S(1)} collective-permute-done((f32[2,128,128]{2,1,0:T(8,128)S(1)}, f32[2,128,128]{2,1,0:T(8,128)S(1)}, u32[]{:S(2)}, u32[]{:S(2)}) %collective-permute-start.27) | collective-permute-done | bytes 131104 | tf_op jit(solution)/shard_map/ppermute | solution.py:152
  163.6 1.0 shard_map.56.own
  164.6 0.9 collective-permute-done.29.factor
  165.5 2.6 %shard_map.57 = f32[2048,512]{1,0:T(8,128)} custom-call(s32[2]{0:T(128)S(1)} %pad_add_fusion.place, f32[4,2,128,128]{3,2,1,0:T(8,128)S(1)} %collective-permute-done.29.factor, f32[4,256,512]{2,1,0:T(8,128)S(1)} %get-tuple-element.62.other.blocks, f32[4,256,512]{2,1,0:T(8,128)S(1)} %shard_map.56.own), custom_call_target="tpu_custom_call" | custom-call | flops 402653184 | bytes 2097152 | tf_op jit(solution)/shard_map/pallas_call | solution.py:308
  (50 shorter events, 4.4 us)
Async XLA Ops:
  2.4 17.9 %collective-permute-start.1 = (bf16[256,1024]{1,0:T(8,128)(2,1)S(1)}, bf16[256,1024]{1,0:T(8,128)(2,1)S(1)}, u32[]{:S(2)}, u32[]{:S(2)}) collective-permute-start(bf16[256,1024]{1,0:T(8,128)(2,1)S(1)} %bitcast.31), channel_id=1, source_target_pairs={{0,8},{8,16},{16,24},{24,0},{1,9},{9,17},{17,25},{25,1},{2,10},{10... | collective-permute-start | bytes 1572872 | tf_op jit(solution)/shard_map/ppermute | solution.py:155
  5.6 24.7 %collective-permute-start.2 = (bf16[256,1024]{1,0:T(8,128)(2,1)S(1)}, bf16[256,1024]{1,0:T(8,128)(2,1)S(1)}, u32[]{:S(2)}, u32[]{:S(2)}) collective-permute-start(bf16[256,1024]{1,0:T(8,128)(2,1)S(1)} %bitcast.32), channel_id=1, source_target_pairs={{0,24},{8,0},{16,8},{24,16},{1,25},{9,1},{17,9},{25,17},{2,26},{10... | collective-permute-start | bytes 1572872 | tf_op jit(solution)/shard_map/ppermute | solution.py:155
  7.9 45.1 %collective-permute-start = (bf16[256,1024]{1,0:T(8,128)(2,1)S(1)}, bf16[256,1024]{1,0:T(8,128)(2,1)S(1)}, u32[]{:S(2)}, u32[]{:S(2)}) collective-permute-start(bf16[256,1024]{1,0:T(8,128)(2,1)S(1)} %bitcast.30), channel_id=1, source_target_pairs={{0,16},{8,24},{16,0},{24,8},{1,17},{9,25},{17,1},{25,9},{2,18},{10... | collective-permute-start | bytes 1572872 | tf_op jit(solution)/shard_map/ppermute | solution.py:155
  30.3 22.8 %copy-start.1 = (bf16[1024,512]{1,0:T(8,128)(2,1)S(1)}, bf16[1024,512]{1,0:T(8,128)(2,1)}, u32[]{:S(2)}) copy-start(bf16[1024,512]{1,0:T(8,128)(2,1)} %refs_1_.1) | copy-start | bytes 3145732
  30.4 9.3 %collective-permute-start.5 = (bf16[1,128,1024]{2,1,0:T(8,128)(2,1)S(1)}, bf16[1,128,1024]{2,1,0:T(8,128)(2,1)S(1)}, u32[]{:S(2)}, u32[]{:S(2)}) collective-permute-start(bf16[1,128,1024]{2,1,0:T(8,128)(2,1)S(1)} %get-tuple-element.77), channel_id=1, source_target_pairs={{0,2},{1,3},{2,0},{3,1},{4,6},{5,7},{6,4},{7,5},{8,10},{9,11},{10,... | collective-permute-start | bytes 786440 | tf_op jit(solution)/shard_map/ppermute | solution.py:152
  31.9 12.0 %collective-permute-start.6 = (bf16[1,128,1024]{2,1,0:T(8,128)(2,1)S(1)}, bf16[1,128,1024]{2,1,0:T(8,128)(2,1)S(1)}, u32[]{:S(2)}, u32[]{:S(2)}) collective-permute-start(bf16[1,128,1024]{2,1,0:T(8,128)(2,1)S(1)} %get-tuple-element.78), channel_id=1, source_target_pairs={{0,2},{1,3},{2,0},{3,1},{4,6},{5,7},{6,4},{7,5},{8,10},{9,11},{10,... | collective-permute-start | bytes 786440 | tf_op jit(solution)/shard_map/ppermute | solution.py:152
  32.5 11.5 %collective-permute-start.3 = (bf16[1,128,1024]{2,1,0:T(8,128)(2,1)S(1)}, bf16[1,128,1024]{2,1,0:T(8,128)(2,1)S(1)}, u32[]{:S(2)}, u32[]{:S(2)}) collective-permute-start(bf16[1,128,1024]{2,1,0:T(8,128)(2,1)S(1)} %get-tuple-element.79), channel_id=1, source_target_pairs={{0,4},{1,5},{2,6},{3,7},{4,0},{5,1},{6,2},{7,3},{8,12},{9,13},{10,... | collective-permute-start | bytes 786440 | tf_op jit(solution)/shard_map/ppermute | solution.py:152
  34.1 11.4 %collective-permute-start.4 = (bf16[1,128,1024]{2,1,0:T(8,128)(2,1)S(1)}, bf16[1,128,1024]{2,1,0:T(8,128)(2,1)S(1)}, u32[]{:S(2)}, u32[]{:S(2)}) collective-permute-start(bf16[1,128,1024]{2,1,0:T(8,128)(2,1)S(1)} %get-tuple-element.80), channel_id=1, source_target_pairs={{0,4},{1,5},{2,6},{3,7},{4,0},{5,1},{6,2},{7,3},{8,12},{9,13},{10,... | collective-permute-start | bytes 786440 | tf_op jit(solution)/shard_map/ppermute | solution.py:152
  53.1 26.9 %collective-permute-start.11 = (bf16[1024,512]{1,0:T(8,128)(2,1)S(1)}, bf16[1024,512]{1,0:T(8,128)(2,1)S(1)}, u32[]{:S(2)}, u32[]{:S(2)}) collective-permute-start(bf16[1024,512]{1,0:T(8,128)(2,1)S(1)} %copy-done.1), channel_id=1, source_target_pairs={{0,8},{8,16},{16,24},{24,0},{1,9},{9,17},{17,25},{25,1},{2,10},{10... | collective-permute-start | bytes 3145736 | tf_op jit(solution)/shard_map/ppermute | solution.py:155
  53.3 14.8 %collective-permute-start.7 = (bf16[1,256,1024]{2,1,0:T(8,128)(2,1)S(1)}, bf16[1,256,1024]{2,1,0:T(8,128)(2,1)S(1)}, u32[]{:S(2)}, u32[]{:S(2)}) collective-permute-start(bf16[1,256,1024]{2,1,0:T(8,128)(2,1)S(1)} %bitcast.28), channel_id=1, source_target_pairs={{0,2},{1,3},{2,0},{3,1},{4,6},{5,7},{6,4},{7,5},{8,10},{9,11},{10,... | collective-permute-start | bytes 1572872 | tf_op jit(solution)/shard_map/ppermute | solution.py:152
  54.8 23.3 %collective-permute-start.8 = (bf16[1,256,1024]{2,1,0:T(8,128)(2,1)S(1)}, bf16[1,256,1024]{2,1,0:T(8,128)(2,1)S(1)}, u32[]{:S(2)}, u32[]{:S(2)}) collective-permute-start(bf16[1,256,1024]{2,1,0:T(8,128)(2,1)S(1)} %pad_maximum_fusion.4), channel_id=1, source_target_pairs={{0,2},{1,3},{2,0},{3,1},{4,6},{5,7},{6,4},{7,5},{8,10},{9,11},{10,... | collective-permute-start | bytes 1572872 | tf_op jit(solution)/shard_map/ppermute | solution.py:152
  55.4 22.9 %collective-permute-start.9 = (bf16[1,256,1024]{2,1,0:T(8,128)(2,1)S(1)}, bf16[1,256,1024]{2,1,0:T(8,128)(2,1)S(1)}, u32[]{:S(2)}, u32[]{:S(2)}) collective-permute-start(bf16[1,256,1024]{2,1,0:T(8,128)(2,1)S(1)} %bitcast.25), channel_id=1, source_target_pairs={{0,4},{1,5},{2,6},{3,7},{4,0},{5,1},{6,2},{7,3},{8,12},{9,13},{10,... | collective-permute-start | bytes 1572872 | tf_op jit(solution)/shard_map/ppermute | solution.py:152
  56.9 22.8 %collective-permute-start.10 = (bf16[1,256,1024]{2,1,0:T(8,128)(2,1)S(1)}, bf16[1,256,1024]{2,1,0:T(8,128)(2,1)S(1)}, u32[]{:S(2)}, u32[]{:S(2)}) collective-permute-start(bf16[1,256,1024]{2,1,0:T(8,128)(2,1)S(1)} %pad_maximum_fusion.5), channel_id=1, source_target_pairs={{0,4},{1,5},{2,6},{3,7},{4,0},{5,1},{6,2},{7,3},{8,12},{9,13},{10,... | collective-permute-start | bytes 1572872 | tf_op jit(solution)/shard_map/ppermute | solution.py:152
  80.2 27.6 %collective-permute-start.15 = (bf16[4,256,1024]{2,1,0:T(8,128)(2,1)S(1)}, bf16[4,256,1024]{2,1,0:T(8,128)(2,1)S(1)}, u32[]{:S(2)}, u32[]{:S(2)}) collective-permute-start(bf16[4,256,1024]{2,1,0:T(8,128)(2,1)S(1)} %constant_dynamic-update-slice_fusion.2.queries), channel_id=1, source_target_pairs={{0,1},{1,0},{2,3},{3,2},{4,5},{5,4},{6,7},{7,6},{8,9},{9,8},{10,11... | collective-permute-start | bytes 6291464 | tf_op jit(solution)/shard_map/ppermute | solution.py:152
  80.4 27.5 %collective-permute-start.14 = (bf16[4,256,1024]{2,1,0:T(8,128)(2,1)S(1)}, bf16[4,256,1024]{2,1,0:T(8,128)(2,1)S(1)}, u32[]{:S(2)}, u32[]{:S(2)}) collective-permute-start(bf16[4,256,1024]{2,1,0:T(8,128)(2,1)S(1)} %constant_dynamic-update-slice_fusion.refs_2_), channel_id=1, source_target_pairs={{0,1},{1,0},{2,3},{3,2},{4,5},{5,4},{6,7},{7,6},{8,9},{9,8},{10,11... | collective-permute-start | bytes 6291464 | tf_op jit(solution)/shard_map/ppermute | solution.py:152
  80.9 26.9 %collective-permute-start.18 = (bf16[1024,512]{1,0:T(8,128)(2,1)S(1)}, bf16[1024,512]{1,0:T(8,128)(2,1)S(1)}, u32[]{:S(2)}, u32[]{:S(2)}) collective-permute-start(bf16[1024,512]{1,0:T(8,128)(2,1)S(1)} %collective-permute-done.11.refs_4_), channel_id=1, source_target_pairs={{0,8},{8,16},{16,24},{24,0},{1,9},{9,17},{17,25},{25,1},{2,10},{10... | collective-permute-start | bytes 3145736 | tf_op jit(solution)/shard_map/ppermute | solution.py:155
  81.0 8.4 %collective-permute-start.12 = (bf16[1,128,1024]{2,1,0:T(8,128)(2,1)S(1)}, bf16[1,128,1024]{2,1,0:T(8,128)(2,1)S(1)}, u32[]{:S(2)}, u32[]{:S(2)}) collective-permute-start(bf16[1,128,1024]{2,1,0:T(8,128)(2,1)S(1)} %get-tuple-element.76), channel_id=1, source_target_pairs={{0,4},{1,5},{2,6},{3,7},{4,0},{5,1},{6,2},{7,3},{8,12},{9,13},{10,... | collective-permute-start | bytes 786440 | tf_op jit(solution)/shard_map/ppermute | solution.py:152
  82.5 8.4 %collective-permute-start.13 = (bf16[1,128,1024]{2,1,0:T(8,128)(2,1)S(1)}, bf16[1,128,1024]{2,1,0:T(8,128)(2,1)S(1)}, u32[]{:S(2)}, u32[]{:S(2)}) collective-permute-start(bf16[1,128,1024]{2,1,0:T(8,128)(2,1)S(1)} %get-tuple-element.75), channel_id=1, source_target_pairs={{0,2},{1,3},{2,0},{3,1},{4,6},{5,7},{6,4},{7,5},{8,10},{9,11},{10,... | collective-permute-start | bytes 786440 | tf_op jit(solution)/shard_map/ppermute | solution.py:152
  89.4 13.1 %collective-permute-start.16 = (bf16[2,128,1024]{2,1,0:T(8,128)(2,1)S(1)}, bf16[2,128,1024]{2,1,0:T(8,128)(2,1)S(1)}, u32[]{:S(2)}, u32[]{:S(2)}) collective-permute-start(bf16[2,128,1024]{2,1,0:T(8,128)(2,1)S(1)} %pad_maximum_fusion.6), channel_id=1, source_target_pairs={{0,2},{1,3},{2,0},{3,1},{4,6},{5,7},{6,4},{7,5},{8,10},{9,11},{10,... | collective-permute-start | bytes 1572872 | tf_op jit(solution)/shard_map/ppermute | solution.py:152
  91.0 17.8 %copy-start = (f32[2048,512]{1,0:T(8,128)S(1)}, f32[2048,512]{1,0:T(8,128)}, u32[]{:S(2)}) copy-start(f32[2048,512]{1,0:T(8,128)} %total.1) | copy-start | bytes 12582916
  91.0 12.9 %collective-permute-start.17 = (bf16[2,128,1024]{2,1,0:T(8,128)(2,1)S(1)}, bf16[2,128,1024]{2,1,0:T(8,128)(2,1)S(1)}, u32[]{:S(2)}, u32[]{:S(2)}) collective-permute-start(bf16[2,128,1024]{2,1,0:T(8,128)(2,1)S(1)} %pad_maximum_fusion.7), channel_id=1, source_target_pairs={{0,4},{1,5},{2,6},{3,7},{4,0},{5,1},{6,2},{7,3},{8,12},{9,13},{10,... | collective-permute-start | bytes 1572872 | tf_op jit(solution)/shard_map/ppermute | solution.py:152
  108.0 7.9 %collective-permute-start.20 = (bf16[4,128,1024]{2,1,0:T(8,128)(2,1)S(1)}, bf16[4,128,1024]{2,1,0:T(8,128)(2,1)S(1)}, u32[]{:S(2)}, u32[]{:S(2)}) collective-permute-start(bf16[4,128,1024]{2,1,0:T(8,128)(2,1)S(1)} %constant_dynamic-update-slice_fusion.6.refs_2_), channel_id=1, source_target_pairs={{0,1},{1,0},{2,3},{3,2},{4,5},{5,4},{6,7},{7,6},{8,9},{9,8},{10,11... | collective-permute-start | bytes 3145736 | tf_op jit(solution)/shard_map/ppermute | solution.py:152
  108.1 7.8 %collective-permute-start.19 = (bf16[4,128,1024]{2,1,0:T(8,128)(2,1)S(1)}, bf16[4,128,1024]{2,1,0:T(8,128)(2,1)S(1)}, u32[]{:S(2)}, u32[]{:S(2)}) collective-permute-start(bf16[4,128,1024]{2,1,0:T(8,128)(2,1)S(1)} %constant_dynamic-update-slice_fusion.4.refs_0_), channel_id=1, source_target_pairs={{0,1},{1,0},{2,3},{3,2},{4,5},{5,4},{6,7},{7,6},{8,9},{9,8},{10,11... | collective-permute-start | bytes 3145736 | tf_op jit(solution)/shard_map/ppermute | solution.py:152
  108.7 27.1 %collective-permute-start.21 = (bf16[1024,512]{1,0:T(8,128)(2,1)S(1)}, bf16[1024,512]{1,0:T(8,128)(2,1)S(1)}, u32[]{:S(2)}, u32[]{:S(2)}) collective-permute-start(bf16[1024,512]{1,0:T(8,128)(2,1)S(1)} %collective-permute-done.18.refs_4_), channel_id=1, source_target_pairs={{0,8},{8,16},{16,24},{24,0},{1,9},{9,17},{17,25},{25,1},{2,10},{10... | collective-permute-start | bytes 3145736 | tf_op jit(solution)/shard_map/ppermute | solution.py:155
  138.2 2.6 %collective-permute-start.22 = (f32[4,2,128,128]{3,2,1,0:T(8,128)S(1)}, f32[4,2,128,128]{3,2,1,0:T(8,128)S(1)}, u32[]{:S(2)}, u32[]{:S(2)}) collective-permute-start(f32[4,2,128,128]{3,2,1,0:T(8,128)S(1)} %get-tuple-element.60), channel_id=1, source_target_pairs={{0,1},{1,0},{2,3},{3,2},{4,5},{5,4},{6,7},{7,6},{8,9},{9,8},{10,11... | collective-permute-start | bytes 1572872 | tf_op jit(solution)/shard_map/ppermute | solution.py:152
  140.9 7.1 %collective-permute-start.25 = (f32[2,128,128]{2,1,0:T(8,128)S(1)}, f32[2,128,128]{2,1,0:T(8,128)S(1)}, u32[]{:S(2)}, u32[]{:S(2)}) collective-permute-start(f32[2,128,128]{2,1,0:T(8,128)S(1)} %get-tuple-element.71), channel_id=1, source_target_pairs={{0,6},{1,7},{2,4},{3,5},{4,2},{5,3},{6,0},{7,1},{8,14},{9,15},{10,... | collective-permute-start | bytes 393224 | tf_op jit(solution)/shard_map/ppermute | solution.py:152
  143.4 7.1 %collective-permute-start.24 = (f32[2,128,128]{2,1,0:T(8,128)S(1)}, f32[2,128,128]{2,1,0:T(8,128)S(1)}, u32[]{:S(2)}, u32[]{:S(2)}) collective-permute-start(f32[2,128,128]{2,1,0:T(8,128)S(1)} %get-tuple-element.72), channel_id=1, source_target_pairs={{0,4},{1,5},{2,6},{3,7},{4,0},{5,1},{6,2},{7,3},{8,12},{9,13},{10,... | collective-permute-start | bytes 393224 | tf_op jit(solution)/shard_map/ppermute | solution.py:152
  143.9 6.7 %collective-permute-start.23 = (f32[2,128,128]{2,1,0:T(8,128)S(1)}, f32[2,128,128]{2,1,0:T(8,128)S(1)}, u32[]{:S(2)}, u32[]{:S(2)}) collective-permute-start(f32[2,128,128]{2,1,0:T(8,128)S(1)} %get-tuple-element.73), channel_id=1, source_target_pairs={{0,2},{1,3},{2,0},{3,1},{4,6},{5,7},{6,4},{7,5},{8,10},{9,11},{10,... | collective-permute-start | bytes 393224 | tf_op jit(solution)/shard_map/ppermute | solution.py:152
  154.3 7.4 %collective-permute-start.28 = (f32[2,128,128]{2,1,0:T(8,128)S(1)}, f32[2,128,128]{2,1,0:T(8,128)S(1)}, u32[]{:S(2)}, u32[]{:S(2)}) collective-permute-start(f32[2,128,128]{2,1,0:T(8,128)S(1)} %shard_map.55), channel_id=1, source_target_pairs={{0,6},{1,7},{2,4},{3,5},{4,2},{5,3},{6,0},{7,1},{8,14},{9,15},{10,... | collective-permute-start | bytes 393224 | tf_op jit(solution)/shard_map/ppermute | solution.py:152
  156.0 7.4 %collective-permute-start.27 = (f32[2,128,128]{2,1,0:T(8,128)S(1)}, f32[2,128,128]{2,1,0:T(8,128)S(1)}, u32[]{:S(2)}, u32[]{:S(2)}) collective-permute-start(f32[2,128,128]{2,1,0:T(8,128)S(1)} %shard_map.55), channel_id=1, source_target_pairs={{0,4},{1,5},{2,6},{3,7},{4,0},{5,1},{6,2},{7,3},{8,12},{9,13},{10,... | collective-permute-start | bytes 393224 | tf_op jit(solution)/shard_map/ppermute | solution.py:152
  157.3 6.2 %collective-permute-start.26 = (f32[2,128,128]{2,1,0:T(8,128)S(1)}, f32[2,128,128]{2,1,0:T(8,128)S(1)}, u32[]{:S(2)}, u32[]{:S(2)}) collective-permute-start(f32[2,128,128]{2,1,0:T(8,128)S(1)} %shard_map.55), channel_id=1, source_target_pairs={{0,2},{1,3},{2,0},{3,1},{4,6},{5,7},{6,4},{7,5},{8,10},{9,11},{10,... | collective-permute-start | bytes 393224 | tf_op jit(solution)/shard_map/ppermute | solution.py:152
  163.6 2.0 %collective-permute-start.29 = (f32[4,2,128,128]{3,2,1,0:T(8,128)S(1)}, f32[4,2,128,128]{3,2,1,0:T(8,128)S(1)}, u32[]{:S(2)}, u32[]{:S(2)}) collective-permute-start(f32[4,2,128,128]{3,2,1,0:T(8,128)S(1)} %pad_maximum_fusion.8.factor), channel_id=1, source_target_pairs={{0,1},{1,0},{2,3},{3,2},{4,5},{5,4},{6,7},{7,6},{8,9},{9,8},{10,11... | collective-permute-start | bytes 1572872 | tf_op jit(solution)/shard_map/ppermute | solution.py:152

commit v5 on v4

--- a/solution.py
+++ b/solution.py
@@ -161,10 +161,11 @@
     def both(held, got):
         return [jnp.concatenate(pair) for pair in zip(held, got)]
 
-    pieces = [
-        lax.dynamic_slice(query_grads, (0, lax.rem(z + k, depth) * row_count + c * pair_rows), (tokens, pair_rows)).T
-        for k in range(1, depth)
-    ]
+    taken, starts = {}, [lax.rem(z + k, depth) * row_count + c * pair_rows for k in range(depth)]
+    for k in (1, 3, 2):
+        taken[k] = lax.dynamic_slice(query_grads, (0, starts[k]), (tokens, pair_rows)).T
+        taken[k], starts = lax.optimization_barrier((taken[k], starts))
+    pieces = [taken[k] for k in range(1, depth)]
     turns = ((4, 2), (2, 4))
     half = pair_rows // 2
 

time: 168 us -> 168 us (level)
  waiting for transfers between devices: 109 us -> 104 us
  local copies, waits for them, and re-layouts: 2.67 us -> 5 us
  starting transfers between devices: 29.4 us -> 31.1 us
    ppermute x24, waiting for transfers between devices: 59.5 us -> 54.8 us  [over(): return lax.ppermute(value, 'cols', [(i, i ^ bits) for i in range(owners)])]
    dynamic_slice x1 -> x3, local copies, waits for them, and re-layouts: 1.49 us -> 3.81 us  [shards(): lax.dynamic_slice(query_grads, (0, starts[k]), (tokens, pair_rows))]
    ppermute x6, starting transfers between devices: 6.49 us -> 8.19 us  [onward(): lax.ppermute(value, 'dp', [(i, (i + k) % depth) for i in range(depth)])]
where the time goes in v5:
time: 168 us
  waiting for transfers between devices  104 us (62%)
  starting transfers between devices  31.1 us (19%)
  Pallas kernels  25.5 us (15%)
  local copies, waits for them, and re-layouts  5 us (3%)
    ppermute x24, waiting for transfers between devices, over(): return lax.ppermute(value, 'cols', [(i, i ^ bits) for i in range(owners)])  54.8 us
    ppermute x6, waiting for transfers between devices, onward(): lax.ppermute(value, 'dp', [(i, (i + k) % depth) for i in range(depth)])  49.3 us
    ppermute x24, starting transfers between devices, over(): return lax.ppermute(value, 'cols', [(i, i ^ bits) for i in range(owners)])  23 us
    pallas_call x2, Pallas kernels, accumulate(): pl.pallas_call(functools.partial(accumulate_kernel, layouts, decay), grid...  10.7 us
    ppermute x6, starting transfers between devices, onward(): lax.ppermute(value, 'dp', [(i, (i + k) % depth) for i in range(depth)])  8.19 us
    pallas_call x2, Pallas kernels, last(): pl.pallas_call(functools.partial(last_kernel, core), in_specs=[in_smem] +...  4.95 us
    dynamic_slice x3, local copies, waits for them, and re-layouts, shards(): lax.dynamic_slice(query_grads, (0, starts[k]), (tokens, pair_rows))  3.81 us
    pallas_call x1, Pallas kernels, shards(): pl.pallas_call(polynomial_kernel, out_shape=jax.ShapeDtypeStruct(pieces[0...  3.62 us
  transfers between devices with their start and end apart: 30, of which 22 were waited for; matrix products, arithmetic and copies ran while one was open for 1% of the time, Pallas kernels for 10%

profile of v5, /device:TPU:0, one launch (start us, length us, event | category | flops | bytes accessed | tf_op | source)
XLA Modules:
  0.0 167.6 jit_solution(7827372003497061928)
XLA Ops:
  0.7 1.1 constant_dynamic-slice_fusion.2
  2.0 1.4 constant_dynamic-slice_fusion.1
  3.5 5.1 %collective-permute-start.2 = (bf16[256,1024]{1,0:T(8,128)(2,1)S(1)}, bf16[256,1024]{1,0:T(8,128)(2,1)S(1)}, u32[]{:S(2)}, u32[]{:S(2)}) collective-permute-start(bf16[256,1024]{1,0:T(8,128)(2,1)S(1)} %bitcast.32), channel_id=1, source_target_pairs={{0,24},{8,0},{16,8},{24,16},{1,25},{9,1},{17,9},{25,17},{2,26},{10... | collective-permute-start | bytes 1572872 | tf_op jit(solution)/shard_map/ppermute | solution.py:155
  8.6 1.4 constant_dynamic-slice_fusion
  10.2 1.1 collective-permute-start
  11.3 9.7 %collective-permute-done.2 = bf16[256,1024]{1,0:T(8,128)(2,1)S(1)} collective-permute-done((bf16[256,1024]{1,0:T(8,128)(2,1)S(1)}, bf16[256,1024]{1,0:T(8,128)(2,1)S(1)}, u32[]{:S(2)}, u32[]{:S(2)}) %collective-permute-start.2) | collective-permute-done | bytes 524320 | tf_op jit(solution)/shard_map/ppermute | solution.py:155
  21.0 12.2 %collective-permute-done.1 = bf16[256,1024]{1,0:T(8,128)(2,1)S(1)} collective-permute-done((bf16[256,1024]{1,0:T(8,128)(2,1)S(1)}, bf16[256,1024]{1,0:T(8,128)(2,1)S(1)}, u32[]{:S(2)}, u32[]{:S(2)}) %collective-permute-start.1) | collective-permute-done | bytes 524320 | tf_op jit(solution)/shard_map/ppermute | solution.py:155
  33.3 1.6 collective-permute-start.5
  35.4 1.6 collective-permute-start.3
  37.5 4.6 %collective-permute-done.5 = bf16[1,128,1024]{2,1,0:T(8,128)(2,1)S(1)} collective-permute-done((bf16[1,128,1024]{2,1,0:T(8,128)(2,1)S(1)}, bf16[1,128,1024]{2,1,0:T(8,128)(2,1)S(1)}, u32[]{:S(2)}, u32[]{:S(2)}) %collective-permute-start.5) | collective-permute-done | bytes 262176 | tf_op jit(solution)/shard_map/ppermute | solution.py:152
  42.1 2.8 %collective-permute-done.6 = bf16[1,128,1024]{2,1,0:T(8,128)(2,1)S(1)} collective-permute-done((bf16[1,128,1024]{2,1,0:T(8,128)(2,1)S(1)}, bf16[1,128,1024]{2,1,0:T(8,128)(2,1)S(1)}, u32[]{:S(2)}, u32[]{:S(2)}) %collective-permute-start.6) | collective-permute-done | bytes 262176 | tf_op jit(solution)/shard_map/ppermute | solution.py:152
  45.0 1.5 collective-permute-done.4
  46.5 6.9 %collective-permute-done = bf16[256,1024]{1,0:T(8,128)(2,1)S(1)} collective-permute-done((bf16[256,1024]{1,0:T(8,128)(2,1)S(1)}, bf16[256,1024]{1,0:T(8,128)(2,1)S(1)}, u32[]{:S(2)}, u32[]{:S(2)}) %collective-permute-start) | collective-permute-done | bytes 524320 | tf_op jit(solution)/shard_map/ppermute | solution.py:155
  53.4 2.0 %collective-permute-start.11 = (bf16[1024,512]{1,0:T(8,128)(2,1)S(1)}, bf16[1024,512]{1,0:T(8,128)(2,1)S(1)}, u32[]{:S(2)}, u32[]{:S(2)}) collective-permute-start(bf16[1024,512]{1,0:T(8,128)(2,1)S(1)} %copy-done.1), channel_id=1, source_target_pairs={{0,8},{8,16},{16,24},{24,0},{1,9},{9,17},{17,25},{25,1},{2,10},{10... | collective-permute-start | bytes 3145736 | tf_op jit(solution)/shard_map/ppermute | solution.py:155
  55.4 1.5 collective-permute-start.7
  56.9 0.5 collective-permute-start.8
  57.5 1.5 collective-permute-start.9
  59.7 10.6 %collective-permute-done.7 = bf16[1,256,1024]{2,1,0:T(8,128)(2,1)S(1)} collective-permute-done((bf16[1,256,1024]{2,1,0:T(8,128)(2,1)S(1)}, bf16[1,256,1024]{2,1,0:T(8,128)(2,1)S(1)}, u32[]{:S(2)}, u32[]{:S(2)}) %collective-permute-start.7) | collective-permute-done | bytes 524320 | tf_op jit(solution)/shard_map/ppermute | solution.py:152
  70.3 7.2 %collective-permute-done.8 = bf16[1,256,1024]{2,1,0:T(8,128)(2,1)S(1)} collective-permute-done((bf16[1,256,1024]{2,1,0:T(8,128)(2,1)S(1)}, bf16[1,256,1024]{2,1,0:T(8,128)(2,1)S(1)}, u32[]{:S(2)}, u32[]{:S(2)}) %collective-permute-start.8) | collective-permute-done | bytes 524320 | tf_op jit(solution)/shard_map/ppermute | solution.py:152
  77.6 1.4 collective-permute-done.10
  79.6 0.6 collective-permute-start.14
  80.2 1.6 collective-permute-start.12
  81.8 1.5 collective-permute-start.13
  83.3 5.3 %collective-permute-done.12 = bf16[1,128,1024]{2,1,0:T(8,128)(2,1)S(1)} collective-permute-done((bf16[1,128,1024]{2,1,0:T(8,128)(2,1)S(1)}, bf16[1,128,1024]{2,1,0:T(8,128)(2,1)S(1)}, u32[]{:S(2)}, u32[]{:S(2)}) %collective-permute-start.12) | collective-permute-done | bytes 262176 | tf_op jit(solution)/shard_map/ppermute | solution.py:152
  88.6 1.6 collective-permute-start.16
  90.3 1.6 collective-permute-start.17
  91.9 9.9 %collective-permute-done.16 = bf16[2,128,1024]{2,1,0:T(8,128)(2,1)S(1)} collective-permute-done((bf16[2,128,1024]{2,1,0:T(8,128)(2,1)S(1)}, bf16[2,128,1024]{2,1,0:T(8,128)(2,1)S(1)}, u32[]{:S(2)}, u32[]{:S(2)}) %collective-permute-start.16) | collective-permute-done | bytes 524320 | tf_op jit(solution)/shard_map/ppermute | solution.py:152
  101.8 1.3 collective-permute-done.17
  103.1 4.0 %collective-permute-done.18.refs_4_ = bf16[1024,512]{1,0:T(8,128)(2,1)S(1)} collective-permute-done((bf16[1024,512]{1,0:T(8,128)(2,1)S(1)}, bf16[1024,512]{1,0:T(8,128)(2,1)S(1)}, u32[]{:S(2)}, u32[]{:S(2)}) %collective-permute-start.18) | collective-permute-done | bytes 1048608 | tf_op jit(solution)/shard_map/ppermute | solution.py:155
  107.4 0.6 collective-permute-start.19
  108.0 7.2 %shard_map.50.total = f32[2048,512]{1,0:T(8,128)S(1)} custom-call(s32[2]{0:T(128)S(1)} %pad_add_fusion.place, f32[2048,512]{1,0:T(8,128)S(1)} %copy-done, bf16[1024,8192]{1,0:T(8,128)(2,1)} %refs_0_.1, bf16[1024,512]{1,0:T(8,128)(2,1)S(1)} %copy-done.1, bf16[4,256,1024]{2,1,0:T(8,128)(2,1)S(1)} %constant_dynamic-update-slice_fusion.refs_2_, ...), custom_call_target="tpu_custom_call" | custom-call | flops 4294967296 | bytes 16777216 | tf_op jit(solution)/shard_map/pallas_call | solution.py:224
  115.2 3.5 %shard_map.51.total = f32[2048,512]{1,0:T(8,128)S(1)} custom-call(s32[2]{0:T(128)S(1)} %pad_add_fusion.place, f32[2048,512]{1,0:T(8,128)S(1)} %shard_map.50.total, bf16[4,128,1024]{2,1,0:T(8,128)(2,1)S(1)} %constant_dynamic-update-slice_fusion.4.refs_0_, bf16[4,128,1024]{2,1,0:T(8,128)(2,1)S(1)} %collective-permute-done.19.refs_1_, ...), custom_call_target="tpu_custom_call" | custom-call | flops 2147483648 | bytes 12582912 | tf_op jit(solution)/shard_map/pallas_call | solution.py:224
  118.8 16.3 %collective-permute-done.21.x_ref = bf16[1024,512]{1,0:T(8,128)(2,1)S(1)} collective-permute-done((bf16[1024,512]{1,0:T(8,128)(2,1)S(1)}, bf16[1024,512]{1,0:T(8,128)(2,1)S(1)}, u32[]{:S(2)}, u32[]{:S(2)}) %collective-permute-start.21) | collective-permute-done | bytes 1048608 | tf_op jit(solution)/shard_map/ppermute | solution.py:155
  135.0 2.5 %shard_map.53 = (f32[4,256,512]{2,1,0:T(8,128)S(1)}, f32[4,2,128,128]{3,2,1,0:T(8,128)S(1)}) custom-call(s32[2]{0:T(128)S(1)} %pad_add_fusion.place, f32[2048,512]{1,0:T(8,128)S(1)} %shard_map.51.total, bf16[4,256,1024]{2,1,0:T(8,128)(2,1)S(1)} %collective-permute-done.15.queries, bf16[1024,512]{1,0:T(8,128)(2,1)S(1)} %collective-permute-done.21.x_ref), custom_call_target="tpu_custom_call" | custom-call | flops 1073741824 | bytes 2097152 | tf_op jit(solution)/shard_map/pallas_call | solution.py:260
  137.6 2.5 %shard_map.52 = (f32[4,256,512]{2,1,0:T(8,128)S(1)}, f32[4,2,128,128]{3,2,1,0:T(8,128)S(1)}) custom-call(s32[2]{0:T(128)S(1)} %pad_add_fusion.place, f32[2048,512]{1,0:T(8,128)S(1)} %shard_map.51.total, bf16[4,256,1024]{2,1,0:T(8,128)(2,1)S(1)} %constant_dynamic-update-slice_fusion.2.queries, bf16[1024,512]{1,0:T(8,128)(2,1)S(1)} %collective-permute-done.21.x_ref), custom_call_target="tpu_custom_call" | custom-call | flops 1073741824 | bytes 2097152 | tf_op jit(solution)/shard_map/pallas_call | solution.py:260
  140.2 2.5 %collective-permute-start.25 = (f32[2,128,128]{2,1,0:T(8,128)S(1)}, f32[2,128,128]{2,1,0:T(8,128)S(1)}, u32[]{:S(2)}, u32[]{:S(2)}) collective-permute-start(f32[2,128,128]{2,1,0:T(8,128)S(1)} %get-tuple-element.80), channel_id=1, source_target_pairs={{0,6},{1,7},{2,4},{3,5},{4,2},{5,3},{6,0},{7,1},{8,14},{9,15},{10,... | collective-permute-start | bytes 393224 | tf_op jit(solution)/shard_map/ppermute | solution.py:152
  143.2 0.6 collective-permute-start.23
  143.8 2.6 %shard_map.54 = f32[2048,512]{1,0:T(8,128)} custom-call(s32[2]{0:T(128)S(1)} %pad_add_fusion.place, f32[4,256,512]{2,1,0:T(8,128)S(1)} %get-tuple-element.73.own.blocks, f32[4,256,512]{2,1,0:T(8,128)S(1)} %get-tuple-element.74.other.blocks), custom_call_target="tpu_custom_call" | custom-call | bytes 8388608 | tf_op jit(solution)/shard_map/pallas_call | solution.py:277
  146.4 1.0 collective-permute-done.25.refs_3_
  147.4 2.5 %collective-permute-done.24.refs_2_ = f32[2,128,128]{2,1,0:T(8,128)S(1)} collective-permute-done((f32[2,128,128]{2,1,0:T(8,128)S(1)}, f32[2,128,128]{2,1,0:T(8,128)S(1)}, u32[]{:S(2)}, u32[]{:S(2)}) %collective-permute-start.24) | collective-permute-done | bytes 131104 | tf_op jit(solution)/shard_map/ppermute | solution.py:152
  150.0 3.6 %shard_map.55 = f32[2,128,128]{2,1,0:T(8,128)S(1)} custom-call(f32[2,128,128]{2,1,0:T(8,128)S(1)} %get-tuple-element.76.refs_0_, f32[2,128,128]{2,1,0:T(8,128)S(1)} %collective-permute-done.23.refs_1_, f32[2,128,128]{2,1,0:T(8,128)S(1)} %collective-permute-done.24.refs_2_, f32[2,128,128]{2,1,0:T(8,128)S(1)} %collective-permute-done.25.refs_3_), custom_call_target="tpu_custom_call" | custom-call | tf_op jit(solution)/shard_map/pallas_call | solution.py:289
  153.6 1.7 %collective-permute-start.28 = (f32[2,128,128]{2,1,0:T(8,128)S(1)}, f32[2,128,128]{2,1,0:T(8,128)S(1)}, u32[]{:S(2)}, u32[]{:S(2)}) collective-permute-start(f32[2,128,128]{2,1,0:T(8,128)S(1)} %shard_map.55), channel_id=1, source_target_pairs={{0,6},{1,7},{2,4},{3,5},{4,2},{5,3},{6,0},{7,1},{8,14},{9,15},{10,... | collective-permute-start | bytes 393224 | tf_op jit(solution)/shard_map/ppermute | solution.py:152
  155.3 1.3 collective-permute-start.27
  157.1 3.8 %collective-permute-done.28 = f32[2,128,128]{2,1,0:T(8,128)S(1)} collective-permute-done((f32[2,128,128]{2,1,0:T(8,128)S(1)}, f32[2,128,128]{2,1,0:T(8,128)S(1)}, u32[]{:S(2)}, u32[]{:S(2)}) %collective-permute-start.28) | collective-permute-done | bytes 131104 | tf_op jit(solution)/shard_map/ppermute | solution.py:152
  161.0 1.8 %collective-permute-done.27 = f32[2,128,128]{2,1,0:T(8,128)S(1)} collective-permute-done((f32[2,128,128]{2,1,0:T(8,128)S(1)}, f32[2,128,128]{2,1,0:T(8,128)S(1)}, u32[]{:S(2)}, u32[]{:S(2)}) %collective-permute-start.27) | collective-permute-done | bytes 131104 | tf_op jit(solution)/shard_map/ppermute | solution.py:152
  162.9 1.0 shard_map.56.own
  163.9 0.9 collective-permute-done.29.factor
  164.8 2.6 %shard_map.57 = f32[2048,512]{1,0:T(8,128)} custom-call(s32[2]{0:T(128)S(1)} %pad_add_fusion.place, f32[4,2,128,128]{3,2,1,0:T(8,128)S(1)} %collective-permute-done.29.factor, f32[4,256,512]{2,1,0:T(8,128)S(1)} %get-tuple-element.74.other.blocks, f32[4,256,512]{2,1,0:T(8,128)S(1)} %shard_map.56.own), custom_call_target="tpu_custom_call" | custom-call | flops 402653184 | bytes 2097152 | tf_op jit(solution)/shard_map/pallas_call | solution.py:309
  (52 shorter events, 5.2 us)
Async XLA Ops:
  3.5 17.4 %collective-permute-start.2 = (bf16[256,1024]{1,0:T(8,128)(2,1)S(1)}, bf16[256,1024]{1,0:T(8,128)(2,1)S(1)}, u32[]{:S(2)}, u32[]{:S(2)}) collective-permute-start(bf16[256,1024]{1,0:T(8,128)(2,1)S(1)} %bitcast.32), channel_id=1, source_target_pairs={{0,24},{8,0},{16,8},{24,16},{1,25},{9,1},{17,9},{25,17},{2,26},{10... | collective-permute-start | bytes 1572872 | tf_op jit(solution)/shard_map/ppermute | solution.py:155
  8.6 24.6 %collective-permute-start.1 = (bf16[256,1024]{1,0:T(8,128)(2,1)S(1)}, bf16[256,1024]{1,0:T(8,128)(2,1)S(1)}, u32[]{:S(2)}, u32[]{:S(2)}) collective-permute-start(bf16[256,1024]{1,0:T(8,128)(2,1)S(1)} %bitcast.31), channel_id=1, source_target_pairs={{0,8},{8,16},{16,24},{24,0},{1,9},{9,17},{17,25},{25,1},{2,10},{10... | collective-permute-start | bytes 1572872 | tf_op jit(solution)/shard_map/ppermute | solution.py:155
  10.2 43.2 %collective-permute-start = (bf16[256,1024]{1,0:T(8,128)(2,1)S(1)}, bf16[256,1024]{1,0:T(8,128)(2,1)S(1)}, u32[]{:S(2)}, u32[]{:S(2)}) collective-permute-start(bf16[256,1024]{1,0:T(8,128)(2,1)S(1)} %bitcast.30), channel_id=1, source_target_pairs={{0,16},{8,24},{16,0},{24,8},{1,17},{9,25},{17,1},{25,9},{2,18},{10... | collective-permute-start | bytes 1572872 | tf_op jit(solution)/shard_map/ppermute | solution.py:155
  33.2 20.2 %copy-start.1 = (bf16[1024,512]{1,0:T(8,128)(2,1)S(1)}, bf16[1024,512]{1,0:T(8,128)(2,1)}, u32[]{:S(2)}) copy-start(bf16[1024,512]{1,0:T(8,128)(2,1)} %refs_1_.1) | copy-start | bytes 3145732
  33.3 8.8 %collective-permute-start.5 = (bf16[1,128,1024]{2,1,0:T(8,128)(2,1)S(1)}, bf16[1,128,1024]{2,1,0:T(8,128)(2,1)S(1)}, u32[]{:S(2)}, u32[]{:S(2)}) collective-permute-start(bf16[1,128,1024]{2,1,0:T(8,128)(2,1)S(1)} %get-tuple-element.86), channel_id=1, source_target_pairs={{0,2},{1,3},{2,0},{3,1},{4,6},{5,7},{6,4},{7,5},{8,10},{9,11},{10,... | collective-permute-start | bytes 786440 | tf_op jit(solution)/shard_map/ppermute | solution.py:152
  34.8 10.1 %collective-permute-start.6 = (bf16[1,128,1024]{2,1,0:T(8,128)(2,1)S(1)}, bf16[1,128,1024]{2,1,0:T(8,128)(2,1)S(1)}, u32[]{:S(2)}, u32[]{:S(2)}) collective-permute-start(bf16[1,128,1024]{2,1,0:T(8,128)(2,1)S(1)} %get-tuple-element.87), channel_id=1, source_target_pairs={{0,2},{1,3},{2,0},{3,1},{4,6},{5,7},{6,4},{7,5},{8,10},{9,11},{10,... | collective-permute-start | bytes 786440 | tf_op jit(solution)/shard_map/ppermute | solution.py:152
  35.4 9.6 %collective-permute-start.3 = (bf16[1,128,1024]{2,1,0:T(8,128)(2,1)S(1)}, bf16[1,128,1024]{2,1,0:T(8,128)(2,1)S(1)}, u32[]{:S(2)}, u32[]{:S(2)}) collective-permute-start(bf16[1,128,1024]{2,1,0:T(8,128)(2,1)S(1)} %get-tuple-element.88), channel_id=1, source_target_pairs={{0,4},{1,5},{2,6},{3,7},{4,0},{5,1},{6,2},{7,3},{8,12},{9,13},{10,... | collective-permute-start | bytes 786440 | tf_op jit(solution)/shard_map/ppermute | solution.py:152
  37.0 9.5 %collective-permute-start.4 = (bf16[1,128,1024]{2,1,0:T(8,128)(2,1)S(1)}, bf16[1,128,1024]{2,1,0:T(8,128)(2,1)S(1)}, u32[]{:S(2)}, u32[]{:S(2)}) collective-permute-start(bf16[1,128,1024]{2,1,0:T(8,128)(2,1)S(1)} %get-tuple-element.89), channel_id=1, source_target_pairs={{0,4},{1,5},{2,6},{3,7},{4,0},{5,1},{6,2},{7,3},{8,12},{9,13},{10,... | collective-permute-start | bytes 786440 | tf_op jit(solution)/shard_map/ppermute | solution.py:152
  53.4 25.8 %collective-permute-start.11 = (bf16[1024,512]{1,0:T(8,128)(2,1)S(1)}, bf16[1024,512]{1,0:T(8,128)(2,1)S(1)}, u32[]{:S(2)}, u32[]{:S(2)}) collective-permute-start(bf16[1024,512]{1,0:T(8,128)(2,1)S(1)} %copy-done.1), channel_id=1, source_target_pairs={{0,8},{8,16},{16,24},{24,0},{1,9},{9,17},{17,25},{25,1},{2,10},{10... | collective-permute-start | bytes 3145736 | tf_op jit(solution)/shard_map/ppermute | solution.py:155
  55.4 14.9 %collective-permute-start.7 = (bf16[1,256,1024]{2,1,0:T(8,128)(2,1)S(1)}, bf16[1,256,1024]{2,1,0:T(8,128)(2,1)S(1)}, u32[]{:S(2)}, u32[]{:S(2)}) collective-permute-start(bf16[1,256,1024]{2,1,0:T(8,128)(2,1)S(1)} %bitcast.28), channel_id=1, source_target_pairs={{0,2},{1,3},{2,0},{3,1},{4,6},{5,7},{6,4},{7,5},{8,10},{9,11},{10,... | collective-permute-start | bytes 1572872 | tf_op jit(solution)/shard_map/ppermute | solution.py:152
  56.9 20.5 %collective-permute-start.8 = (bf16[1,256,1024]{2,1,0:T(8,128)(2,1)S(1)}, bf16[1,256,1024]{2,1,0:T(8,128)(2,1)S(1)}, u32[]{:S(2)}, u32[]{:S(2)}) collective-permute-start(bf16[1,256,1024]{2,1,0:T(8,128)(2,1)S(1)} %pad_maximum_fusion.4), channel_id=1, source_target_pairs={{0,2},{1,3},{2,0},{3,1},{4,6},{5,7},{6,4},{7,5},{8,10},{9,11},{10,... | collective-permute-start | bytes 1572872 | tf_op jit(solution)/shard_map/ppermute | solution.py:152
  57.5 20.1 %collective-permute-start.9 = (bf16[1,256,1024]{2,1,0:T(8,128)(2,1)S(1)}, bf16[1,256,1024]{2,1,0:T(8,128)(2,1)S(1)}, u32[]{:S(2)}, u32[]{:S(2)}) collective-permute-start(bf16[1,256,1024]{2,1,0:T(8,128)(2,1)S(1)} %bitcast.25), channel_id=1, source_target_pairs={{0,4},{1,5},{2,6},{3,7},{4,0},{5,1},{6,2},{7,3},{8,12},{9,13},{10,... | collective-permute-start | bytes 1572872 | tf_op jit(solution)/shard_map/ppermute | solution.py:152
  59.0 19.9 %collective-permute-start.10 = (bf16[1,256,1024]{2,1,0:T(8,128)(2,1)S(1)}, bf16[1,256,1024]{2,1,0:T(8,128)(2,1)S(1)}, u32[]{:S(2)}, u32[]{:S(2)}) collective-permute-start(bf16[1,256,1024]{2,1,0:T(8,128)(2,1)S(1)} %pad_maximum_fusion.5), channel_id=1, source_target_pairs={{0,4},{1,5},{2,6},{3,7},{4,0},{5,1},{6,2},{7,3},{8,12},{9,13},{10,... | collective-permute-start | bytes 1572872 | tf_op jit(solution)/shard_map/ppermute | solution.py:152
  79.5 27.6 %collective-permute-start.15 = (bf16[4,256,1024]{2,1,0:T(8,128)(2,1)S(1)}, bf16[4,256,1024]{2,1,0:T(8,128)(2,1)S(1)}, u32[]{:S(2)}, u32[]{:S(2)}) collective-permute-start(bf16[4,256,1024]{2,1,0:T(8,128)(2,1)S(1)} %constant_dynamic-update-slice_fusion.2.queries), channel_id=1, source_target_pairs={{0,1},{1,0},{2,3},{3,2},{4,5},{5,4},{6,7},{7,6},{8,9},{9,8},{10,11... | collective-permute-start | bytes 6291464 | tf_op jit(solution)/shard_map/ppermute | solution.py:152
  79.6 27.5 %collective-permute-start.14 = (bf16[4,256,1024]{2,1,0:T(8,128)(2,1)S(1)}, bf16[4,256,1024]{2,1,0:T(8,128)(2,1)S(1)}, u32[]{:S(2)}, u32[]{:S(2)}) collective-permute-start(bf16[4,256,1024]{2,1,0:T(8,128)(2,1)S(1)} %constant_dynamic-update-slice_fusion.refs_2_), channel_id=1, source_target_pairs={{0,1},{1,0},{2,3},{3,2},{4,5},{5,4},{6,7},{7,6},{8,9},{9,8},{10,11... | collective-permute-start | bytes 6291464 | tf_op jit(solution)/shard_map/ppermute | solution.py:152
  80.2 26.9 %collective-permute-start.18 = (bf16[1024,512]{1,0:T(8,128)(2,1)S(1)}, bf16[1024,512]{1,0:T(8,128)(2,1)S(1)}, u32[]{:S(2)}, u32[]{:S(2)}) collective-permute-start(bf16[1024,512]{1,0:T(8,128)(2,1)S(1)} %collective-permute-done.11.refs_4_), channel_id=1, source_target_pairs={{0,8},{8,16},{16,24},{24,0},{1,9},{9,17},{17,25},{25,1},{2,10},{10... | collective-permute-start | bytes 3145736 | tf_op jit(solution)/shard_map/ppermute | solution.py:155
  80.2 8.4 %collective-permute-start.12 = (bf16[1,128,1024]{2,1,0:T(8,128)(2,1)S(1)}, bf16[1,128,1024]{2,1,0:T(8,128)(2,1)S(1)}, u32[]{:S(2)}, u32[]{:S(2)}) collective-permute-start(bf16[1,128,1024]{2,1,0:T(8,128)(2,1)S(1)} %get-tuple-element.85), channel_id=1, source_target_pairs={{0,4},{1,5},{2,6},{3,7},{4,0},{5,1},{6,2},{7,3},{8,12},{9,13},{10,... | collective-permute-start | bytes 786440 | tf_op jit(solution)/shard_map/ppermute | solution.py:152
  81.8 8.4 %collective-permute-start.13 = (bf16[1,128,1024]{2,1,0:T(8,128)(2,1)S(1)}, bf16[1,128,1024]{2,1,0:T(8,128)(2,1)S(1)}, u32[]{:S(2)}, u32[]{:S(2)}) collective-permute-start(bf16[1,128,1024]{2,1,0:T(8,128)(2,1)S(1)} %get-tuple-element.84), channel_id=1, source_target_pairs={{0,2},{1,3},{2,0},{3,1},{4,6},{5,7},{6,4},{7,5},{8,10},{9,11},{10,... | collective-permute-start | bytes 786440 | tf_op jit(solution)/shard_map/ppermute | solution.py:152
  88.6 13.1 %collective-permute-start.16 = (bf16[2,128,1024]{2,1,0:T(8,128)(2,1)S(1)}, bf16[2,128,1024]{2,1,0:T(8,128)(2,1)S(1)}, u32[]{:S(2)}, u32[]{:S(2)}) collective-permute-start(bf16[2,128,1024]{2,1,0:T(8,128)(2,1)S(1)} %pad_maximum_fusion.6), channel_id=1, source_target_pairs={{0,2},{1,3},{2,0},{3,1},{4,6},{5,7},{6,4},{7,5},{8,10},{9,11},{10,... | collective-permute-start | bytes 1572872 | tf_op jit(solution)/shard_map/ppermute | solution.py:152
  90.3 17.8 %copy-start = (f32[2048,512]{1,0:T(8,128)S(1)}, f32[2048,512]{1,0:T(8,128)}, u32[]{:S(2)}) copy-start(f32[2048,512]{1,0:T(8,128)} %total.1) | copy-start | bytes 12582916
  90.3 12.9 %collective-permute-start.17 = (bf16[2,128,1024]{2,1,0:T(8,128)(2,1)S(1)}, bf16[2,128,1024]{2,1,0:T(8,128)(2,1)S(1)}, u32[]{:S(2)}, u32[]{:S(2)}) collective-permute-start(bf16[2,128,1024]{2,1,0:T(8,128)(2,1)S(1)} %pad_maximum_fusion.7), channel_id=1, source_target_pairs={{0,4},{1,5},{2,6},{3,7},{4,0},{5,1},{6,2},{7,3},{8,12},{9,13},{10,... | collective-permute-start | bytes 1572872 | tf_op jit(solution)/shard_map/ppermute | solution.py:152
  107.3 7.9 %collective-permute-start.20 = (bf16[4,128,1024]{2,1,0:T(8,128)(2,1)S(1)}, bf16[4,128,1024]{2,1,0:T(8,128)(2,1)S(1)}, u32[]{:S(2)}, u32[]{:S(2)}) collective-permute-start(bf16[4,128,1024]{2,1,0:T(8,128)(2,1)S(1)} %constant_dynamic-update-slice_fusion.6.refs_2_), channel_id=1, source_target_pairs={{0,1},{1,0},{2,3},{3,2},{4,5},{5,4},{6,7},{7,6},{8,9},{9,8},{10,11... | collective-permute-start | bytes 3145736 | tf_op jit(solution)/shard_map/ppermute | solution.py:152
  107.4 7.8 %collective-permute-start.19 = (bf16[4,128,1024]{2,1,0:T(8,128)(2,1)S(1)}, bf16[4,128,1024]{2,1,0:T(8,128)(2,1)S(1)}, u32[]{:S(2)}, u32[]{:S(2)}) collective-permute-start(bf16[4,128,1024]{2,1,0:T(8,128)(2,1)S(1)} %constant_dynamic-update-slice_fusion.4.refs_0_), channel_id=1, source_target_pairs={{0,1},{1,0},{2,3},{3,2},{4,5},{5,4},{6,7},{7,6},{8,9},{9,8},{10,11... | collective-permute-start | bytes 3145736 | tf_op jit(solution)/shard_map/ppermute | solution.py:152
  107.9 27.1 %collective-permute-start.21 = (bf16[1024,512]{1,0:T(8,128)(2,1)S(1)}, bf16[1024,512]{1,0:T(8,128)(2,1)S(1)}, u32[]{:S(2)}, u32[]{:S(2)}) collective-permute-start(bf16[1024,512]{1,0:T(8,128)(2,1)S(1)} %collective-permute-done.18.refs_4_), channel_id=1, source_target_pairs={{0,8},{8,16},{16,24},{24,0},{1,9},{9,17},{17,25},{25,1},{2,10},{10... | collective-permute-start | bytes 3145736 | tf_op jit(solution)/shard_map/ppermute | solution.py:155
  137.5 2.6 %collective-permute-start.22 = (f32[4,2,128,128]{3,2,1,0:T(8,128)S(1)}, f32[4,2,128,128]{3,2,1,0:T(8,128)S(1)}, u32[]{:S(2)}, u32[]{:S(2)}) collective-permute-start(f32[4,2,128,128]{3,2,1,0:T(8,128)S(1)} %get-tuple-element.72), channel_id=1, source_target_pairs={{0,1},{1,0},{2,3},{3,2},{4,5},{5,4},{6,7},{7,6},{8,9},{9,8},{10,11... | collective-permute-start | bytes 1572872 | tf_op jit(solution)/shard_map/ppermute | solution.py:152
  140.2 7.2 %collective-permute-start.25 = (f32[2,128,128]{2,1,0:T(8,128)S(1)}, f32[2,128,128]{2,1,0:T(8,128)S(1)}, u32[]{:S(2)}, u32[]{:S(2)}) collective-permute-start(f32[2,128,128]{2,1,0:T(8,128)S(1)} %get-tuple-element.80), channel_id=1, source_target_pairs={{0,6},{1,7},{2,4},{3,5},{4,2},{5,3},{6,0},{7,1},{8,14},{9,15},{10,... | collective-permute-start | bytes 393224 | tf_op jit(solution)/shard_map/ppermute | solution.py:152
  142.7 7.2 %collective-permute-start.24 = (f32[2,128,128]{2,1,0:T(8,128)S(1)}, f32[2,128,128]{2,1,0:T(8,128)S(1)}, u32[]{:S(2)}, u32[]{:S(2)}) collective-permute-start(f32[2,128,128]{2,1,0:T(8,128)S(1)} %get-tuple-element.81), channel_id=1, source_target_pairs={{0,4},{1,5},{2,6},{3,7},{4,0},{5,1},{6,2},{7,3},{8,12},{9,13},{10,... | collective-permute-start | bytes 393224 | tf_op jit(solution)/shard_map/ppermute | solution.py:152
  143.2 6.8 %collective-permute-start.23 = (f32[2,128,128]{2,1,0:T(8,128)S(1)}, f32[2,128,128]{2,1,0:T(8,128)S(1)}, u32[]{:S(2)}, u32[]{:S(2)}) collective-permute-start(f32[2,128,128]{2,1,0:T(8,128)S(1)} %get-tuple-element.82), channel_id=1, source_target_pairs={{0,2},{1,3},{2,0},{3,1},{4,6},{5,7},{6,4},{7,5},{8,10},{9,11},{10,... | collective-permute-start | bytes 393224 | tf_op jit(solution)/shard_map/ppermute | solution.py:152
  153.6 7.4 %collective-permute-start.28 = (f32[2,128,128]{2,1,0:T(8,128)S(1)}, f32[2,128,128]{2,1,0:T(8,128)S(1)}, u32[]{:S(2)}, u32[]{:S(2)}) collective-permute-start(f32[2,128,128]{2,1,0:T(8,128)S(1)} %shard_map.55), channel_id=1, source_target_pairs={{0,6},{1,7},{2,4},{3,5},{4,2},{5,3},{6,0},{7,1},{8,14},{9,15},{10,... | collective-permute-start | bytes 393224 | tf_op jit(solution)/shard_map/ppermute | solution.py:152
  155.3 7.4 %collective-permute-start.27 = (f32[2,128,128]{2,1,0:T(8,128)S(1)}, f32[2,128,128]{2,1,0:T(8,128)S(1)}, u32[]{:S(2)}, u32[]{:S(2)}) collective-permute-start(f32[2,128,128]{2,1,0:T(8,128)S(1)} %shard_map.55), channel_id=1, source_target_pairs={{0,4},{1,5},{2,6},{3,7},{4,0},{5,1},{6,2},{7,3},{8,12},{9,13},{10,... | collective-permute-start | bytes 393224 | tf_op jit(solution)/shard_map/ppermute | solution.py:152
  156.6 6.2 %collective-permute-start.26 = (f32[2,128,128]{2,1,0:T(8,128)S(1)}, f32[2,128,128]{2,1,0:T(8,128)S(1)}, u32[]{:S(2)}, u32[]{:S(2)}) collective-permute-start(f32[2,128,128]{2,1,0:T(8,128)S(1)} %shard_map.55), channel_id=1, source_target_pairs={{0,2},{1,3},{2,0},{3,1},{4,6},{5,7},{6,4},{7,5},{8,10},{9,11},{10,... | collective-permute-start | bytes 393224 | tf_op jit(solution)/shard_map/ppermute | solution.py:152
  162.8 2.0 %collective-permute-start.29 = (f32[4,2,128,128]{3,2,1,0:T(8,128)S(1)}, f32[4,2,128,128]{3,2,1,0:T(8,128)S(1)}, u32[]{:S(2)}, u32[]{:S(2)}) collective-permute-start(f32[4,2,128,128]{3,2,1,0:T(8,128)S(1)} %pad_maximum_fusion.8.factor), channel_id=1, source_target_pairs={{0,1},{1,0},{2,3},{3,2},{4,5},{5,4},{6,7},{7,6},{8,9},{9,8},{10,11... | collective-permute-start | bytes 1572872 | tf_op jit(solution)/shard_map/ppermute | solution.py:152

commit v6 on v4

--- a/solution.py
+++ b/solution.py
@@ -161,10 +161,13 @@
     def both(held, got):
         return [jnp.concatenate(pair) for pair in zip(held, got)]
 
-    pieces = [
-        lax.dynamic_slice(query_grads, (0, lax.rem(z + k, depth) * row_count + c * pair_rows), (tokens, pair_rows)).T
-        for k in range(1, depth)
-    ]
+    starts = [lax.rem(z + k, depth) * row_count + c * pair_rows for k in range(depth)]
+
+    def taken(start):
+        return lax.dynamic_slice(query_grads, (0, start), (tokens, pair_rows)).T
+
+    first, third, starts = lax.optimization_barrier((taken(starts[1]), taken(starts[3]), starts))
+    pieces = [first, taken(starts[2]), third]
     turns = ((4, 2), (2, 4))
     half = pair_rows // 2
 

time: 168 us -> 169 us (level)
  no operation moved by 1% of the time
where the time goes in v6:
time: 169 us; the launch traced here: 168 us
  waiting for transfers between devices  108 us (64%)
  starting transfers between devices  29.4 us (17%)
  Pallas kernels  25.5 us (15%)
  local copies, waits for them, and re-layouts  3.83 us (2%)
    ppermute x24, waiting for transfers between devices, over(): return lax.ppermute(value, 'cols', [(i, i ^ bits) for i in range(owners)])  59.3 us
    ppermute x6, waiting for transfers between devices, onward(): lax.ppermute(value, 'dp', [(i, (i + k) % depth) for i in range(depth)])  48.5 us
    ppermute x24, starting transfers between devices, over(): return lax.ppermute(value, 'cols', [(i, i ^ bits) for i in range(owners)])  23 us
    pallas_call x2, Pallas kernels, accumulate(): pl.pallas_call(functools.partial(accumulate_kernel, layouts, decay), grid...  10.7 us
    ppermute x6, starting transfers between devices, onward(): lax.ppermute(value, 'dp', [(i, (i + k) % depth) for i in range(depth)])  6.44 us
    pallas_call x2, Pallas kernels, last(): pl.pallas_call(functools.partial(last_kernel, core), in_specs=[in_smem] +...  4.93 us
    pallas_call x1, Pallas kernels, shards(): pl.pallas_call(polynomial_kernel, out_shape=jax.ShapeDtypeStruct(pieces[0...  3.62 us
  transfers between devices with their start and end apart: 30, of which 22 were waited for; matrix products, arithmetic and copies ran while one was open for 1% of the time, Pallas kernels for 10%

profile of v6, /device:TPU:0, one launch (start us, length us, event | category | flops | bytes accessed | tf_op | source)
XLA Modules:
  0.0 168.3 jit_solution(11790940485676208602)
XLA Ops:
  0.7 1.3 constant_dynamic-slice_fusion.1
  2.4 3.1 %collective-permute-start.1 = (bf16[256,1024]{1,0:T(8,128)(2,1)S(1)}, bf16[256,1024]{1,0:T(8,128)(2,1)S(1)}, u32[]{:S(2)}, u32[]{:S(2)}) collective-permute-start(bf16[256,1024]{1,0:T(8,128)(2,1)S(1)} %bitcast.32), channel_id=1, source_target_pairs={{0,8},{8,16},{16,24},{24,0},{1,9},{9,17},{17,25},{25,1},{2,10},{10... | collective-permute-start | bytes 1572872 | tf_op jit(solution)/shard_map/ppermute | solution.py:155
  5.4 2.1 %collective-permute-start.2 = (bf16[256,1024]{1,0:T(8,128)(2,1)S(1)}, bf16[256,1024]{1,0:T(8,128)(2,1)S(1)}, u32[]{:S(2)}, u32[]{:S(2)}) collective-permute-start(bf16[256,1024]{1,0:T(8,128)(2,1)S(1)} %bitcast.31), channel_id=1, source_target_pairs={{0,24},{8,0},{16,8},{24,16},{1,25},{9,1},{17,9},{25,17},{2,26},{10... | collective-permute-start | bytes 1572872 | tf_op jit(solution)/shard_map/ppermute | solution.py:155
  7.5 1.4 constant_dynamic-slice_fusion
  9.1 1.0 collective-permute-start
  10.1 10.1 %collective-permute-done.1 = bf16[256,1024]{1,0:T(8,128)(2,1)S(1)} collective-permute-done((bf16[256,1024]{1,0:T(8,128)(2,1)S(1)}, bf16[256,1024]{1,0:T(8,128)(2,1)S(1)}, u32[]{:S(2)}, u32[]{:S(2)}) %collective-permute-start.1) | collective-permute-done | bytes 524320 | tf_op jit(solution)/shard_map/ppermute | solution.py:155
  20.3 9.8 %collective-permute-done.2 = bf16[256,1024]{1,0:T(8,128)(2,1)S(1)} collective-permute-done((bf16[256,1024]{1,0:T(8,128)(2,1)S(1)}, bf16[256,1024]{1,0:T(8,128)(2,1)S(1)}, u32[]{:S(2)}, u32[]{:S(2)}) %collective-permute-start.2) | collective-permute-done | bytes 524320 | tf_op jit(solution)/shard_map/ppermute | solution.py:155
  30.1 1.6 collective-permute-start.5
  31.7 0.5 collective-permute-start.6
  32.2 1.6 collective-permute-start.3
  34.3 5.1 %collective-permute-done.5 = bf16[1,128,1024]{2,1,0:T(8,128)(2,1)S(1)} collective-permute-done((bf16[1,128,1024]{2,1,0:T(8,128)(2,1)S(1)}, bf16[1,128,1024]{2,1,0:T(8,128)(2,1)S(1)}, u32[]{:S(2)}, u32[]{:S(2)}) %collective-permute-start.5) | collective-permute-done | bytes 262176 | tf_op jit(solution)/shard_map/ppermute | solution.py:152
  39.4 4.0 %collective-permute-done.6 = bf16[1,128,1024]{2,1,0:T(8,128)(2,1)S(1)} collective-permute-done((bf16[1,128,1024]{2,1,0:T(8,128)(2,1)S(1)}, bf16[1,128,1024]{2,1,0:T(8,128)(2,1)S(1)}, u32[]{:S(2)}, u32[]{:S(2)}) %collective-permute-start.6) | collective-permute-done | bytes 262176 | tf_op jit(solution)/shard_map/ppermute | solution.py:152
  43.4 1.5 collective-permute-done.4
  45.0 8.1 %collective-permute-done = bf16[256,1024]{1,0:T(8,128)(2,1)S(1)} collective-permute-done((bf16[256,1024]{1,0:T(8,128)(2,1)S(1)}, bf16[256,1024]{1,0:T(8,128)(2,1)S(1)}, u32[]{:S(2)}, u32[]{:S(2)}) %collective-permute-start) | collective-permute-done | bytes 524320 | tf_op jit(solution)/shard_map/ppermute | solution.py:155
  53.3 1.5 collective-permute-start.7
  54.8 0.5 collective-permute-start.8
  55.4 1.5 collective-permute-start.9
  57.6 10.6 %collective-permute-done.7 = bf16[1,256,1024]{2,1,0:T(8,128)(2,1)S(1)} collective-permute-done((bf16[1,256,1024]{2,1,0:T(8,128)(2,1)S(1)}, bf16[1,256,1024]{2,1,0:T(8,128)(2,1)S(1)}, u32[]{:S(2)}, u32[]{:S(2)}) %collective-permute-start.7) | collective-permute-done | bytes 524320 | tf_op jit(solution)/shard_map/ppermute | solution.py:152
  68.2 10.0 %collective-permute-done.8 = bf16[1,256,1024]{2,1,0:T(8,128)(2,1)S(1)} collective-permute-done((bf16[1,256,1024]{2,1,0:T(8,128)(2,1)S(1)}, bf16[1,256,1024]{2,1,0:T(8,128)(2,1)S(1)}, u32[]{:S(2)}, u32[]{:S(2)}) %collective-permute-start.8) | collective-permute-done | bytes 524320 | tf_op jit(solution)/shard_map/ppermute | solution.py:152
  78.3 1.4 collective-permute-done.10
  80.4 0.6 collective-permute-start.14
  81.0 1.6 collective-permute-start.12
  82.5 1.5 collective-permute-start.13
  84.0 5.3 %collective-permute-done.12 = bf16[1,128,1024]{2,1,0:T(8,128)(2,1)S(1)} collective-permute-done((bf16[1,128,1024]{2,1,0:T(8,128)(2,1)S(1)}, bf16[1,128,1024]{2,1,0:T(8,128)(2,1)S(1)}, u32[]{:S(2)}, u32[]{:S(2)}) %collective-permute-start.12) | collective-permute-done | bytes 262176 | tf_op jit(solution)/shard_map/ppermute | solution.py:152
  89.4 1.6 collective-permute-start.16
  91.0 1.6 collective-permute-start.17
  92.6 9.9 %collective-permute-done.16 = bf16[2,128,1024]{2,1,0:T(8,128)(2,1)S(1)} collective-permute-done((bf16[2,128,1024]{2,1,0:T(8,128)(2,1)S(1)}, bf16[2,128,1024]{2,1,0:T(8,128)(2,1)S(1)}, u32[]{:S(2)}, u32[]{:S(2)}) %collective-permute-start.16) | collective-permute-done | bytes 524320 | tf_op jit(solution)/shard_map/ppermute | solution.py:152
  102.5 1.3 collective-permute-done.17
  103.9 4.0 %collective-permute-done.18.refs_4_ = bf16[1024,512]{1,0:T(8,128)(2,1)S(1)} collective-permute-done((bf16[1024,512]{1,0:T(8,128)(2,1)S(1)}, bf16[1024,512]{1,0:T(8,128)(2,1)S(1)}, u32[]{:S(2)}, u32[]{:S(2)}) %collective-permute-start.18) | collective-permute-done | bytes 1048608 | tf_op jit(solution)/shard_map/ppermute | solution.py:155
  108.1 0.6 collective-permute-start.19
  108.7 7.2 %shard_map.50.total = f32[2048,512]{1,0:T(8,128)S(1)} custom-call(s32[2]{0:T(128)S(1)} %pad_add_fusion.place, f32[2048,512]{1,0:T(8,128)S(1)} %copy-done, bf16[1024,8192]{1,0:T(8,128)(2,1)} %refs_0_.1, bf16[1024,512]{1,0:T(8,128)(2,1)S(1)} %copy-done.1, bf16[4,256,1024]{2,1,0:T(8,128)(2,1)S(1)} %constant_dynamic-update-slice_fusion.refs_2_, ...), custom_call_target="tpu_custom_call" | custom-call | flops 4294967296 | bytes 16777216 | tf_op jit(solution)/shard_map/pallas_call | solution.py:226
  115.9 3.5 %shard_map.51.total = f32[2048,512]{1,0:T(8,128)S(1)} custom-call(s32[2]{0:T(128)S(1)} %pad_add_fusion.place, f32[2048,512]{1,0:T(8,128)S(1)} %shard_map.50.total, bf16[4,128,1024]{2,1,0:T(8,128)(2,1)S(1)} %constant_dynamic-update-slice_fusion.4.refs_0_, bf16[4,128,1024]{2,1,0:T(8,128)(2,1)S(1)} %collective-permute-done.19.refs_1_, ...), custom_call_target="tpu_custom_call" | custom-call | flops 2147483648 | bytes 12582912 | tf_op jit(solution)/shard_map/pallas_call | solution.py:226
  119.5 16.3 %collective-permute-done.21.x_ref = bf16[1024,512]{1,0:T(8,128)(2,1)S(1)} collective-permute-done((bf16[1024,512]{1,0:T(8,128)(2,1)S(1)}, bf16[1024,512]{1,0:T(8,128)(2,1)S(1)}, u32[]{:S(2)}, u32[]{:S(2)}) %collective-permute-start.21) | collective-permute-done | bytes 1048608 | tf_op jit(solution)/shard_map/ppermute | solution.py:155
  135.8 2.5 %shard_map.53 = (f32[4,256,512]{2,1,0:T(8,128)S(1)}, f32[4,2,128,128]{3,2,1,0:T(8,128)S(1)}) custom-call(s32[2]{0:T(128)S(1)} %pad_add_fusion.place, f32[2048,512]{1,0:T(8,128)S(1)} %shard_map.51.total, bf16[4,256,1024]{2,1,0:T(8,128)(2,1)S(1)} %collective-permute-done.15.queries, bf16[1024,512]{1,0:T(8,128)(2,1)S(1)} %collective-permute-done.21.x_ref), custom_call_target="tpu_custom_call" | custom-call | flops 1073741824 | bytes 2097152 | tf_op jit(solution)/shard_map/pallas_call | solution.py:262
  138.3 2.5 %shard_map.52 = (f32[4,256,512]{2,1,0:T(8,128)S(1)}, f32[4,2,128,128]{3,2,1,0:T(8,128)S(1)}) custom-call(s32[2]{0:T(128)S(1)} %pad_add_fusion.place, f32[2048,512]{1,0:T(8,128)S(1)} %shard_map.51.total, bf16[4,256,1024]{2,1,0:T(8,128)(2,1)S(1)} %constant_dynamic-update-slice_fusion.2.queries, bf16[1024,512]{1,0:T(8,128)(2,1)S(1)} %collective-permute-done.21.x_ref), custom_call_target="tpu_custom_call" | custom-call | flops 1073741824 | bytes 2097152 | tf_op jit(solution)/shard_map/pallas_call | solution.py:262
  140.9 2.5 %collective-permute-start.25 = (f32[2,128,128]{2,1,0:T(8,128)S(1)}, f32[2,128,128]{2,1,0:T(8,128)S(1)}, u32[]{:S(2)}, u32[]{:S(2)}) collective-permute-start(f32[2,128,128]{2,1,0:T(8,128)S(1)} %get-tuple-element.76), channel_id=1, source_target_pairs={{0,6},{1,7},{2,4},{3,5},{4,2},{5,3},{6,0},{7,1},{8,14},{9,15},{10,... | collective-permute-start | bytes 393224 | tf_op jit(solution)/shard_map/ppermute | solution.py:152
  143.9 0.5 collective-permute-start.23
  144.5 2.6 %shard_map.54 = f32[2048,512]{1,0:T(8,128)} custom-call(s32[2]{0:T(128)S(1)} %pad_add_fusion.place, f32[4,256,512]{2,1,0:T(8,128)S(1)} %get-tuple-element.67.own.blocks, f32[4,256,512]{2,1,0:T(8,128)S(1)} %get-tuple-element.68.other.blocks), custom_call_target="tpu_custom_call" | custom-call | bytes 8388608 | tf_op jit(solution)/shard_map/pallas_call | solution.py:279
  147.1 1.0 collective-permute-done.25.refs_3_
  148.1 2.5 %collective-permute-done.24.refs_2_ = f32[2,128,128]{2,1,0:T(8,128)S(1)} collective-permute-done((f32[2,128,128]{2,1,0:T(8,128)S(1)}, f32[2,128,128]{2,1,0:T(8,128)S(1)}, u32[]{:S(2)}, u32[]{:S(2)}) %collective-permute-start.24) | collective-permute-done | bytes 131104 | tf_op jit(solution)/shard_map/ppermute | solution.py:152
  150.7 3.6 %shard_map.55 = f32[2,128,128]{2,1,0:T(8,128)S(1)} custom-call(f32[2,128,128]{2,1,0:T(8,128)S(1)} %get-tuple-element.70.refs_0_, f32[2,128,128]{2,1,0:T(8,128)S(1)} %collective-permute-done.23.refs_1_, f32[2,128,128]{2,1,0:T(8,128)S(1)} %collective-permute-done.24.refs_2_, f32[2,128,128]{2,1,0:T(8,128)S(1)} %collective-permute-done.25.refs_3_), custom_call_target="tpu_custom_call" | custom-call | tf_op jit(solution)/shard_map/pallas_call | solution.py:291
  154.3 1.7 %collective-permute-start.28 = (f32[2,128,128]{2,1,0:T(8,128)S(1)}, f32[2,128,128]{2,1,0:T(8,128)S(1)}, u32[]{:S(2)}, u32[]{:S(2)}) collective-permute-start(f32[2,128,128]{2,1,0:T(8,128)S(1)} %shard_map.55), channel_id=1, source_target_pairs={{0,6},{1,7},{2,4},{3,5},{4,2},{5,3},{6,0},{7,1},{8,14},{9,15},{10,... | collective-permute-start | bytes 393224 | tf_op jit(solution)/shard_map/ppermute | solution.py:152
  156.0 1.3 collective-permute-start.27
  157.9 3.8 %collective-permute-done.28 = f32[2,128,128]{2,1,0:T(8,128)S(1)} collective-permute-done((f32[2,128,128]{2,1,0:T(8,128)S(1)}, f32[2,128,128]{2,1,0:T(8,128)S(1)}, u32[]{:S(2)}, u32[]{:S(2)}) %collective-permute-start.28) | collective-permute-done | bytes 131104 | tf_op jit(solution)/shard_map/ppermute | solution.py:152
  161.7 1.8 %collective-permute-done.27 = f32[2,128,128]{2,1,0:T(8,128)S(1)} collective-permute-done((f32[2,128,128]{2,1,0:T(8,128)S(1)}, f32[2,128,128]{2,1,0:T(8,128)S(1)}, u32[]{:S(2)}, u32[]{:S(2)}) %collective-permute-start.27) | collective-permute-done | bytes 131104 | tf_op jit(solution)/shard_map/ppermute | solution.py:152
  163.6 1.0 shard_map.56.own
  164.6 0.9 collective-permute-done.29.factor
  165.5 2.6 %shard_map.57 = f32[2048,512]{1,0:T(8,128)} custom-call(s32[2]{0:T(128)S(1)} %pad_add_fusion.place, f32[4,2,128,128]{3,2,1,0:T(8,128)S(1)} %collective-permute-done.29.factor, f32[4,256,512]{2,1,0:T(8,128)S(1)} %get-tuple-element.68.other.blocks, f32[4,256,512]{2,1,0:T(8,128)S(1)} %shard_map.56.own), custom_call_target="tpu_custom_call" | custom-call | flops 402653184 | bytes 2097152 | tf_op jit(solution)/shard_map/pallas_call | solution.py:311
  (51 shorter events, 4.9 us)
Async XLA Ops:
  2.4 17.9 %collective-permute-start.1 = (bf16[256,1024]{1,0:T(8,128)(2,1)S(1)}, bf16[256,1024]{1,0:T(8,128)(2,1)S(1)}, u32[]{:S(2)}, u32[]{:S(2)}) collective-permute-start(bf16[256,1024]{1,0:T(8,128)(2,1)S(1)} %bitcast.32), channel_id=1, source_target_pairs={{0,8},{8,16},{16,24},{24,0},{1,9},{9,17},{17,25},{25,1},{2,10},{10... | collective-permute-start | bytes 1572872 | tf_op jit(solution)/shard_map/ppermute | solution.py:155
  5.4 24.6 %collective-permute-start.2 = (bf16[256,1024]{1,0:T(8,128)(2,1)S(1)}, bf16[256,1024]{1,0:T(8,128)(2,1)S(1)}, u32[]{:S(2)}, u32[]{:S(2)}) collective-permute-start(bf16[256,1024]{1,0:T(8,128)(2,1)S(1)} %bitcast.31), channel_id=1, source_target_pairs={{0,24},{8,0},{16,8},{24,16},{1,25},{9,1},{17,9},{25,17},{2,26},{10... | collective-permute-start | bytes 1572872 | tf_op jit(solution)/shard_map/ppermute | solution.py:155
  9.1 44.0 %collective-permute-start = (bf16[256,1024]{1,0:T(8,128)(2,1)S(1)}, bf16[256,1024]{1,0:T(8,128)(2,1)S(1)}, u32[]{:S(2)}, u32[]{:S(2)}) collective-permute-start(bf16[256,1024]{1,0:T(8,128)(2,1)S(1)} %bitcast.30), channel_id=1, source_target_pairs={{0,16},{8,24},{16,0},{24,8},{1,17},{9,25},{17,1},{25,9},{2,18},{10... | collective-permute-start | bytes 1572872 | tf_op jit(solution)/shard_map/ppermute | solution.py:155
  30.1 23.0 %copy-start.1 = (bf16[1024,512]{1,0:T(8,128)(2,1)S(1)}, bf16[1024,512]{1,0:T(8,128)(2,1)}, u32[]{:S(2)}) copy-start(bf16[1024,512]{1,0:T(8,128)(2,1)} %refs_1_.1) | copy-start | bytes 3145732
  30.1 9.3 %collective-permute-start.5 = (bf16[1,128,1024]{2,1,0:T(8,128)(2,1)S(1)}, bf16[1,128,1024]{2,1,0:T(8,128)(2,1)S(1)}, u32[]{:S(2)}, u32[]{:S(2)}) collective-permute-start(bf16[1,128,1024]{2,1,0:T(8,128)(2,1)S(1)} %get-tuple-element.82), channel_id=1, source_target_pairs={{0,2},{1,3},{2,0},{3,1},{4,6},{5,7},{6,4},{7,5},{8,10},{9,11},{10,... | collective-permute-start | bytes 786440 | tf_op jit(solution)/shard_map/ppermute | solution.py:152
  31.7 11.7 %collective-permute-start.6 = (bf16[1,128,1024]{2,1,0:T(8,128)(2,1)S(1)}, bf16[1,128,1024]{2,1,0:T(8,128)(2,1)S(1)}, u32[]{:S(2)}, u32[]{:S(2)}) collective-permute-start(bf16[1,128,1024]{2,1,0:T(8,128)(2,1)S(1)} %get-tuple-element.83), channel_id=1, source_target_pairs={{0,2},{1,3},{2,0},{3,1},{4,6},{5,7},{6,4},{7,5},{8,10},{9,11},{10,... | collective-permute-start | bytes 786440 | tf_op jit(solution)/shard_map/ppermute | solution.py:152
  32.2 11.2 %collective-permute-start.3 = (bf16[1,128,1024]{2,1,0:T(8,128)(2,1)S(1)}, bf16[1,128,1024]{2,1,0:T(8,128)(2,1)S(1)}, u32[]{:S(2)}, u32[]{:S(2)}) collective-permute-start(bf16[1,128,1024]{2,1,0:T(8,128)(2,1)S(1)} %get-tuple-element.84), channel_id=1, source_target_pairs={{0,4},{1,5},{2,6},{3,7},{4,0},{5,1},{6,2},{7,3},{8,12},{9,13},{10,... | collective-permute-start | bytes 786440 | tf_op jit(solution)/shard_map/ppermute | solution.py:152
  33.8 11.1 %collective-permute-start.4 = (bf16[1,128,1024]{2,1,0:T(8,128)(2,1)S(1)}, bf16[1,128,1024]{2,1,0:T(8,128)(2,1)S(1)}, u32[]{:S(2)}, u32[]{:S(2)}) collective-permute-start(bf16[1,128,1024]{2,1,0:T(8,128)(2,1)S(1)} %get-tuple-element.85), channel_id=1, source_target_pairs={{0,4},{1,5},{2,6},{3,7},{4,0},{5,1},{6,2},{7,3},{8,12},{9,13},{10,... | collective-permute-start | bytes 786440 | tf_op jit(solution)/shard_map/ppermute | solution.py:152
  53.1 26.9 %collective-permute-start.11 = (bf16[1024,512]{1,0:T(8,128)(2,1)S(1)}, bf16[1024,512]{1,0:T(8,128)(2,1)S(1)}, u32[]{:S(2)}, u32[]{:S(2)}) collective-permute-start(bf16[1024,512]{1,0:T(8,128)(2,1)S(1)} %copy-done.1), channel_id=1, source_target_pairs={{0,8},{8,16},{16,24},{24,0},{1,9},{9,17},{17,25},{25,1},{2,10},{10... | collective-permute-start | bytes 3145736 | tf_op jit(solution)/shard_map/ppermute | solution.py:155
  53.3 14.8 %collective-permute-start.7 = (bf16[1,256,1024]{2,1,0:T(8,128)(2,1)S(1)}, bf16[1,256,1024]{2,1,0:T(8,128)(2,1)S(1)}, u32[]{:S(2)}, u32[]{:S(2)}) collective-permute-start(bf16[1,256,1024]{2,1,0:T(8,128)(2,1)S(1)} %bitcast.28), channel_id=1, source_target_pairs={{0,2},{1,3},{2,0},{3,1},{4,6},{5,7},{6,4},{7,5},{8,10},{9,11},{10,... | collective-permute-start | bytes 1572872 | tf_op jit(solution)/shard_map/ppermute | solution.py:152
  54.8 23.3 %collective-permute-start.8 = (bf16[1,256,1024]{2,1,0:T(8,128)(2,1)S(1)}, bf16[1,256,1024]{2,1,0:T(8,128)(2,1)S(1)}, u32[]{:S(2)}, u32[]{:S(2)}) collective-permute-start(bf16[1,256,1024]{2,1,0:T(8,128)(2,1)S(1)} %pad_maximum_fusion.4), channel_id=1, source_target_pairs={{0,2},{1,3},{2,0},{3,1},{4,6},{5,7},{6,4},{7,5},{8,10},{9,11},{10,... | collective-permute-start | bytes 1572872 | tf_op jit(solution)/shard_map/ppermute | solution.py:152
  55.4 22.9 %collective-permute-start.9 = (bf16[1,256,1024]{2,1,0:T(8,128)(2,1)S(1)}, bf16[1,256,1024]{2,1,0:T(8,128)(2,1)S(1)}, u32[]{:S(2)}, u32[]{:S(2)}) collective-permute-start(bf16[1,256,1024]{2,1,0:T(8,128)(2,1)S(1)} %bitcast.25), channel_id=1, source_target_pairs={{0,4},{1,5},{2,6},{3,7},{4,0},{5,1},{6,2},{7,3},{8,12},{9,13},{10,... | collective-permute-start | bytes 1572872 | tf_op jit(solution)/shard_map/ppermute | solution.py:152
  56.9 22.8 %collective-permute-start.10 = (bf16[1,256,1024]{2,1,0:T(8,128)(2,1)S(1)}, bf16[1,256,1024]{2,1,0:T(8,128)(2,1)S(1)}, u32[]{:S(2)}, u32[]{:S(2)}) collective-permute-start(bf16[1,256,1024]{2,1,0:T(8,128)(2,1)S(1)} %pad_maximum_fusion.5), channel_id=1, source_target_pairs={{0,4},{1,5},{2,6},{3,7},{4,0},{5,1},{6,2},{7,3},{8,12},{9,13},{10,... | collective-permute-start | bytes 1572872 | tf_op jit(solution)/shard_map/ppermute | solution.py:152
  80.2 27.6 %collective-permute-start.15 = (bf16[4,256,1024]{2,1,0:T(8,128)(2,1)S(1)}, bf16[4,256,1024]{2,1,0:T(8,128)(2,1)S(1)}, u32[]{:S(2)}, u32[]{:S(2)}) collective-permute-start(bf16[4,256,1024]{2,1,0:T(8,128)(2,1)S(1)} %constant_dynamic-update-slice_fusion.2.queries), channel_id=1, source_target_pairs={{0,1},{1,0},{2,3},{3,2},{4,5},{5,4},{6,7},{7,6},{8,9},{9,8},{10,11... | collective-permute-start | bytes 6291464 | tf_op jit(solution)/shard_map/ppermute | solution.py:152
  80.4 27.5 %collective-permute-start.14 = (bf16[4,256,1024]{2,1,0:T(8,128)(2,1)S(1)}, bf16[4,256,1024]{2,1,0:T(8,128)(2,1)S(1)}, u32[]{:S(2)}, u32[]{:S(2)}) collective-permute-start(bf16[4,256,1024]{2,1,0:T(8,128)(2,1)S(1)} %constant_dynamic-update-slice_fusion.refs_2_), channel_id=1, source_target_pairs={{0,1},{1,0},{2,3},{3,2},{4,5},{5,4},{6,7},{7,6},{8,9},{9,8},{10,11... | collective-permute-start | bytes 6291464 | tf_op jit(solution)/shard_map/ppermute | solution.py:152
  80.9 26.9 %collective-permute-start.18 = (bf16[1024,512]{1,0:T(8,128)(2,1)S(1)}, bf16[1024,512]{1,0:T(8,128)(2,1)S(1)}, u32[]{:S(2)}, u32[]{:S(2)}) collective-permute-start(bf16[1024,512]{1,0:T(8,128)(2,1)S(1)} %collective-permute-done.11.refs_4_), channel_id=1, source_target_pairs={{0,8},{8,16},{16,24},{24,0},{1,9},{9,17},{17,25},{25,1},{2,10},{10... | collective-permute-start | bytes 3145736 | tf_op jit(solution)/shard_map/ppermute | solution.py:155
  81.0 8.4 %collective-permute-start.12 = (bf16[1,128,1024]{2,1,0:T(8,128)(2,1)S(1)}, bf16[1,128,1024]{2,1,0:T(8,128)(2,1)S(1)}, u32[]{:S(2)}, u32[]{:S(2)}) collective-permute-start(bf16[1,128,1024]{2,1,0:T(8,128)(2,1)S(1)} %get-tuple-element.81), channel_id=1, source_target_pairs={{0,4},{1,5},{2,6},{3,7},{4,0},{5,1},{6,2},{7,3},{8,12},{9,13},{10,... | collective-permute-start | bytes 786440 | tf_op jit(solution)/shard_map/ppermute | solution.py:152
  82.5 8.4 %collective-permute-start.13 = (bf16[1,128,1024]{2,1,0:T(8,128)(2,1)S(1)}, bf16[1,128,1024]{2,1,0:T(8,128)(2,1)S(1)}, u32[]{:S(2)}, u32[]{:S(2)}) collective-permute-start(bf16[1,128,1024]{2,1,0:T(8,128)(2,1)S(1)} %get-tuple-element.80), channel_id=1, source_target_pairs={{0,2},{1,3},{2,0},{3,1},{4,6},{5,7},{6,4},{7,5},{8,10},{9,11},{10,... | collective-permute-start | bytes 786440 | tf_op jit(solution)/shard_map/ppermute | solution.py:152
  89.4 13.1 %collective-permute-start.16 = (bf16[2,128,1024]{2,1,0:T(8,128)(2,1)S(1)}, bf16[2,128,1024]{2,1,0:T(8,128)(2,1)S(1)}, u32[]{:S(2)}, u32[]{:S(2)}) collective-permute-start(bf16[2,128,1024]{2,1,0:T(8,128)(2,1)S(1)} %pad_maximum_fusion.6), channel_id=1, source_target_pairs={{0,2},{1,3},{2,0},{3,1},{4,6},{5,7},{6,4},{7,5},{8,10},{9,11},{10,... | collective-permute-start | bytes 1572872 | tf_op jit(solution)/shard_map/ppermute | solution.py:152
  91.0 17.8 %copy-start = (f32[2048,512]{1,0:T(8,128)S(1)}, f32[2048,512]{1,0:T(8,128)}, u32[]{:S(2)}) copy-start(f32[2048,512]{1,0:T(8,128)} %total.1) | copy-start | bytes 12582916
  91.0 12.9 %collective-permute-start.17 = (bf16[2,128,1024]{2,1,0:T(8,128)(2,1)S(1)}, bf16[2,128,1024]{2,1,0:T(8,128)(2,1)S(1)}, u32[]{:S(2)}, u32[]{:S(2)}) collective-permute-start(bf16[2,128,1024]{2,1,0:T(8,128)(2,1)S(1)} %pad_maximum_fusion.7), channel_id=1, source_target_pairs={{0,4},{1,5},{2,6},{3,7},{4,0},{5,1},{6,2},{7,3},{8,12},{9,13},{10,... | collective-permute-start | bytes 1572872 | tf_op jit(solution)/shard_map/ppermute | solution.py:152
  108.0 7.9 %collective-permute-start.20 = (bf16[4,128,1024]{2,1,0:T(8,128)(2,1)S(1)}, bf16[4,128,1024]{2,1,0:T(8,128)(2,1)S(1)}, u32[]{:S(2)}, u32[]{:S(2)}) collective-permute-start(bf16[4,128,1024]{2,1,0:T(8,128)(2,1)S(1)} %constant_dynamic-update-slice_fusion.6.refs_2_), channel_id=1, source_target_pairs={{0,1},{1,0},{2,3},{3,2},{4,5},{5,4},{6,7},{7,6},{8,9},{9,8},{10,11... | collective-permute-start | bytes 3145736 | tf_op jit(solution)/shard_map/ppermute | solution.py:152
  108.1 7.8 %collective-permute-start.19 = (bf16[4,128,1024]{2,1,0:T(8,128)(2,1)S(1)}, bf16[4,128,1024]{2,1,0:T(8,128)(2,1)S(1)}, u32[]{:S(2)}, u32[]{:S(2)}) collective-permute-start(bf16[4,128,1024]{2,1,0:T(8,128)(2,1)S(1)} %constant_dynamic-update-slice_fusion.4.refs_0_), channel_id=1, source_target_pairs={{0,1},{1,0},{2,3},{3,2},{4,5},{5,4},{6,7},{7,6},{8,9},{9,8},{10,11... | collective-permute-start | bytes 3145736 | tf_op jit(solution)/shard_map/ppermute | solution.py:152
  108.7 27.1 %collective-permute-start.21 = (bf16[1024,512]{1,0:T(8,128)(2,1)S(1)}, bf16[1024,512]{1,0:T(8,128)(2,1)S(1)}, u32[]{:S(2)}, u32[]{:S(2)}) collective-permute-start(bf16[1024,512]{1,0:T(8,128)(2,1)S(1)} %collective-permute-done.18.refs_4_), channel_id=1, source_target_pairs={{0,8},{8,16},{16,24},{24,0},{1,9},{9,17},{17,25},{25,1},{2,10},{10... | collective-permute-start | bytes 3145736 | tf_op jit(solution)/shard_map/ppermute | solution.py:155
  138.2 2.6 %collective-permute-start.22 = (f32[4,2,128,128]{3,2,1,0:T(8,128)S(1)}, f32[4,2,128,128]{3,2,1,0:T(8,128)S(1)}, u32[]{:S(2)}, u32[]{:S(2)}) collective-permute-start(f32[4,2,128,128]{3,2,1,0:T(8,128)S(1)} %get-tuple-element.66), channel_id=1, source_target_pairs={{0,1},{1,0},{2,3},{3,2},{4,5},{5,4},{6,7},{7,6},{8,9},{9,8},{10,11... | collective-permute-start | bytes 1572872 | tf_op jit(solution)/shard_map/ppermute | solution.py:152
  140.9 7.1 %collective-permute-start.25 = (f32[2,128,128]{2,1,0:T(8,128)S(1)}, f32[2,128,128]{2,1,0:T(8,128)S(1)}, u32[]{:S(2)}, u32[]{:S(2)}) collective-permute-start(f32[2,128,128]{2,1,0:T(8,128)S(1)} %get-tuple-element.76), channel_id=1, source_target_pairs={{0,6},{1,7},{2,4},{3,5},{4,2},{5,3},{6,0},{7,1},{8,14},{9,15},{10,... | collective-permute-start | bytes 393224 | tf_op jit(solution)/shard_map/ppermute | solution.py:152
  143.4 7.2 %collective-permute-start.24 = (f32[2,128,128]{2,1,0:T(8,128)S(1)}, f32[2,128,128]{2,1,0:T(8,128)S(1)}, u32[]{:S(2)}, u32[]{:S(2)}) collective-permute-start(f32[2,128,128]{2,1,0:T(8,128)S(1)} %get-tuple-element.77), channel_id=1, source_target_pairs={{0,4},{1,5},{2,6},{3,7},{4,0},{5,1},{6,2},{7,3},{8,12},{9,13},{10,... | collective-permute-start | bytes 393224 | tf_op jit(solution)/shard_map/ppermute | solution.py:152
  143.9 6.8 %collective-permute-start.23 = (f32[2,128,128]{2,1,0:T(8,128)S(1)}, f32[2,128,128]{2,1,0:T(8,128)S(1)}, u32[]{:S(2)}, u32[]{:S(2)}) collective-permute-start(f32[2,128,128]{2,1,0:T(8,128)S(1)} %get-tuple-element.78), channel_id=1, source_target_pairs={{0,2},{1,3},{2,0},{3,1},{4,6},{5,7},{6,4},{7,5},{8,10},{9,11},{10,... | collective-permute-start | bytes 393224 | tf_op jit(solution)/shard_map/ppermute | solution.py:152
  154.3 7.4 %collective-permute-start.28 = (f32[2,128,128]{2,1,0:T(8,128)S(1)}, f32[2,128,128]{2,1,0:T(8,128)S(1)}, u32[]{:S(2)}, u32[]{:S(2)}) collective-permute-start(f32[2,128,128]{2,1,0:T(8,128)S(1)} %shard_map.55), channel_id=1, source_target_pairs={{0,6},{1,7},{2,4},{3,5},{4,2},{5,3},{6,0},{7,1},{8,14},{9,15},{10,... | collective-permute-start | bytes 393224 | tf_op jit(solution)/shard_map/ppermute | solution.py:152
  156.0 7.4 %collective-permute-start.27 = (f32[2,128,128]{2,1,0:T(8,128)S(1)}, f32[2,128,128]{2,1,0:T(8,128)S(1)}, u32[]{:S(2)}, u32[]{:S(2)}) collective-permute-start(f32[2,128,128]{2,1,0:T(8,128)S(1)} %shard_map.55), channel_id=1, source_target_pairs={{0,4},{1,5},{2,6},{3,7},{4,0},{5,1},{6,2},{7,3},{8,12},{9,13},{10,... | collective-permute-start | bytes 393224 | tf_op jit(solution)/shard_map/ppermute | solution.py:152
  157.3 6.2 %collective-permute-start.26 = (f32[2,128,128]{2,1,0:T(8,128)S(1)}, f32[2,128,128]{2,1,0:T(8,128)S(1)}, u32[]{:S(2)}, u32[]{:S(2)}) collective-permute-start(f32[2,128,128]{2,1,0:T(8,128)S(1)} %shard_map.55), channel_id=1, source_target_pairs={{0,2},{1,3},{2,0},{3,1},{4,6},{5,7},{6,4},{7,5},{8,10},{9,11},{10,... | collective-permute-start | bytes 393224 | tf_op jit(solution)/shard_map/ppermute | solution.py:152
  163.6 2.0 %collective-permute-start.29 = (f32[4,2,128,128]{3,2,1,0:T(8,128)S(1)}, f32[4,2,128,128]{3,2,1,0:T(8,128)S(1)}, u32[]{:S(2)}, u32[]{:S(2)}) collective-permute-start(f32[4,2,128,128]{3,2,1,0:T(8,128)S(1)} %pad_maximum_fusion.8.factor), channel_id=1, source_target_pairs={{0,1},{1,0},{2,3},{3,2},{4,5},{5,4},{6,7},{7,6},{8,9},{9,8},{10,11... | collective-permute-start | bytes 1572872 | tf_op jit(solution)/shard_map/ppermute | solution.py:152
